TPU v7x, 256 devices: a whole 4x4x8 slice. The times are simulated.
256 devices in a mesh: dp: 32 (over z_lo, y, core), shard: 8 (over x, z_hi).
Axes of the slice: x: 4, y: 4, z: 8 (z_hi: 2, z_lo: 4; z = z_hi * 4 + z_lo), core: 2. Of those that a mesh axis runs over, the one named last changes fastest.
Arguments:
- inputs: bfloat16 [32768, 8192], P(('dp', 'shard')), may hold values from -6 to 6
- grad_out: bfloat16 [32768, 1024], P(('dp', 'shard')), may hold values from -6 to 6
- weight: bfloat16 [8192, 1024], P('shard'), may hold values from -0.1875 to 0.1875
- projector: bfloat16 [8192, 512], P('shard'), may hold values from -0.0625 to 0.0625
- first_moment: float32 [512, 1024], P('dp'), may hold values from -320 to 320
- second_moment: float32 [512, 1024], P('dp'), may hold values from 8192 to 131072
Outputs:
- input_grad: bfloat16 [32768, 8192], P(('dp', 'shard'))
- weight_update: float32 [8192, 1024], P('shard')
- new_first: float32 [512, 1024], P('dp')
- new_second: float32 [512, 1024], P('dp')
All inputs are finite; a program needn't handle non-finite values.
Results may differ from a plain program's by a relative error of at most 0.009.
Values may be sent and summed in bfloat16 or wider, within the bound.
No kernel may reach another device: no remote copies, remote signals or barrier semaphores. Data moves between devices by JAX's collectives and lax.ppermute only.
A program may use at most 128 MiB of HBM per device.

v0:
```python
import jax
import jax.numpy as jnp
from jax import lax
from jax.sharding import PartitionSpec as P

beta_one = 0.9
beta_two = 0.999
bias_one = 0.999973438601112
bias_two = 0.0952078528862904
epsilon = 1e-08


def widen(values):
    return values.astype(jnp.float32)


def adam_step(projected_grad, first_moment, second_moment):
    new_first = beta_one * first_moment + (1.0 - beta_one) * projected_grad
    new_second = beta_two * second_moment + (1.0 - beta_two) * projected_grad * projected_grad
    direction = new_first / bias_one / (jnp.sqrt(new_second / bias_two) + epsilon)
    return (new_first, new_second, direction.astype(jnp.bfloat16))


def body(inputs, grad_out, weight, projector, first_moment, second_moment):
    contract_last = (((1,), (1,)), ((), ()))
    contract_first = (((0,), (0,)), ((), ()))
    wide_grads = widen(grad_out)
    wide_inputs = widen(inputs)
    input_grad = lax.dot_general(
        wide_grads,
        widen(lax.all_gather(weight, "shard", axis=0, tiled=True)),
        contract_last,
        preferred_element_type=jnp.float32,
    ).astype(jnp.bfloat16)
    projected = jnp.dot(
        wide_inputs,
        widen(lax.all_gather(projector, "shard", axis=0, tiled=True)),
        preferred_element_type=jnp.float32,
    )
    partial_value = lax.dot_general(
        projected,
        wide_grads,
        contract_first,
        precision=lax.Precision.HIGHEST,
        preferred_element_type=jnp.float32,
    )
    owned_rows = lax.psum_scatter(partial_value, "dp", scatter_dimension=0, tiled=True)
    owned_rows = lax.psum(owned_rows.astype(jnp.bfloat16), "shard").astype(jnp.float32)
    new_first, new_second, direction = adam_step(owned_rows, first_moment, second_moment)
    wide_projector = widen(projector)
    weight_update = jnp.dot(
        wide_projector,
        widen(lax.all_gather(direction, "dp", axis=0, tiled=True)),
        preferred_element_type=jnp.float32,
    )
    return (input_grad, weight_update, new_first, new_second)


def solution(mesh):
    return jax.shard_map(
        body,
        mesh=mesh,
        in_specs=(
            P(("dp", "shard"), None),
            P(("dp", "shard"), None),
            P("shard", None),
            P("shard", None),
            P("dp", None),
            P("dp", None),
        ),
        out_specs=(P(("dp", "shard"), None), P("shard", None), P("dp", None), P("dp", None)),
        check_vma=False,
    )
```

profile of v0, /device:TPU:8, one launch (start us, length us, event | category | flops | bytes accessed | tf_op | source)
XLA Modules:
  0.0 767.7 jit_solution(3651376065196709832)
XLA Ops:
  7.2 0.0 copy-start
  7.2 0.0 all-gather.6.cloned.1.call-start
  7.2 0.7 all-gather.6.cloned.1.call-update
  7.9 0.0 copy-start.1
  7.9 0.0 reduce-scatter.2.cloned.1.call-start
  8.0 178.9 %all-gather.6.cloned.1.call-done = bf16[8192,512]{1,0:T(8,128)(2,1)} async-done(((bf16[1024,512]{1,0:T(8,128)(2,1)}), bf16[8192,512]{1,0:T(8,128)(2,1)}) %all-gather.6.cloned.1.call-update) | async-done | bytes 8388624 | tf_op jit(solution)/shard_map/all_gather | solution.py:37
  186.9 0.0 copy-done
  186.9 4.6 fusion.4
  191.5 0.0 copy-done.1
  191.5 0.0 copy-start.3
  191.6 0.0 copy-start.2
  191.6 2.4 fusion.5
  193.9 0.0 reduce-scatter.2.cloned.1.call-update
  193.9 0.0 all-gather.8.cloned.1.call-start
  194.0 136.0 %reduce-scatter.2.cloned.1.call-done = f32[16,1024]{1,0:T(8,128)} async-done(((f32[512,1024]{1,0:T(8,128)}), f32[16,1024]{1,0:T(8,128)}) %reduce-scatter.2.cloned.1.call-update) | async-done | bytes 65552 | tf_op jit(solution)/shard_map/reduce_scatter | solution.py:47
  330.0 0.8 convert_element_type.9
  330.8 51.4 %psum.7 = bf16[16,1024]{1,0:T(8,128)(2,1)S(1)} all-reduce(bf16[16,1024]{1,0:T(8,128)(2,1)S(1)} %convert_element_type.9), channel_id=1, replica_groups=mesh['dp'=32,'shard'=8] {'shard'}, use_global_device_ids=true, to_apply=%region_1.0 | all-reduce | flops 16384 | bytes 65536 | tf_op jit(solution)/shard_map/psum | solution.py:48
  382.2 0.0 copy-done.3
  382.2 1.5 divide_convert_fusion
  383.7 0.0 all-gather.8.cloned.1.call-update
  383.8 0.0 all-gather.4.cloned.1.call-start
  383.8 0.5 all-gather.4.cloned.1.call-update
  384.3 54.8 %all-gather.8.cloned.1.call-done = bf16[512,1024]{1,0:T(8,128)(2,1)} async-done(((bf16[16,1024]{1,0:T(8,128)(2,1)}), bf16[512,1024]{1,0:T(8,128)(2,1)}) %all-gather.8.cloned.1.call-update) | async-done | bytes 1048592 | tf_op jit(solution)/shard_map/all_gather | solution.py:53
  439.2 0.0 copy-done.2
  439.2 4.5 convolution_bitcast_fusion
  443.6 5.3 copy.10
  449.0 299.5 %all-gather.4.cloned.1.call-done = bf16[8192,1024]{1,0:T(8,128)(2,1)} async-done(((bf16[1024,1024]{1,0:T(8,128)(2,1)}), bf16[8192,1024]{1,0:T(8,128)(2,1)}) %all-gather.4.cloned.1.call-update) | async-done | bytes 16777232 | tf_op jit(solution)/shard_map/all_gather | solution.py:31
  748.5 12.7 %convolution_convert_fusion = bf16[128,8192]{1,0:T(8,128)(2,1)} fusion(bf16[128,1024]{1,0:T(8,128)(2,1)S(1)} %copy-done.1, bf16[8192,1024]{1,0:T(8,128)(2,1)} %all-gather.4.cloned.1.call-done), kind=kOutput, calls=%fused_computation | convolution fusion | flops 2148532224 | bytes 19136512 | tf_op jit(solution)/shard_map/dot_general | solution.py:29
Async XLA Ops:
  7.2 179.7 %copy-start = (bf16[128,8192]{1,0:T(8,128)(2,1)S(1)}, bf16[128,8192]{1,0:T(8,128)(2,1)}, u32[]{:S(2)}) copy-start(bf16[128,8192]{1,0:T(8,128)(2,1)} %param.6) | copy-start | bytes 6291460
  7.2 179.7 %all-gather.6.cloned.1.call-start = ((), (), s32[]{:S(2)}) async-start(), calls=%async_computation.2 | async-start | bytes 9437184 | tf_op jit(solution)/shard_map/all_gather | solution.py:37
  7.9 183.6 %copy-start.1 = (bf16[128,1024]{1,0:T(8,128)(2,1)S(1)}, bf16[128,1024]{1,0:T(8,128)(2,1)}, u32[]{:S(2)}) copy-start(bf16[128,1024]{1,0:T(8,128)(2,1)} %param.7) | copy-start | bytes 786436
  7.9 322.1 %reduce-scatter.2.cloned.1.call-start = ((), (), s32[]{:S(2)}) async-start(), calls=%async_computation.3 | async-start | bytes 2162688 | tf_op jit(solution)/shard_map/reduce_scatter | solution.py:47
  191.5 190.7 %copy-start.3 = (f32[16,1024]{1,0:T(8,128)S(1)}, f32[16,1024]{1,0:T(8,128)}, u32[]{:S(2)}) copy-start(f32[16,1024]{1,0:T(8,128)} %param.10) | copy-start | bytes 196612
  191.6 247.6 %copy-start.2 = (bf16[1024,512]{1,0:T(8,128)(2,1)S(1)}, bf16[1024,512]{1,0:T(8,128)(2,1)}, u32[]{:S(2)}) copy-start(bf16[1024,512]{1,0:T(8,128)(2,1)} %param.9) | copy-start | bytes 3145732
  193.9 245.2 %all-gather.8.cloned.1.call-start = ((), (), s32[]{:S(2)}) async-start(), calls=%async_computation.4 | async-start | bytes 1081344 | tf_op jit(solution)/shard_map/all_gather | solution.py:53
  383.8 364.7 %all-gather.4.cloned.1.call-start = ((), (), s32[]{:S(2)}) async-start(), calls=%async_computation.1 | async-start | bytes 18874368 | tf_op jit(solution)/shard_map/all_gather | solution.py:31
Sparse Core Ops, SparseCore 0:
  10.6 176.2 all-gather.5
  194.1 135.8 reduce-scatter.1
  383.9 55.2 all-gather.7
  442.0 306.4 all-gather.3
where the time goes:
time: 769 us; the launch traced here: 768 us
  waiting for transfers between devices  670 us (87%)
  blocking collectives  51.4 us (7%)
  matrix products  24.2 us (3%)
  between operations  13.8 us (2%)
    all_gather x1, waiting for transfers between devices, body(): lax.all_gather(weight, 'shard', axis=0, tiled=True)  300 us
    all_gather x1, waiting for transfers between devices, body(): lax.all_gather(projector, 'shard', axis=0, tiled=True)  179 us
    reduce_scatter x1, waiting for transfers between devices, body(): lax.psum_scatter(partial_value, 'dp', scatter_dimension=0, tiled=True)  136 us
    all_gather x1, waiting for transfers between devices, body(): lax.all_gather(direction, 'dp', axis=0, tiled=True)  54.8 us
    psum x1, blocking collectives, body(): lax.psum(owned_rows.astype(jnp.bfloat16), 'shard').astype(jnp.float32)  51.4 us
  transfers between devices with their start and end apart: 4, of which 4 were waited for; matrix products, arithmetic and copies ran while one was open for 1% of the time, Pallas kernels for 0%

commit v1 on v0

v1 whole, which is shorter than its diff:
```python
import itertools

import jax
import jax.numpy as jnp
from jax import lax
from jax.sharding import Mesh
from jax.sharding import PartitionSpec as P

beta_one = 0.9
beta_two = 0.999
bias_one = 0.999973438601112
bias_two = 0.0952078528862904
epsilon = 1e-08

NAMES = ("zl", "y", "c", "x", "zh")
SIZES = {"zl": 4, "y": 4, "c": 2, "x": 4, "zh": 2}
DP = ("zl", "y", "c")
SHARD = ("x", "zh")
WIDE = jnp.float32
NARROW = jnp.bfloat16


def send(value, **shift):
    axes = tuple(name for name in NAMES if name in shift)
    sizes = [SIZES[name] for name in axes]
    flat = {at: i for i, at in enumerate(itertools.product(*map(range, sizes)))}
    pairs = [
        (i, flat[tuple((p + shift[n]) % s for p, n, s in zip(at, axes, sizes))])
        for at, i in flat.items()
    ]
    return lax.ppermute(value, axes, pairs)


def adam_step(projected_grad, first_moment, second_moment):
    new_first = beta_one * first_moment + (1.0 - beta_one) * projected_grad
    new_second = beta_two * second_moment + (1.0 - beta_two) * projected_grad * projected_grad
    direction = new_first / bias_one / (jnp.sqrt(new_second / bias_two) + epsilon)
    return (new_first, new_second, direction.astype(NARROW))


def dot(a, b, contract):
    return lax.dot_general(a, b, ((contract[:1], contract[1:]), ((), ())), preferred_element_type=WIDE)


def slot_permutation():
    row = lax.broadcasted_iota(jnp.int32, (512, 512), 0)
    slot = lax.broadcasted_iota(jnp.int32, (512, 512), 1)
    cc, dy, dz, low = slot // 256, slot // 64 % 4, slot // 16 % 4, slot % 16
    zl = (lax.axis_index("zl") + dz) % 4
    y = (lax.axis_index("y") + dy) % 4
    c = (lax.axis_index("c") + cc) % 2
    return (row == ((zl * 4 + y) * 2 + c) * 16 + low).astype(NARROW)


def fold(slots, axis):
    rows = slots.shape[0] // 4
    total = slots[:rows].astype(WIDE)
    for s in (1, 2, 3):
        total = total + send(slots[rows * s : rows * s + rows], **{axis: s}).astype(WIDE)
    return total


def spread(own, axis):
    return jnp.concatenate([own] + [send(own, **{axis: -s}) for s in (1, 2, 3)], 0)


def swap_shard(mine):
    half = mine.shape[0] // 2
    c, zh = lax.axis_index("c"), lax.axis_index("zh")
    part = send(lax.dynamic_slice_in_dim(mine, c * half, half, 0), zh=1)
    other = send(part, c=1)
    both = jnp.zeros((4 * half, mine.shape[1]), mine.dtype)
    both = lax.dynamic_update_slice_in_dim(both, mine, zh * 2 * half, 0)
    both = lax.dynamic_update_slice_in_dim(both, part, (1 - zh) * 2 * half + c * half, 0)
    return lax.dynamic_update_slice_in_dim(both, other, (1 - zh) * 2 * half + (1 - c) * half, 0)


def body(inputs, grad_out, weight, projector, first_moment, second_moment):
    x = lax.axis_index("x")

    columns = [lax.dynamic_slice_in_dim(inputs, (x + s) % 4 * 2048, 2048, 1) for s in range(4)]
    tokens = [columns[0]] + [send(columns[s], x=s) for s in (1, 2, 3)]
    grads = [grad_out] + [send(grad_out, x=s) for s in (1, 2, 3)]
    tokens = jnp.concatenate(tokens, 0)
    grads = jnp.concatenate(grads, 0)

    order = slot_permutation()
    basis = swap_shard(projector)
    basis = dot(basis, order, (1, 0)).astype(NARROW)
    own_basis = dot(projector, order, (1, 0)).astype(NARROW)

    projected = dot(tokens, basis, (1, 0)).astype(NARROW)
    partial = dot(projected, grads, (0, 0))

    kept = partial[:256] + send(partial[256:].astype(NARROW), c=1).astype(WIDE)
    kept = fold(kept.astype(NARROW), "y")
    kept = fold(kept.astype(NARROW), "zl")
    kept = kept + send(kept, zh=1)
    far = [send(kept, x=s) for s in (1, 2, 3)]
    projected_grad = (kept + far[1]) + (far[0] + far[2])

    new_first, new_second, direction = adam_step(projected_grad, first_moment, second_moment)

    near = spread(spread(direction, "zl"), "y")
    far = send(near, c=1)
    weight_update = dot(own_basis, jnp.concatenate([near, far], 0), (1, 0))

    both = swap_shard(weight)
    block = dot(grads, both, (1, 1)).astype(NARROW)
    input_grad = jnp.zeros(inputs.shape, NARROW)
    for s in range(4):
        part = block[128 * s : 128 * s + 128]
        part = send(part, x=-s) if s else part
        input_grad = lax.dynamic_update_slice_in_dim(input_grad, part, (x + s) % 4 * 2048, 1)
    return (input_grad, weight_update, new_first, new_second)


def solution(mesh):
    fine = Mesh(mesh.devices.reshape([SIZES[name] for name in NAMES]), NAMES)
    return jax.shard_map(
        body,
        mesh=fine,
        in_specs=(
            P(DP + SHARD, None),
            P(DP + SHARD, None),
            P(SHARD, None),
            P(SHARD, None),
            P(DP, None),
            P(DP, None),
        ),
        out_specs=(P(DP + SHARD, None), P(SHARD, None), P(DP, None), P(DP, None)),
        check_vma=False,
    )
```

time: 769 us -> 203 us (0.26)
  waiting for transfers between devices: 670 us -> 97.6 us
  starting transfers between devices: 0.16 us -> 55.6 us
  blocking collectives: 51.4 us -> 0 us
  local copies, waits for them, and re-layouts: 5.36 us -> 27.9 us
  between operations: 13.8 us -> 0.95 us
  matrix products: 24.2 us -> 16 us
    all_gather x3 -> x0, waiting for transfers between devices: 533 us -> none  [the longest x1 300 us: body(): lax.all_gather(weight, 'shard', axis=0, tiled=True)]
    reduce_scatter x1 -> x0, waiting for transfers between devices: 136 us -> none  [body(): lax.psum_scatter(partial_value, 'dp', scatter_dimension=0, tiled=True)]
    ppermute x0 -> x31, waiting for transfers between devices: none -> 97.6 us  [send(): return lax.ppermute(value, axes, pairs)]
    ppermute x0 -> x31, starting transfers between devices: none -> 55.6 us  [send(): return lax.ppermute(value, axes, pairs)]
    psum x1 -> x0, blocking collectives: 51.4 us -> none  [body(): lax.psum(owned_rows.astype(jnp.bfloat16), 'shard').astype(jnp.float32)]
    dot_general x4, matrix products: 24.2 us -> 16 us  [dot(): lax.dot_general(a, b, ((contract[:1], contract[1:]), ((), ())), preferred...]
  transfers between devices with their start and end apart: 4 -> 31, of which waited for: 4 -> 18; matrix products, arithmetic and copies ran while one was open for 1% -> 17% of each run, Pallas kernels for 0% -> 0%
where the time goes in v1:
time: 203 us; the launch traced here: 199 us
  waiting for transfers between devices  97.6 us (48%)
  starting transfers between devices  55.6 us (27%)
  local copies, waits for them, and re-layouts  27.9 us (14%)
  matrix products  16 us (8%)
    ppermute x31, waiting for transfers between devices, send(): return lax.ppermute(value, axes, pairs)  97.6 us
    ppermute x31, starting transfers between devices, send(): return lax.ppermute(value, axes, pairs)  55.6 us
    dot_general x4, matrix products, dot(): lax.dot_general(a, b, ((contract[:1], contract[1:]), ((), ())), preferred...  16 us
    unnamed x29, local copies, waits for them, and re-layouts  10.4 us
  transfers between devices with their start and end apart: 31, of which 18 were waited for; matrix products, arithmetic and copies ran while one was open for 17% of the time, Pallas kernels for 0%

profile of v1, /device:TPU:8, one launch (start us, length us, event | category | flops | bytes accessed | tf_op | source)
XLA Modules:
  0.0 199.0 jit_solution(620212120392548549)
XLA Ops:
  0.6 1.6 collective-permute-start
  2.2 2.7 %collective-permute-start.1 = (bf16[128,1024]{1,0:T(8,128)(2,1)}, bf16[128,1024]{1,0:T(8,128)(2,1)}, u32[]{:S(2)}, u32[]{:S(2)}) collective-permute-start(bf16[128,1024]{1,0:T(8,128)(2,1)} %param.7), channel_id=1, source_target_pairs={{0,4},{2,6},{4,0},{6,2},{1,5},{3,7},{5,1},{7,3},{8,12},{10,14},{12... | collective-permute-start | bytes 786440 | tf_op jit(solution)/shard_map/ppermute | solution.py:31
  4.9 1.4 collective-permute-start.2
  6.4 1.9 constant_dynamic-slice_fusion
  8.2 7.2 %collective-permute-start.11 = (bf16[512,512]{1,0:T(8,128)(2,1)}, bf16[512,512]{1,0:T(8,128)(2,1)}, u32[]{:S(2)}, u32[]{:S(2)}) collective-permute-start(bf16[512,512]{1,0:T(8,128)(2,1)} %constant_dynamic-slice_fusion), channel_id=1, source_target_pairs={{0,1},{1,0},{2,3},{3,2},{4,5},{5,4},{6,7},{7,6},{8,9},{9,8},{10,11... | collective-permute-start | bytes 1572872 | tf_op jit(solution)/shard_map/ppermute | solution.py:31
  15.4 2.9 %constant_dynamic-slice_fusion.4 = (bf16[128,2048]{1,0:T(8,128)(2,1)}, bf16[128,2048]{1,0:T(8,128)(2,1)}, bf16[128,2048]{1,0:T(8,128)(2,1)}, bf16[128,2048]{1,0:T(8,128)(2,1)}) fusion(bf16[128,8192]{1,0:T(8,128)(2,1)} %param.6, s32[]{:T(128)S(6)} %select_n.101, s32[]{:T(128)S(6)} %select_n.103, s32[]{:T(128)S(6)} %select_n.107, s32[]{:T(128)S(6)} %select_n.105), kind=kLoop, calls=%fused_computation.89 | loop fusion | bytes 4194320 | tf_op jit(solution)/shard_map/dynamic_slice | solution.py:81
  19.8 9.3 %collective-permute-done.11 = bf16[512,512]{1,0:T(8,128)(2,1)} collective-permute-done((bf16[512,512]{1,0:T(8,128)(2,1)}, bf16[512,512]{1,0:T(8,128)(2,1)}, u32[]{:S(2)}, u32[]{:S(2)}) %collective-permute-start.11) | collective-permute-done | bytes 524320 | tf_op jit(solution)/shard_map/ppermute | solution.py:31
  29.7 1.7 constant_dynamic-update-slice_fusion.2
  32.0 1.7 constant_dynamic-update-slice_fusion.1
  33.7 1.7 constant_dynamic-update-slice_fusion
  35.4 1.1 constant_dynamic-update-slice_fusion.20
  36.4 1.1 constant_dynamic-update-slice_fusion.19
  37.5 2.6 %convolution_convert_fusion.1 = bf16[2048,512]{1,0:T(8,128)(2,1)} fusion(bf16[2048,512]{1,0:T(8,128)(2,1)S(1)} %constant_dynamic-update-slice_fusion.19, s32[512]{0:T(512)S(1)} %get-tuple-element.39, s32[512]{0:T(512)S(1)} %get-tuple-element.42, s32[512]{0:T(512)S(1)} %get-tuple-element.40, s32[512]{0:T(512)S(1)} %get-tuple-element.43, s32[]{:T(128)S(6)} %axis_index.67, ...), kind=kOutput, calls=%fused_computation.1 | convolution fusion | flops 1092878336 | bytes 4212748 | tf_op jit(solution)/shard_map/dot_general | solution.py:42
  40.1 5.5 %collective-permute-done.9 = bf16[128,2048]{1,0:T(8,128)(2,1)S(1)} collective-permute-done((bf16[128,2048]{1,0:T(8,128)(2,1)}, bf16[128,2048]{1,0:T(8,128)(2,1)S(1)}, u32[]{:S(2)}, u32[]{:S(2)}) %collective-permute-start.9) | collective-permute-done | bytes 524320 | tf_op jit(solution)/shard_map/ppermute | solution.py:31
  45.7 10.8 %collective-permute-done.8 = bf16[128,2048]{1,0:T(8,128)(2,1)S(1)} collective-permute-done((bf16[128,2048]{1,0:T(8,128)(2,1)}, bf16[128,2048]{1,0:T(8,128)(2,1)S(1)}, u32[]{:S(2)}, u32[]{:S(2)}) %collective-permute-start.8) | collective-permute-done | bytes 524320 | tf_op jit(solution)/shard_map/ppermute | solution.py:31
  57.3 5.9 %fusion.13 = f32[512,1024]{1,0:T(8,128)} fusion(bf16[512,1024]{1,0:T(8,128)(2,1)} %constant_dynamic-update-slice_fusion, bf16[2048,512]{1,0:T(8,128)(2,1)} %convolution_convert_fusion.1, bf16[128,2048]{1,0:T(8,128)(2,1)} %collective-permute-done.10, bf16[128,2048]{1,0:T(8,128)(2,1)} %copy-done.8, bf16[128,2048]{1,0:T(8,128)(2,1)} %copy-done.9, ...), kind=kOutput, calls=%fused_computation.32 | convolution fusion | flops 1619263488 | bytes 7340032 | tf_op jit(solution)/shard_map/dot_general | solution.py:42
  63.1 1.4 slice.78
  64.8 14.1 %collective-permute-start.3 = (bf16[512,1024]{1,0:T(8,128)(2,1)S(1)}, bf16[512,1024]{1,0:T(8,128)(2,1)S(1)}, u32[]{:S(2)}, u32[]{:S(2)}) collective-permute-start(bf16[512,1024]{1,0:T(8,128)(2,1)S(1)} %constant_dynamic-slice_fusion.5), channel_id=1, source_target_pairs={{0,1},{1,0},{2,3},{3,2},{4,5},{5,4},{6,7},{7,6},{8,9},{9,8},{10,11... | collective-permute-start | bytes 3145736 | tf_op jit(solution)/shard_map/ppermute | solution.py:31
  79.6 2.6 %collective-permute-start.15 = (bf16[64,1024]{1,0:T(8,128)(2,1)S(1)}, bf16[64,1024]{1,0:T(8,128)(2,1)S(1)}, u32[]{:S(2)}, u32[]{:S(2)}) collective-permute-start(bf16[64,1024]{1,0:T(8,128)(2,1)S(1)} %get-tuple-element.18), channel_id=1, source_target_pairs={{0,32},{16,48},{32,0},{48,16},{1,33},{17,49},{33,1},{49,17},{2,34}... | collective-permute-start | bytes 393224 | tf_op jit(solution)/shard_map/ppermute | solution.py:31
  82.2 1.9 collective-permute-start.14
  84.8 3.8 %collective-permute-done.15 = bf16[64,1024]{1,0:T(8,128)(2,1)S(1)} collective-permute-done((bf16[64,1024]{1,0:T(8,128)(2,1)S(1)}, bf16[64,1024]{1,0:T(8,128)(2,1)S(1)}, u32[]{:S(2)}, u32[]{:S(2)}) %collective-permute-start.15) | collective-permute-done | bytes 131104 | tf_op jit(solution)/shard_map/ppermute | solution.py:31
  89.7 3.1 %collective-permute-start.18 = (bf16[16,1024]{1,0:T(8,128)(2,1)S(1)}, bf16[16,1024]{1,0:T(8,128)(2,1)S(1)}, u32[]{:S(2)}, u32[]{:S(2)}) collective-permute-start(bf16[16,1024]{1,0:T(8,128)(2,1)S(1)} %get-tuple-element.27), channel_id=1, source_target_pairs={{0,128},{64,192},{128,0},{192,64},{1,129},{65,193},{129,1},{193,65... | collective-permute-start | bytes 98312 | tf_op jit(solution)/shard_map/ppermute | solution.py:31
  92.8 0.9 collective-permute-start.17
  93.6 30.6 %collective-permute-done.19 = bf16[16,1024]{1,0:T(8,128)(2,1)S(1)} collective-permute-done((bf16[16,1024]{1,0:T(8,128)(2,1)S(1)}, bf16[16,1024]{1,0:T(8,128)(2,1)S(1)}, u32[]{:S(2)}, u32[]{:S(2)}) %collective-permute-start.19) | collective-permute-done | bytes 32800 | tf_op jit(solution)/shard_map/ppermute | solution.py:31
  124.3 2.1 %collective-permute-done.18 = bf16[16,1024]{1,0:T(8,128)(2,1)S(1)} collective-permute-done((bf16[16,1024]{1,0:T(8,128)(2,1)S(1)}, bf16[16,1024]{1,0:T(8,128)(2,1)S(1)}, u32[]{:S(2)}, u32[]{:S(2)}) %collective-permute-start.18) | collective-permute-done | bytes 32800 | tf_op jit(solution)/shard_map/ppermute | solution.py:31
  127.8 7.2 %collective-permute-done.20 = f32[16,1024]{1,0:T(8,128)S(1)} collective-permute-done((f32[16,1024]{1,0:T(8,128)S(1)}, f32[16,1024]{1,0:T(8,128)S(1)}, u32[]{:S(2)}, u32[]{:S(2)}) %collective-permute-start.20) | collective-permute-done | bytes 65568 | tf_op jit(solution)/shard_map/ppermute | solution.py:31
  135.1 3.2 %collective-permute-start.23 = (f32[16,1024]{1,0:T(8,128)S(1)}, f32[16,1024]{1,0:T(8,128)S(1)}, u32[]{:S(2)}, u32[]{:S(2)}) collective-permute-start(f32[16,1024]{1,0:T(8,128)S(1)} %add.213), channel_id=1, source_target_pairs={{0,6},{2,0},{4,2},{6,4},{1,7},{3,1},{5,3},{7,5},{8,14},{10,8},{12,... | collective-permute-start | bytes 196616 | tf_op jit(solution)/shard_map/ppermute | solution.py:31
  138.5 2.8 %collective-permute-done.22 = f32[16,1024]{1,0:T(8,128)S(1)} collective-permute-done((f32[16,1024]{1,0:T(8,128)S(1)}, f32[16,1024]{1,0:T(8,128)S(1)}, u32[]{:S(2)}, u32[]{:S(2)}) %collective-permute-start.22) | collective-permute-done | bytes 65568 | tf_op jit(solution)/shard_map/ppermute | solution.py:31
  141.3 2.8 %collective-permute-done.21 = f32[16,1024]{1,0:T(8,128)S(1)} collective-permute-done((f32[16,1024]{1,0:T(8,128)S(1)}, f32[16,1024]{1,0:T(8,128)S(1)}, u32[]{:S(2)}, u32[]{:S(2)}) %collective-permute-start.21) | collective-permute-done | bytes 65568 | tf_op jit(solution)/shard_map/ppermute | solution.py:31
  144.8 4.3 %collective-permute-start.24 = (bf16[16,1024]{1,0:T(8,128)(2,1)S(1)}, bf16[16,1024]{1,0:T(8,128)(2,1)S(1)}, u32[]{:S(2)}, u32[]{:S(2)}) collective-permute-start(bf16[16,1024]{1,0:T(8,128)(2,1)S(1)} %get-tuple-element.5), channel_id=1, source_target_pairs={{0,192},{64,0},{128,64},{192,128},{1,193},{65,1},{129,65},{193,129... | collective-permute-start | bytes 98312 | tf_op jit(solution)/shard_map/ppermute | solution.py:31
  149.2 1.1 collective-permute-start.25
  150.3 2.0 %collective-permute-start.26 = (bf16[16,1024]{1,0:T(8,128)(2,1)S(1)}, bf16[16,1024]{1,0:T(8,128)(2,1)S(1)}, u32[]{:S(2)}, u32[]{:S(2)}) collective-permute-start(bf16[16,1024]{1,0:T(8,128)(2,1)S(1)} %get-tuple-element.5), channel_id=1, source_target_pairs={{0,64},{64,128},{128,192},{192,0},{1,65},{65,129},{129,193},{193,1... | collective-permute-start | bytes 98312 | tf_op jit(solution)/shard_map/ppermute | solution.py:31
  152.9 1.4 collective-permute-done.25
  154.3 1.7 collective-permute-done.26
  156.5 2.6 %collective-permute-start.28 = (bf16[64,1024]{1,0:T(8,128)(2,1)S(1)}, bf16[64,1024]{1,0:T(8,128)(2,1)S(1)}, u32[]{:S(2)}, u32[]{:S(2)}) collective-permute-start(bf16[64,1024]{1,0:T(8,128)(2,1)S(1)} %pad_maximum_fusion), channel_id=1, source_target_pairs={{0,32},{16,48},{32,0},{48,16},{1,33},{17,49},{33,1},{49,17},{2,34}... | collective-permute-start | bytes 393224 | tf_op jit(solution)/shard_map/ppermute | solution.py:31
  159.1 1.9 collective-permute-start.29
  165.3 2.4 %convolution_convert_fusion = bf16[512,2048]{1,0:T(8,128)(2,1)S(1)} fusion(bf16[512,1024]{1,0:T(8,128)(2,1)S(1)} %copy-done.7, bf16[2048,1024]{1,0:T(8,128)(2,1)S(1)} %constant_dynamic-update-slice_fusion.25), kind=kOutput, calls=%fused_computation | convolution fusion | flops 2148532224 | bytes 7340032 | tf_op jit(solution)/shard_map/dot_general | solution.py:42
  167.9 1.2 fusion.49
  170.0 1.1 collective-permute-start.7
  171.1 0.8 constant_dynamic-update-slice_fusion.11
  172.0 5.1 %fusion.8 = f32[1024,1024]{1,0:T(8,128)} fusion(bf16[512,1024]{1,0:T(8,128)(2,1)} %constant_dynamic-update-slice_fusion.11, bf16[1024,512]{1,0:T(8,128)(2,1)S(1)} %copy-done.1, s32[512]{0:T(512)S(1)} %get-tuple-element.39, s32[512]{0:T(512)S(1)} %get-tuple-element.42, s32[512]{0:T(512)S(1)} %get-tuple-element.40, s32[512]{0:T(512)S(1)} %get-tuple-element.43, ...), kind=kOutput, calls=%fused_computation.30 | convolution fusion | flops 1629487104 | bytes 6309900 | tf_op jit(solution)/shard_map/dot_general | solution.py:42
  177.1 7.1 %collective-permute-done.5 = bf16[128,2048]{1,0:T(8,128)(2,1)} collective-permute-done((bf16[128,2048]{1,0:T(8,128)(2,1)}, bf16[128,2048]{1,0:T(8,128)(2,1)}, u32[]{:S(2)}, u32[]{:S(2)}) %collective-permute-start.5) | collective-permute-done | bytes 524320 | tf_op jit(solution)/shard_map/ppermute | solution.py:31
  184.1 1.1 constant_dynamic-update-slice_fusion.24
  185.2 0.9 collective-permute-done.6
  186.1 1.1 constant_dynamic-update-slice_fusion.23
  187.2 9.4 %collective-permute-done.7 = bf16[128,2048]{1,0:T(8,128)(2,1)} collective-permute-done((bf16[128,2048]{1,0:T(8,128)(2,1)}, bf16[128,2048]{1,0:T(8,128)(2,1)}, u32[]{:S(2)}, u32[]{:S(2)}) %collective-permute-start.7) | collective-permute-done | bytes 524320 | tf_op jit(solution)/shard_map/ppermute | solution.py:31
  196.6 1.1 constant_dynamic-update-slice_fusion.22
  197.7 1.3 copy-done.2
  (81 shorter events, 14.9 us)
Async XLA Ops:
  0.6 28.5 %collective-permute-start = (bf16[128,1024]{1,0:T(8,128)(2,1)}, bf16[128,1024]{1,0:T(8,128)(2,1)}, u32[]{:S(2)}, u32[]{:S(2)}) collective-permute-start(bf16[128,1024]{1,0:T(8,128)(2,1)} %param.7), channel_id=1, source_target_pairs={{0,2},{2,4},{4,6},{6,0},{1,3},{3,5},{5,7},{7,1},{8,10},{10,12},{12... | collective-permute-start | bytes 786440 | tf_op jit(solution)/shard_map/ppermute | solution.py:31
  2.2 29.2 %collective-permute-start.1 = (bf16[128,1024]{1,0:T(8,128)(2,1)}, bf16[128,1024]{1,0:T(8,128)(2,1)}, u32[]{:S(2)}, u32[]{:S(2)}) collective-permute-start(bf16[128,1024]{1,0:T(8,128)(2,1)} %param.7), channel_id=1, source_target_pairs={{0,4},{2,6},{4,0},{6,2},{1,5},{3,7},{5,1},{7,3},{8,12},{10,14},{12... | collective-permute-start | bytes 786440 | tf_op jit(solution)/shard_map/ppermute | solution.py:31
  4.9 28.8 %collective-permute-start.2 = (bf16[128,1024]{1,0:T(8,128)(2,1)}, bf16[128,1024]{1,0:T(8,128)(2,1)}, u32[]{:S(2)}, u32[]{:S(2)}) collective-permute-start(bf16[128,1024]{1,0:T(8,128)(2,1)} %param.7), channel_id=1, source_target_pairs={{0,6},{2,0},{4,2},{6,4},{1,7},{3,1},{5,3},{7,5},{8,14},{10,8},{12,... | collective-permute-start | bytes 786440 | tf_op jit(solution)/shard_map/ppermute | solution.py:31
  8.2 20.8 %collective-permute-start.11 = (bf16[512,512]{1,0:T(8,128)(2,1)}, bf16[512,512]{1,0:T(8,128)(2,1)}, u32[]{:S(2)}, u32[]{:S(2)}) collective-permute-start(bf16[512,512]{1,0:T(8,128)(2,1)} %constant_dynamic-slice_fusion), channel_id=1, source_target_pairs={{0,1},{1,0},{2,3},{3,2},{4,5},{5,4},{6,7},{7,6},{8,9},{9,8},{10,11... | collective-permute-start | bytes 1572872 | tf_op jit(solution)/shard_map/ppermute | solution.py:31
  15.4 3.0 %copy-start.4 = (bf16[128,1024]{1,0:T(8,128)(2,1)S(1)}, bf16[128,1024]{1,0:T(8,128)(2,1)}, u32[]{:S(2)}) copy-start(bf16[128,1024]{1,0:T(8,128)(2,1)} %param.7) | copy-start | bytes 786436
  18.3 1.3 copy-start.1
  18.3 21.8 %collective-permute-start.10 = (bf16[128,2048]{1,0:T(8,128)(2,1)}, bf16[128,2048]{1,0:T(8,128)(2,1)}, u32[]{:S(2)}, u32[]{:S(2)}) collective-permute-start(bf16[128,2048]{1,0:T(8,128)(2,1)} %get-tuple-element.10), channel_id=1, source_target_pairs={{0,6},{2,0},{4,2},{6,4},{1,7},{3,1},{5,3},{7,5},{8,14},{10,8},{12,... | collective-permute-start | bytes 1572872 | tf_op jit(solution)/shard_map/ppermute | solution.py:31
  29.1 7.4 %collective-permute-start.12 = (bf16[512,512]{1,0:T(8,128)(2,1)}, bf16[512,512]{1,0:T(8,128)(2,1)}, u32[]{:S(2)}, u32[]{:S(2)}) collective-permute-start(bf16[512,512]{1,0:T(8,128)(2,1)} %collective-permute-done.11), channel_id=1, source_target_pairs={{0,8},{8,0},{1,9},{9,1},{2,10},{10,2},{3,11},{11,3},{4,12},{12,4},... | collective-permute-start | bytes 1572872 | tf_op jit(solution)/shard_map/ppermute | solution.py:31
  29.1 16.6 %collective-permute-start.9 = (bf16[128,2048]{1,0:T(8,128)(2,1)}, bf16[128,2048]{1,0:T(8,128)(2,1)S(1)}, u32[]{:S(2)}, u32[]{:S(2)}) collective-permute-start(bf16[128,2048]{1,0:T(8,128)(2,1)} %get-tuple-element.11), channel_id=1, source_target_pairs={{0,4},{2,6},{4,0},{6,2},{1,5},{3,7},{5,1},{7,3},{8,12},{10,14},{12... | collective-permute-start | bytes 1572872 | tf_op jit(solution)/shard_map/ppermute | solution.py:31
  31.4 25.1 %collective-permute-start.8 = (bf16[128,2048]{1,0:T(8,128)(2,1)}, bf16[128,2048]{1,0:T(8,128)(2,1)S(1)}, u32[]{:S(2)}, u32[]{:S(2)}) collective-permute-start(bf16[128,2048]{1,0:T(8,128)(2,1)} %get-tuple-element.9), channel_id=1, source_target_pairs={{0,2},{2,4},{4,6},{6,0},{1,3},{3,5},{5,7},{7,1},{8,10},{10,12},{12... | collective-permute-start | bytes 1572872 | tf_op jit(solution)/shard_map/ppermute | solution.py:31
  45.7 10.8 %copy-start.8 = (bf16[128,2048]{1,0:T(8,128)(2,1)}, bf16[128,2048]{1,0:T(8,128)(2,1)S(1)}, u32[]{:S(2)}) copy-start(bf16[128,2048]{1,0:T(8,128)(2,1)S(1)} %collective-permute-done.9) | copy-start | bytes 1572868
  56.5 0.8 copy-start.9
  57.3 7.4 %copy-start = (bf16[1024,1024]{1,0:T(8,128)(2,1)S(1)}, bf16[1024,1024]{1,0:T(8,128)(2,1)}, u32[]{:S(2)}) copy-start(bf16[1024,1024]{1,0:T(8,128)(2,1)} %param.8) | copy-start | bytes 6291460
  63.1 15.8 %copy-start.3 = (f32[512,1024]{1,0:T(8,128)S(1)}, f32[512,1024]{1,0:T(8,128)}, u32[]{:S(2)}) copy-start(f32[512,1024]{1,0:T(8,128)} %fusion.13) | copy-start | bytes 6291460
  64.6 14.3 %collective-permute-start.13 = (bf16[256,1024]{1,0:T(8,128)(2,1)S(1)}, bf16[256,1024]{1,0:T(8,128)(2,1)S(1)}, u32[]{:S(2)}, u32[]{:S(2)}) collective-permute-start(bf16[256,1024]{1,0:T(8,128)(2,1)S(1)} %slice.78), channel_id=1, source_target_pairs={{0,8},{8,0},{1,9},{9,1},{2,10},{10,2},{3,11},{11,3},{4,12},{12,4},... | collective-permute-start | bytes 1572872 | tf_op jit(solution)/shard_map/ppermute | solution.py:31
  64.8 62.9 %collective-permute-start.3 = (bf16[512,1024]{1,0:T(8,128)(2,1)S(1)}, bf16[512,1024]{1,0:T(8,128)(2,1)S(1)}, u32[]{:S(2)}, u32[]{:S(2)}) collective-permute-start(bf16[512,1024]{1,0:T(8,128)(2,1)S(1)} %constant_dynamic-slice_fusion.5), channel_id=1, source_target_pairs={{0,1},{1,0},{2,3},{3,2},{4,5},{5,4},{6,7},{7,6},{8,9},{9,8},{10,11... | collective-permute-start | bytes 3145736 | tf_op jit(solution)/shard_map/ppermute | solution.py:31
  79.1 5.7 %collective-permute-start.16 = (bf16[64,1024]{1,0:T(8,128)(2,1)S(1)}, bf16[64,1024]{1,0:T(8,128)(2,1)S(1)}, u32[]{:S(2)}, u32[]{:S(2)}) collective-permute-start(bf16[64,1024]{1,0:T(8,128)(2,1)S(1)} %get-tuple-element.17), channel_id=1, source_target_pairs={{0,48},{16,0},{32,16},{48,32},{1,49},{17,1},{33,17},{49,33},{2,50}... | collective-permute-start | bytes 393224 | tf_op jit(solution)/shard_map/ppermute | solution.py:31
  79.6 9.0 %collective-permute-start.15 = (bf16[64,1024]{1,0:T(8,128)(2,1)S(1)}, bf16[64,1024]{1,0:T(8,128)(2,1)S(1)}, u32[]{:S(2)}, u32[]{:S(2)}) collective-permute-start(bf16[64,1024]{1,0:T(8,128)(2,1)S(1)} %get-tuple-element.18), channel_id=1, source_target_pairs={{0,32},{16,48},{32,0},{48,16},{1,33},{17,49},{33,1},{49,17},{2,34}... | collective-permute-start | bytes 393224 | tf_op jit(solution)/shard_map/ppermute | solution.py:31
  82.2 7.1 %collective-permute-start.14 = (bf16[64,1024]{1,0:T(8,128)(2,1)S(1)}, bf16[64,1024]{1,0:T(8,128)(2,1)S(1)}, u32[]{:S(2)}, u32[]{:S(2)}) collective-permute-start(bf16[64,1024]{1,0:T(8,128)(2,1)S(1)} %get-tuple-element.16), channel_id=1, source_target_pairs={{0,16},{16,32},{32,48},{48,0},{1,17},{17,33},{33,49},{49,1},{2,18}... | collective-permute-start | bytes 393224 | tf_op jit(solution)/shard_map/ppermute | solution.py:31
  89.4 34.8 %collective-permute-start.19 = (bf16[16,1024]{1,0:T(8,128)(2,1)S(1)}, bf16[16,1024]{1,0:T(8,128)(2,1)S(1)}, u32[]{:S(2)}, u32[]{:S(2)}) collective-permute-start(bf16[16,1024]{1,0:T(8,128)(2,1)S(1)} %get-tuple-element.26), channel_id=1, source_target_pairs={{0,192},{64,0},{128,64},{192,128},{1,193},{65,1},{129,65},{193,129... | collective-permute-start | bytes 98312 | tf_op jit(solution)/shard_map/ppermute | solution.py:31
  89.7 36.7 %collective-permute-start.18 = (bf16[16,1024]{1,0:T(8,128)(2,1)S(1)}, bf16[16,1024]{1,0:T(8,128)(2,1)S(1)}, u32[]{:S(2)}, u32[]{:S(2)}) collective-permute-start(bf16[16,1024]{1,0:T(8,128)(2,1)S(1)} %get-tuple-element.27), channel_id=1, source_target_pairs={{0,128},{64,192},{128,0},{192,64},{1,129},{65,193},{129,1},{193,65... | collective-permute-start | bytes 98312 | tf_op jit(solution)/shard_map/ppermute | solution.py:31
  92.8 34.0 %collective-permute-start.17 = (bf16[16,1024]{1,0:T(8,128)(2,1)S(1)}, bf16[16,1024]{1,0:T(8,128)(2,1)S(1)}, u32[]{:S(2)}, u32[]{:S(2)}) collective-permute-start(bf16[16,1024]{1,0:T(8,128)(2,1)S(1)} %get-tuple-element.25), channel_id=1, source_target_pairs={{0,64},{64,128},{128,192},{192,0},{1,65},{65,129},{129,193},{193,1... | collective-permute-start | bytes 98312 | tf_op jit(solution)/shard_map/ppermute | solution.py:31
  126.8 8.3 %collective-permute-start.20 = (f32[16,1024]{1,0:T(8,128)S(1)}, f32[16,1024]{1,0:T(8,128)S(1)}, u32[]{:S(2)}, u32[]{:S(2)}) collective-permute-start(f32[16,1024]{1,0:T(8,128)S(1)} %convert_add_fusion), channel_id=1, source_target_pairs={{0,1},{1,0},{2,3},{3,2},{4,5},{5,4},{6,7},{7,6},{8,9},{9,8},{10,11... | collective-permute-start | bytes 196616 | tf_op jit(solution)/shard_map/ppermute | solution.py:31
  127.7 16.5 %copy-start.5 = (f32[16,1024]{1,0:T(8,128)S(1)}, f32[16,1024]{1,0:T(8,128)}, u32[]{:S(2)}) copy-start(f32[16,1024]{1,0:T(8,128)} %param.10) | copy-start | bytes 196612
  127.7 16.4 %copy-start.6 = (f32[16,1024]{1,0:T(8,128)S(1)}, f32[16,1024]{1,0:T(8,128)}, u32[]{:S(2)}) copy-start(f32[16,1024]{1,0:T(8,128)} %param.11) | copy-start | bytes 196612
  127.7 37.5 %collective-permute-start.4 = (bf16[512,1024]{1,0:T(8,128)(2,1)S(1)}, bf16[512,1024]{1,0:T(8,128)(2,1)S(1)}, u32[]{:S(2)}, u32[]{:S(2)}) collective-permute-start(bf16[512,1024]{1,0:T(8,128)(2,1)S(1)} %collective-permute-done.3), channel_id=1, source_target_pairs={{0,8},{8,0},{1,9},{9,1},{2,10},{10,2},{3,11},{11,3},{4,12},{12,4},... | collective-permute-start | bytes 3145736 | tf_op jit(solution)/shard_map/ppermute | solution.py:31
  135.0 6.3 %collective-permute-start.22 = (f32[16,1024]{1,0:T(8,128)S(1)}, f32[16,1024]{1,0:T(8,128)S(1)}, u32[]{:S(2)}, u32[]{:S(2)}) collective-permute-start(f32[16,1024]{1,0:T(8,128)S(1)} %add.213), channel_id=1, source_target_pairs={{0,2},{2,4},{4,6},{6,0},{1,3},{3,5},{5,7},{7,1},{8,10},{10,12},{12... | collective-permute-start | bytes 196616 | tf_op jit(solution)/shard_map/ppermute | solution.py:31
  135.1 6.2 %collective-permute-start.23 = (f32[16,1024]{1,0:T(8,128)S(1)}, f32[16,1024]{1,0:T(8,128)S(1)}, u32[]{:S(2)}, u32[]{:S(2)}) collective-permute-start(f32[16,1024]{1,0:T(8,128)S(1)} %add.213), channel_id=1, source_target_pairs={{0,6},{2,0},{4,2},{6,4},{1,7},{3,1},{5,3},{7,5},{8,14},{10,8},{12,... | collective-permute-start | bytes 196616 | tf_op jit(solution)/shard_map/ppermute | solution.py:31
  138.3 5.8 %collective-permute-start.21 = (f32[16,1024]{1,0:T(8,128)S(1)}, f32[16,1024]{1,0:T(8,128)S(1)}, u32[]{:S(2)}, u32[]{:S(2)}) collective-permute-start(f32[16,1024]{1,0:T(8,128)S(1)} %add.213), channel_id=1, source_target_pairs={{0,4},{2,6},{4,0},{6,2},{1,5},{3,7},{5,1},{7,3},{8,12},{10,14},{12... | collective-permute-start | bytes 196616 | tf_op jit(solution)/shard_map/ppermute | solution.py:31
  144.8 20.5 %copy-start.7 = (bf16[512,1024]{1,0:T(8,128)(2,1)S(1)}, bf16[512,1024]{1,0:T(8,128)(2,1)}, u32[]{:S(2)}) copy-start(bf16[512,1024]{1,0:T(8,128)(2,1)} %constant_dynamic-update-slice_fusion) | copy-start | bytes 3145732
  144.8 8.1 %collective-permute-start.24 = (bf16[16,1024]{1,0:T(8,128)(2,1)S(1)}, bf16[16,1024]{1,0:T(8,128)(2,1)S(1)}, u32[]{:S(2)}, u32[]{:S(2)}) collective-permute-start(bf16[16,1024]{1,0:T(8,128)(2,1)S(1)} %get-tuple-element.5), channel_id=1, source_target_pairs={{0,192},{64,0},{128,64},{192,128},{1,193},{65,1},{129,65},{193,129... | collective-permute-start | bytes 98312 | tf_op jit(solution)/shard_map/ppermute | solution.py:31
  149.2 5.2 %collective-permute-start.25 = (bf16[16,1024]{1,0:T(8,128)(2,1)S(1)}, bf16[16,1024]{1,0:T(8,128)(2,1)S(1)}, u32[]{:S(2)}, u32[]{:S(2)}) collective-permute-start(bf16[16,1024]{1,0:T(8,128)(2,1)S(1)} %get-tuple-element.5), channel_id=1, source_target_pairs={{0,128},{64,192},{128,0},{192,64},{1,129},{65,193},{129,1},{193,65... | collective-permute-start | bytes 98312 | tf_op jit(solution)/shard_map/ppermute | solution.py:31
  150.3 5.7 %collective-permute-start.26 = (bf16[16,1024]{1,0:T(8,128)(2,1)S(1)}, bf16[16,1024]{1,0:T(8,128)(2,1)S(1)}, u32[]{:S(2)}, u32[]{:S(2)}) collective-permute-start(bf16[16,1024]{1,0:T(8,128)(2,1)S(1)} %get-tuple-element.5), channel_id=1, source_target_pairs={{0,64},{64,128},{128,192},{192,0},{1,65},{65,129},{129,193},{193,1... | collective-permute-start | bytes 98312 | tf_op jit(solution)/shard_map/ppermute | solution.py:31
  156.0 6.9 %collective-permute-start.27 = (bf16[64,1024]{1,0:T(8,128)(2,1)S(1)}, bf16[64,1024]{1,0:T(8,128)(2,1)S(1)}, u32[]{:S(2)}, u32[]{:S(2)}) collective-permute-start(bf16[64,1024]{1,0:T(8,128)(2,1)S(1)} %pad_maximum_fusion), channel_id=1, source_target_pairs={{0,48},{16,0},{32,16},{48,32},{1,49},{17,1},{33,17},{49,33},{2,50}... | collective-permute-start | bytes 393224 | tf_op jit(solution)/shard_map/ppermute | solution.py:31
  156.5 7.1 %collective-permute-start.28 = (bf16[64,1024]{1,0:T(8,128)(2,1)S(1)}, bf16[64,1024]{1,0:T(8,128)(2,1)S(1)}, u32[]{:S(2)}, u32[]{:S(2)}) collective-permute-start(bf16[64,1024]{1,0:T(8,128)(2,1)S(1)} %pad_maximum_fusion), channel_id=1, source_target_pairs={{0,32},{16,48},{32,0},{48,16},{1,33},{17,49},{33,1},{49,17},{2,34}... | collective-permute-start | bytes 393224 | tf_op jit(solution)/shard_map/ppermute | solution.py:31
  159.1 5.4 %collective-permute-start.29 = (bf16[64,1024]{1,0:T(8,128)(2,1)S(1)}, bf16[64,1024]{1,0:T(8,128)(2,1)S(1)}, u32[]{:S(2)}, u32[]{:S(2)}) collective-permute-start(bf16[64,1024]{1,0:T(8,128)(2,1)S(1)} %pad_maximum_fusion), channel_id=1, source_target_pairs={{0,16},{16,32},{32,48},{48,0},{1,17},{17,33},{33,49},{49,1},{2,18}... | collective-permute-start | bytes 393224 | tf_op jit(solution)/shard_map/ppermute | solution.py:31
  165.2 5.9 %collective-permute-start.30 = (bf16[256,1024]{1,0:T(8,128)(2,1)S(1)}, bf16[256,1024]{1,0:T(8,128)(2,1)S(1)}, u32[]{:S(2)}, u32[]{:S(2)}) collective-permute-start(bf16[256,1024]{1,0:T(8,128)(2,1)S(1)} %get-tuple-element.19), channel_id=1, source_target_pairs={{0,8},{8,0},{1,9},{9,1},{2,10},{10,2},{3,11},{11,3},{4,12},{12,4},... | collective-permute-start | bytes 1572872 | tf_op jit(solution)/shard_map/ppermute | solution.py:31
  169.1 15.0 %collective-permute-start.5 = (bf16[128,2048]{1,0:T(8,128)(2,1)}, bf16[128,2048]{1,0:T(8,128)(2,1)}, u32[]{:S(2)}, u32[]{:S(2)}) collective-permute-start(bf16[128,2048]{1,0:T(8,128)(2,1)} %get-tuple-element.14), channel_id=1, source_target_pairs={{0,6},{2,0},{4,2},{6,4},{1,7},{3,1},{5,3},{7,5},{8,14},{10,8},{12,... | collective-permute-start | bytes 1572872 | tf_op jit(solution)/shard_map/ppermute | solution.py:31
  169.5 16.6 %collective-permute-start.6 = (bf16[128,2048]{1,0:T(8,128)(2,1)}, bf16[128,2048]{1,0:T(8,128)(2,1)}, u32[]{:S(2)}, u32[]{:S(2)}) collective-permute-start(bf16[128,2048]{1,0:T(8,128)(2,1)} %get-tuple-element.13), channel_id=1, source_target_pairs={{0,4},{2,6},{4,0},{6,2},{1,5},{3,7},{5,1},{7,3},{8,12},{10,14},{12... | collective-permute-start | bytes 1572872 | tf_op jit(solution)/shard_map/ppermute | solution.py:31
  170.0 26.6 %collective-permute-start.7 = (bf16[128,2048]{1,0:T(8,128)(2,1)}, bf16[128,2048]{1,0:T(8,128)(2,1)}, u32[]{:S(2)}, u32[]{:S(2)}) collective-permute-start(bf16[128,2048]{1,0:T(8,128)(2,1)} %get-tuple-element.12), channel_id=1, source_target_pairs={{0,2},{2,4},{4,6},{6,0},{1,3},{3,5},{5,7},{7,1},{8,10},{10,12},{12... | collective-permute-start | bytes 1572872 | tf_op jit(solution)/shard_map/ppermute | solution.py:31
  197.7 1.3 copy-start.2

commit v2 on v1

v2 whole, which is shorter than its diff:
```python
import functools
import itertools

import jax
import jax.numpy as jnp
from jax import lax
from jax.experimental import pallas as pl
from jax.experimental.pallas import tpu as pltpu
from jax.sharding import Mesh
from jax.sharding import PartitionSpec as P

beta_one = 0.9
beta_two = 0.999
bias_one = 0.999973438601112
bias_two = 0.0952078528862904
epsilon = 1e-08

NAMES = ("zl", "y", "c", "x", "zh")
SIZES = {"zl": 4, "y": 4, "c": 2, "x": 4, "zh": 2}
DP = ("zl", "y", "c")
SHARD = ("x", "zh")
WIDE = jnp.float32
NARROW = jnp.bfloat16


def send(value, **shift):
    axes = tuple(name for name in NAMES if name in shift)
    sizes = [SIZES[name] for name in axes]
    flat = {at: i for i, at in enumerate(itertools.product(*map(range, sizes)))}
    pairs = [
        (i, flat[tuple((p + shift[n]) % s for p, n, s in zip(at, axes, sizes))])
        for at, i in flat.items()
    ]
    return lax.ppermute(value, axes, pairs)


def adam_step(projected_grad, first_moment, second_moment):
    new_first = beta_one * first_moment + (1.0 - beta_one) * projected_grad
    new_second = beta_two * second_moment + (1.0 - beta_two) * projected_grad * projected_grad
    direction = new_first / bias_one / (jnp.sqrt(new_second / bias_two) + epsilon)
    return (new_first, new_second, direction.astype(NARROW))


def dot(a, b, contract):
    return lax.dot_general(a, b, ((contract[:1], contract[1:]), ((), ())), preferred_element_type=WIDE)


def slot_permutation(turned):
    row = lax.broadcasted_iota(jnp.int32, (512, 512), 0)
    slot = lax.broadcasted_iota(jnp.int32, (512, 512), 1)
    cc, dy, dz, low = slot // 256, slot // 64 % 4, slot // 16 % 4, slot % 16
    zl = (lax.axis_index("zl") + dz) % 4 if turned else dz
    y = (lax.axis_index("y") + dy) % 4
    c = (lax.axis_index("c") + cc) % 2
    return (row == ((zl * 4 + y) * 2 + c) * 16 + low).astype(NARROW)


def fold(slots, axis):
    rows = slots.shape[0] // 4
    total = slots[:rows].astype(WIDE)
    for s in (1, 2, 3):
        total = total + send(slots[rows * s : rows * s + rows], **{axis: s}).astype(WIDE)
    return total


def spread(own, axis):
    return join([own] + [send(own, **{axis: -s}) for s in (1, 2, 3)])


def after(value, *others):
    return lax.optimization_barrier((value,) + others)[0]


def join(parts):
    rows, low = parts[0].shape[0], jnp.array(-jnp.inf, parts[0].dtype)
    padded = [
        lax.pad(part, low, ((i * rows, (len(parts) - 1 - i) * rows, 0), (0, 0, 0)))
        for i, part in enumerate(parts)
    ]
    return functools.reduce(jnp.maximum, padded)


def share_of(mine, ways):
    rows = mine.shape[0] // 2 // ways
    at = (lax.axis_index("c") * ways + lax.axis_index("y") % ways) * rows
    return lax.dynamic_slice_in_dim(mine, at, rows, 0)


def assemble(mine, part, other):
    half = part.shape[0]
    c, zh = lax.axis_index("c"), lax.axis_index("zh")
    both = jnp.zeros((4 * half, mine.shape[1]), mine.dtype)
    both = lax.dynamic_update_slice_in_dim(both, mine, zh * 2 * half, 0)
    both = lax.dynamic_update_slice_in_dim(both, part, (1 - zh) * 2 * half + c * half, 0)
    return lax.dynamic_update_slice_in_dim(both, other, (1 - zh) * 2 * half + (1 - c) * half, 0)


def place_kernel(*refs):
    blocks, out = refs[:4], refs[4]
    c, x, y, zh = (lax.axis_index(name) for name in ("c", "x", "y", "zh"))
    for s, block in enumerate(blocks):
        base = lax.rem(x + s, 4) * 2048
        other = base + (1 - zh) * 1024
        spots = [(0, 1024, base + zh * 1024)]
        for cc, dy in itertools.product(range(2), range(4)):
            to = other + lax.rem(c + cc, 2) * 512 + lax.rem(y + dy, 4) * 128
            spots.append((1024 + (cc * 4 + dy) * 128, 128, to))
        for at, size, to in spots:
            out[:, pl.ds(pl.multiple_of(to, 128), size)] = block[:, at : at + size]


def place(blocks):
    return pl.pallas_call(
        place_kernel,
        out_shape=jax.ShapeDtypeStruct((128, 8192), NARROW),
        in_specs=[pl.BlockSpec(memory_space=pltpu.VMEM)] * 4,
        out_specs=pl.BlockSpec(memory_space=pltpu.VMEM),
        cost_estimate=pl.CostEstimate(flops=0, bytes_accessed=4 << 20, transcendentals=0),
        compiler_params=pltpu.CompilerParams(vmem_limit_bytes=16 << 20),
    )(*blocks)


def pair(value):
    return lax.ppermute(value, "y", [(0, 1), (1, 0), (2, 3), (3, 2)])


def body(inputs, grad_out, weight, projector, first_moment, second_moment):
    x, y = lax.axis_index("x"), lax.axis_index("y")

    columns = [lax.dynamic_slice_in_dim(inputs, (x + s) % 4 * 2048, 2048, 1) for s in range(4)]
    cut = [jnp.concatenate([columns[s], grad_out], 1) for s in (1, 2, 3)]
    cut = lax.optimization_barrier((*cut, share_of(projector, 2)))
    tokens = {0: columns[0]}
    grads = {0: grad_out}
    for s in (1, 3, 2):
        both = send(cut[s - 1], x=s)
        tokens[s], grads[s] = both[:, :2048], both[:, 2048:]

    basis_part = send(cut[3], zh=1)
    weight_part = send(after(share_of(weight, 4), basis_part), zh=1)
    basis_pair = pair(basis_part)
    odd = y % 2 == 1
    basis_part = jnp.concatenate(
        [jnp.where(odd, basis_pair, basis_part), jnp.where(odd, basis_part, basis_pair)], 0
    )
    basis = assemble(projector, basis_part, send(basis_part, c=1))
    basis = dot(basis, slot_permutation(False), (1, 0)).astype(NARROW)
    own_basis = dot(projector, slot_permutation(True), (1, 0)).astype(NARROW)

    turn = (0, 1, 3, 2)
    projected = {s: dot(tokens[s], basis, (1, 0)).astype(NARROW) for s in turn}
    projected[2], weight_part = lax.optimization_barrier((projected[2], weight_part))
    far = sum(dot(projected[s][:, 256:], grads[s], (0, 0)) for s in turn)
    near = sum(dot(projected[s][:, :256], grads[s], (0, 0)) for s in turn)

    kept = near + send(far.astype(NARROW), c=1).astype(WIDE)
    weight_part = spread(weight_part, "y")
    kept, weight_part = lax.optimization_barrier((kept.astype(NARROW), weight_part))

    weight_other = send(weight_part, c=1)
    all_grads = after(join([grads[s] for s in range(4)]), kept)
    parts = [dot(all_grads, w, (1, 1)).astype(NARROW) for w in (weight, weight_part, weight_other)]
    home = [jnp.concatenate([part[128 * s : 128 * s + 128] for part in parts], 1) for s in range(4)]

    kept = fold(kept, "y").astype(NARROW)
    kept = after(kept, *home).reshape(4, 1, 16, 1024)
    kept = jnp.broadcast_to(kept, (4, 2, 16, 1024)).reshape(8, 16, 1024)
    kept = lax.all_to_all(kept, ("zl", "zh"), 0, 0, tiled=True).astype(WIDE).sum(0)

    home[1] = send(home[1], x=-1)
    home[3] = send(home[3], x=-3)
    kept = after(kept, home[1], home[3])
    away = {s: send(kept, x=s) for s in (1, 3, 2)}
    projected_grad = (kept + away[2]) + (away[1] + away[3])
    home[2] = send(after(home[2], projected_grad), x=-2)

    new_first, new_second, direction = adam_step(projected_grad, first_moment, second_moment)

    rows = spread(direction, "zl")
    rows = spread(rows, "y")
    rows = after(join([rows, send(rows, c=1)]), *home)
    input_grad = place(home)
    weight_update = dot(own_basis, rows, (1, 0))
    return (input_grad, weight_update, new_first, new_second)


def solution(mesh):
    fine = Mesh(mesh.devices.reshape([SIZES[name] for name in NAMES]), NAMES)
    return jax.shard_map(
        body,
        mesh=fine,
        in_specs=(
            P(DP + SHARD, None),
            P(DP + SHARD, None),
            P(SHARD, None),
            P(SHARD, None),
            P(DP, None),
            P(DP, None),
        ),
        out_specs=(P(DP + SHARD, None), P(SHARD, None), P(DP, None), P(DP, None)),
        check_vma=False,
    )
```

time: 203 us -> 156 us (0.77); the launches traced: 199 us -> 155 us
  waiting for transfers between devices: 97.6 us -> 54.5 us
  local copies, waits for them, and re-layouts: 27.9 us -> 10.1 us
  other arithmetic: 0.98 us -> 10.3 us
  matrix products: 16 us -> 22.1 us
  Pallas kernels: 0 us -> 2.86 us
    ppermute x31 -> x27, waiting for transfers between devices: 97.6 us -> 44 us  [send(): return lax.ppermute(value, axes, pairs)]
    unnamed x29 -> x44, local copies, waits for them, and re-layouts: 10.4 us -> 0.2 us
    dot_general x4 -> x17, matrix products: 16 us -> 22.1 us  [dot(): lax.dot_general(a, b, ((contract[:1], contract[1:]), ((), ())), preferred...]
    all_to_all x0 -> x1, waiting for transfers between devices: none -> 6.11 us  [body(): lax.all_to_all(kept, ('zl', 'zh'), 0, 0, tiled=True).astype(WIDE).sum(0)]
    ppermute x31 -> x27, starting transfers between devices: 55.6 us -> 50.3 us  [send(): return lax.ppermute(value, axes, pairs)]
    concatenate x1 -> x6, other arithmetic: 0.01 us -> 5.17 us  [the longest x4 2.57 us: body(): jnp.concatenate([part[128 * s:128 * s + 128] for part in parts], 1)]
    ppermute x0 -> x1, waiting for transfers between devices: none -> 4.35 us  [pair(): return lax.ppermute(value, 'y', [(0, 1), (1, 0), (2, 3), (3, 2)])]
    all_to_all x0 -> x1, starting transfers between devices: none -> 3.41 us  [body(): lax.all_to_all(kept, ('zl', 'zh'), 0, 0, tiled=True).astype(WIDE).sum(0)]
  transfers between devices with their start and end apart: 31 -> 29, of which waited for: 18 -> 18; matrix products, arithmetic and copies ran while one was open for 17% -> 16% of each run, Pallas kernels for 0% -> 2%
where the time goes in v2:
time: 156 us; the launch traced here: 155 us
  waiting for transfers between devices  54.5 us (35%)
  starting transfers between devices  54.1 us (35%)
  matrix products  22.1 us (14%)
  other arithmetic  10.3 us (7%)
  local copies, waits for them, and re-layouts  10.1 us (6%)
  Pallas kernels  2.86 us (2%)
    ppermute x27, starting transfers between devices, send(): return lax.ppermute(value, axes, pairs)  50.3 us
    ppermute x27, waiting for transfers between devices, send(): return lax.ppermute(value, axes, pairs)  44 us
    dot_general x17, matrix products, dot(): lax.dot_general(a, b, ((contract[:1], contract[1:]), ((), ())), preferred...  22.1 us
    all_to_all x1, waiting for transfers between devices, body(): lax.all_to_all(kept, ('zl', 'zh'), 0, 0, tiled=True).astype(WIDE).sum(0)  6.11 us
    ppermute x1, waiting for transfers between devices, pair(): return lax.ppermute(value, 'y', [(0, 1), (1, 0), (2, 3), (3, 2)])  4.35 us
    all_to_all x1, starting transfers between devices, body(): lax.all_to_all(kept, ('zl', 'zh'), 0, 0, tiled=True).astype(WIDE).sum(0)  3.41 us
    max x5, other arithmetic, join(): return functools.reduce(jnp.maximum, padded)  3.35 us
  transfers between devices with their start and end apart: 29, of which 18 were waited for; matrix products, arithmetic and copies ran while one was open for 16% of the time, Pallas kernels for 2%

profile of v2, /device:TPU:8, one launch (start us, length us, event | category | flops | bytes accessed | tf_op | source)
XLA Modules:
  0.0 155.3 jit_solution(17594929887650472898)
XLA Ops:
  0.7 1.1 constant_dynamic-slice_fusion.1
  1.8 1.5 constant_dynamic-slice_fusion.2
  3.3 1.6 %pad_maximum_fusion = (bf16[128,3072]{1,0:T(8,128)(2,1)}, bf16[128,3072]{1,0:T(8,128)(2,1)}, bf16[128,3072]{1,0:T(8,128)(2,1)}) fusion(bf16[128,1024]{1,0:T(8,128)(2,1)S(1)} %copy-done.1, bf16[128,2048]{1,0:T(8,128)(2,1)S(1)} %get-tuple-element.36, bf16[128,2048]{1,0:T(8,128)(2,1)S(1)} %get-tuple-element.37, bf16[128,2048]{1,0:T(8,128)(2,1)S(1)} %get-tuple-element.38), kind=kLoop, calls=%fused_computation.40 | loop fusion | flops 3932160 | bytes 4194304 | tf_op jit(solution)/shard_map/concatenate | solution.py:131
  4.9 7.2 %collective-permute-start.3 = (bf16[256,512]{1,0:T(8,128)(2,1)S(1)}, bf16[256,512]{1,0:T(8,128)(2,1)S(1)}, u32[]{:S(2)}, u32[]{:S(2)}) collective-permute-start(bf16[256,512]{1,0:T(8,128)(2,1)S(1)} %constant_dynamic-slice_fusion.1), channel_id=1, source_target_pairs={{0,1},{1,0},{2,3},{3,2},{4,5},{5,4},{6,7},{7,6},{8,9},{9,8},{10,11... | collective-permute-start | bytes 786440 | tf_op jit(solution)/shard_map/ppermute | solution.py:34
  12.1 3.0 %collective-permute-start.1 = (bf16[128,3072]{1,0:T(8,128)(2,1)}, bf16[128,3072]{1,0:T(8,128)(2,1)}, u32[]{:S(2)}, u32[]{:S(2)}) collective-permute-start(bf16[128,3072]{1,0:T(8,128)(2,1)} %get-tuple-element.19), channel_id=1, source_target_pairs={{0,4},{2,6},{4,0},{6,2},{1,5},{3,7},{5,1},{7,3},{8,12},{10,14},{12... | collective-permute-start | bytes 2359304 | tf_op jit(solution)/shard_map/ppermute | solution.py:34
  15.7 2.6 %collective-permute-start.2 = (bf16[128,3072]{1,0:T(8,128)(2,1)}, bf16[128,3072]{1,0:T(8,128)(2,1)}, u32[]{:S(2)}, u32[]{:S(2)}) collective-permute-start(bf16[128,3072]{1,0:T(8,128)(2,1)} %get-tuple-element.20), channel_id=1, source_target_pairs={{0,6},{2,0},{4,2},{6,4},{1,7},{3,1},{5,3},{7,5},{8,14},{10,8},{12,... | collective-permute-start | bytes 2359304 | tf_op jit(solution)/shard_map/ppermute | solution.py:34
  18.3 1.2 collective-permute-done.3
  20.0 1.5 broadcast_in_dim.10
  22.6 4.4 %collective-permute-done.4 = bf16[256,512]{1,0:T(8,128)(2,1)} collective-permute-done((bf16[256,512]{1,0:T(8,128)(2,1)S(1)}, bf16[256,512]{1,0:T(8,128)(2,1)}, u32[]{:S(2)}, u32[]{:S(2)}) %collective-permute-start.4) | collective-permute-done | bytes 262176 | tf_op jit(solution)/shard_map/ppermute | solution.py:124
  28.0 1.0 pad_maximum_fusion.6
  29.2 8.6 %collective-permute-start.6 = (bf16[128,1024]{1,0:T(8,128)(2,1)S(1)}, bf16[128,1024]{1,0:T(8,128)(2,1)S(1)}, u32[]{:S(2)}, u32[]{:S(2)}) collective-permute-start(bf16[128,1024]{1,0:T(8,128)(2,1)S(1)} %constant_dynamic-slice_fusion), channel_id=1, source_target_pairs={{0,1},{1,0},{2,3},{3,2},{4,5},{5,4},{6,7},{7,6},{8,9},{9,8},{10,11... | collective-permute-start | bytes 786440 | tf_op jit(solution)/shard_map/ppermute | solution.py:34
  37.8 11.9 %collective-permute-done = bf16[128,3072]{1,0:T(8,128)(2,1)S(1)} collective-permute-done((bf16[128,3072]{1,0:T(8,128)(2,1)}, bf16[128,3072]{1,0:T(8,128)(2,1)S(1)}, u32[]{:S(2)}, u32[]{:S(2)}) %collective-permute-start) | collective-permute-done | bytes 786464 | tf_op jit(solution)/shard_map/ppermute | solution.py:34
  51.7 1.9 %constant_dynamic-update-slice_fusion = bf16[2048,512]{1,0:T(8,128)(2,1)} fusion(bf16[2048,512]{1,0:T(8,128)(2,1)} %get-tuple-element.55, bf16[512,512]{1,0:T(8,128)(2,1)} %collective-permute-done.5, s32[]{:T(128)S(6)} %select_n.139), kind=kLoop, calls=%fused_computation.138 | loop fusion | bytes 1048580 | tf_op jit(solution)/shard_map/dynamic_update_slice | solution.py:95
  53.7 2.9 %convolution_convert_fusion = bf16[2048,512]{1,0:T(8,128)(2,1)S(1)} fusion(bf16[2048,512]{1,0:T(8,128)(2,1)} %constant_dynamic-update-slice_fusion, s32[512]{0:T(512)S(1)} %get-tuple-element.66, s32[512]{0:T(512)S(1)} %get-tuple-element.69, s32[512]{0:T(512)S(1)} %get-tuple-element.67, s32[512]{0:T(512)S(1)} %get-tuple-element.70, s32[]{:T(128)S(6)} %axis_index.36, ...), kind=kOutput, calls=%fused_computation | convolution fusion | flops 1089732608 | bytes 4212744 | tf_op jit(solution)/shard_map/dot_general | solution.py:45
  56.6 1.5 convolution_convert_fusion.5
  58.1 1.6 %collective-permute-start.10 = (bf16[128,1024]{1,0:T(8,128)(2,1)S(1)}, bf16[128,1024]{1,0:T(8,128)(2,1)S(1)}, u32[]{:S(2)}, u32[]{:S(2)}) collective-permute-start(bf16[128,1024]{1,0:T(8,128)(2,1)S(1)} %collective-permute-done.6), channel_id=1, source_target_pairs={{0,16},{16,32},{32,48},{48,0},{1,17},{17,33},{33,49},{49,1},{2,18}... | collective-permute-start | bytes 786440 | tf_op jit(solution)/shard_map/ppermute | solution.py:34
  60.2 2.3 %collective-permute-start.9 = (bf16[128,1024]{1,0:T(8,128)(2,1)S(1)}, bf16[128,1024]{1,0:T(8,128)(2,1)S(1)}, u32[]{:S(2)}, u32[]{:S(2)}) collective-permute-start(bf16[128,1024]{1,0:T(8,128)(2,1)S(1)} %collective-permute-done.6), channel_id=1, source_target_pairs={{0,32},{16,48},{32,0},{48,16},{1,33},{17,49},{33,1},{49,17},{2,34}... | collective-permute-start | bytes 786440 | tf_op jit(solution)/shard_map/ppermute | solution.py:34
  62.5 1.5 convolution_convert_fusion.8
  65.1 1.5 convolution_convert_fusion.6
  66.6 1.3 fusion.86
  68.2 1.3 fusion.5
  70.1 1.3 fusion.88
  71.3 2.7 %collective-permute-done.9 = bf16[128,1024]{1,0:T(8,128)(2,1)S(1)} collective-permute-done((bf16[128,1024]{1,0:T(8,128)(2,1)S(1)}, bf16[128,1024]{1,0:T(8,128)(2,1)S(1)}, u32[]{:S(2)}, u32[]{:S(2)}) %collective-permute-start.9) | collective-permute-done | bytes 262176 | tf_op jit(solution)/shard_map/ppermute | solution.py:34
  74.1 1.3 fusion.4
  75.6 1.3 convolution_convert_fusion.1
  77.0 2.9 %collective-permute-start.14 = (bf16[64,1024]{1,0:T(8,128)(2,1)S(1)}, bf16[64,1024]{1,0:T(8,128)(2,1)S(1)}, u32[]{:S(2)}, u32[]{:S(2)}) collective-permute-start(bf16[64,1024]{1,0:T(8,128)(2,1)S(1)} %get-tuple-element.53), channel_id=1, source_target_pairs={{0,32},{16,48},{32,0},{48,16},{1,33},{17,49},{33,1},{49,17},{2,34}... | collective-permute-start | bytes 393224 | tf_op jit(solution)/shard_map/ppermute | solution.py:34
  79.9 1.3 collective-permute-start.15
  82.1 1.2 collective-permute-done.13
  83.3 1.6 %collective-permute-done.14 = bf16[64,1024]{1,0:T(8,128)(2,1)S(1)} collective-permute-done((bf16[64,1024]{1,0:T(8,128)(2,1)S(1)}, bf16[64,1024]{1,0:T(8,128)(2,1)S(1)}, u32[]{:S(2)}, u32[]{:S(2)}) %collective-permute-start.14) | collective-permute-done | bytes 131104 | tf_op jit(solution)/shard_map/ppermute | solution.py:34
  84.9 2.4 %collective-permute-done.15 = bf16[64,1024]{1,0:T(8,128)(2,1)S(1)} collective-permute-done((bf16[64,1024]{1,0:T(8,128)(2,1)S(1)}, bf16[64,1024]{1,0:T(8,128)(2,1)S(1)}, u32[]{:S(2)}, u32[]{:S(2)}) %collective-permute-start.15) | collective-permute-done | bytes 131104 | tf_op jit(solution)/shard_map/ppermute | solution.py:34
  91.5 3.4 %all-to-all-start = ((bf16[8,16,1024]{2,1,0:T(8,128)(2,1)}), bf16[8,16,1024]{2,1,0:T(8,128)(2,1)S(1)}, u32[]{:S(2)}, u32[]{:S(2)}) async-start(bf16[8,16,1024]{2,1,0:T(8,128)(2,1)} %bitcast.1), calls=%async_computation | async-start | bytes 524288 | tf_op jit(solution)/shard_map/all_to_all | solution.py:168
  95.6 2.6 %collective-permute-start.12 = (bf16[128,2048]{1,0:T(8,128)(2,1)}, bf16[128,2048]{1,0:T(8,128)(2,1)}, u32[]{:S(2)}, u32[]{:S(2)}) collective-permute-start(bf16[128,2048]{1,0:T(8,128)(2,1)} %pad_maximum_fusion.8), channel_id=1, source_target_pairs={{0,6},{2,0},{4,2},{6,4},{1,7},{3,1},{5,3},{7,5},{8,14},{10,8},{12,... | collective-permute-start | bytes 1572872 | tf_op jit(solution)/shard_map/ppermute | solution.py:34
  98.3 6.1 %all-to-all-done = bf16[8,16,1024]{2,1,0:T(8,128)(2,1)S(1)} async-done(((bf16[8,16,1024]{2,1,0:T(8,128)(2,1)}), bf16[8,16,1024]{2,1,0:T(8,128)(2,1)S(1)}, u32[]{:S(2)}, u32[]{:S(2)}) %all-to-all-start) | async-done | bytes 262176 | tf_op jit(solution)/shard_map/all_to_all | solution.py:168
  104.4 5.9 %collective-permute-done.16.refs_3_ = bf16[128,2048]{1,0:T(8,128)(2,1)S(1)} collective-permute-done((bf16[128,2048]{1,0:T(8,128)(2,1)}, bf16[128,2048]{1,0:T(8,128)(2,1)S(1)}, u32[]{:S(2)}, u32[]{:S(2)}) %collective-permute-start.16) | collective-permute-done | bytes 524320 | tf_op jit(solution)/shard_map/ppermute | solution.py:34
  110.3 1.9 %collective-permute-start.17 = (f32[16,1024]{1,0:T(8,128)S(1)}, f32[16,1024]{1,0:T(8,128)S(1)}, u32[]{:S(2)}, u32[]{:S(2)}) collective-permute-start(f32[16,1024]{1,0:T(8,128)S(1)} %convert_reduce_fusion), channel_id=1, source_target_pairs={{0,4},{2,6},{4,0},{6,2},{1,5},{3,7},{5,1},{7,3},{8,12},{10,14},{12... | collective-permute-start | bytes 196616 | tf_op jit(solution)/shard_map/ppermute | solution.py:34
  112.2 2.0 %collective-permute-start.18 = (f32[16,1024]{1,0:T(8,128)S(1)}, f32[16,1024]{1,0:T(8,128)S(1)}, u32[]{:S(2)}, u32[]{:S(2)}) collective-permute-start(f32[16,1024]{1,0:T(8,128)S(1)} %convert_reduce_fusion), channel_id=1, source_target_pairs={{0,2},{2,4},{4,6},{6,0},{1,3},{3,5},{5,7},{7,1},{8,10},{10,12},{12... | collective-permute-start | bytes 196616 | tf_op jit(solution)/shard_map/ppermute | solution.py:34
  114.2 1.2 collective-permute-start.19
  116.1 1.6 %collective-permute-done.18 = f32[16,1024]{1,0:T(8,128)S(1)} collective-permute-done((f32[16,1024]{1,0:T(8,128)S(1)}, f32[16,1024]{1,0:T(8,128)S(1)}, u32[]{:S(2)}, u32[]{:S(2)}) %collective-permute-start.18) | collective-permute-done | bytes 65568 | tf_op jit(solution)/shard_map/ppermute | solution.py:34
  119.2 3.4 %collective-permute-start.21 = (bf16[16,1024]{1,0:T(8,128)(2,1)S(1)}, bf16[16,1024]{1,0:T(8,128)(2,1)S(1)}, u32[]{:S(2)}, u32[]{:S(2)}) collective-permute-start(bf16[16,1024]{1,0:T(8,128)(2,1)S(1)} %get-tuple-element.32), channel_id=1, source_target_pairs={{0,192},{64,0},{128,64},{192,128},{1,193},{65,1},{129,65},{193,129... | collective-permute-start | bytes 98312 | tf_op jit(solution)/shard_map/ppermute | solution.py:34
  122.6 1.1 collective-permute-start.23
  124.2 3.2 %collective-permute-done.22 = bf16[16,1024]{1,0:T(8,128)(2,1)S(1)} collective-permute-done((bf16[16,1024]{1,0:T(8,128)(2,1)S(1)}, bf16[16,1024]{1,0:T(8,128)(2,1)S(1)}, u32[]{:S(2)}, u32[]{:S(2)}) %collective-permute-start.22) | collective-permute-done | bytes 32800 | tf_op jit(solution)/shard_map/ppermute | solution.py:34
  129.1 2.2 %collective-permute-start.25 = (bf16[64,1024]{1,0:T(8,128)(2,1)S(1)}, bf16[64,1024]{1,0:T(8,128)(2,1)S(1)}, u32[]{:S(2)}, u32[]{:S(2)}) collective-permute-start(bf16[64,1024]{1,0:T(8,128)(2,1)S(1)} %pad_maximum_fusion.12), channel_id=1, source_target_pairs={{0,32},{16,48},{32,0},{48,16},{1,33},{17,49},{33,1},{49,17},{2,34}... | collective-permute-start | bytes 393224 | tf_op jit(solution)/shard_map/ppermute | solution.py:34
  131.3 2.5 %collective-permute-start.26 = (bf16[64,1024]{1,0:T(8,128)(2,1)S(1)}, bf16[64,1024]{1,0:T(8,128)(2,1)S(1)}, u32[]{:S(2)}, u32[]{:S(2)}) collective-permute-start(bf16[64,1024]{1,0:T(8,128)(2,1)S(1)} %pad_maximum_fusion.12), channel_id=1, source_target_pairs={{0,16},{16,32},{32,48},{48,0},{1,17},{17,33},{33,49},{49,1},{2,18}... | collective-permute-start | bytes 393224 | tf_op jit(solution)/shard_map/ppermute | solution.py:34
  135.6 1.5 collective-permute-done.26
  137.9 7.0 %collective-permute-done.20.refs_2_ = bf16[128,2048]{1,0:T(8,128)(2,1)} collective-permute-done((bf16[128,2048]{1,0:T(8,128)(2,1)}, bf16[128,2048]{1,0:T(8,128)(2,1)}, u32[]{:S(2)}, u32[]{:S(2)}) %collective-permute-start.20) | collective-permute-done | bytes 524320 | tf_op jit(solution)/shard_map/ppermute | solution.py:34
  144.8 2.9 %shard_map.93 = bf16[128,8192]{1,0:T(8,128)(2,1)} custom-call(bf16[128,2048]{1,0:T(8,128)(2,1)S(1)} %pad_maximum_fusion.7.refs_0_, bf16[128,2048]{1,0:T(8,128)(2,1)} %collective-permute-done.12.refs_1_, bf16[128,2048]{1,0:T(8,128)(2,1)} %collective-permute-done.20.refs_2_, bf16[128,2048]{1,0:T(8,128)(2,1)S(1)} %collective-permute-done.16.refs_3_), custom_call_target="tpu_custom_call" | custom-call | bytes 4194304 | tf_op jit(solution)/shard_map/pallas_call | solution.py:113
  147.8 2.4 %pad_maximum_fusion.3 = bf16[512,1024]{1,0:T(8,128)(2,1)} fusion(bf16[256,1024]{1,0:T(8,128)(2,1)} %collective-permute-done.27, bf16[256,1024]{1,0:T(8,128)(2,1)} %pad_maximum_fusion.11), kind=kLoop, calls=%fused_computation.56 | loop fusion | flops 2097152 | bytes 2097152 | tf_op jit(solution)/shard_map/max | solution.py:80
  150.2 5.1 %fusion.3 = f32[1024,1024]{1,0:T(8,128)} fusion(bf16[512,1024]{1,0:T(8,128)(2,1)} %pad_maximum_fusion.3, bf16[1024,512]{1,0:T(8,128)(2,1)S(1)} %copy-done.3, s32[]{:T(128)S(6)} %axis_index.44, s32[512]{0:T(512)S(1)} %get-tuple-element.66, s32[512]{0:T(512)S(1)} %copy-done.7, s32[512]{0:T(512)S(1)} %get-tuple-element.67, s32[512]{0:T(512)S(1)} %copy-done.9, ...), kind=kOutput, calls=%fused_computation.31 | convolution fusion | flops 1629487104 | bytes 6309900 | tf_op jit(solution)/shard_map/dot_general | solution.py:45
  (107 shorter events, 20.6 us)
Async XLA Ops:
  0.6 28.5 %copy-start = (bf16[1024,1024]{1,0:T(8,128)(2,1)S(1)}, bf16[1024,1024]{1,0:T(8,128)(2,1)}, u32[]{:S(2)}) copy-start(bf16[1024,1024]{1,0:T(8,128)(2,1)} %param.8) | copy-start | bytes 6291460
  0.6 2.7 %copy-start.1 = (bf16[128,1024]{1,0:T(8,128)(2,1)S(1)}, bf16[128,1024]{1,0:T(8,128)(2,1)}, u32[]{:S(2)}) copy-start(bf16[128,1024]{1,0:T(8,128)(2,1)} %param.7) | copy-start | bytes 786436
  4.9 14.6 %collective-permute-start.3 = (bf16[256,512]{1,0:T(8,128)(2,1)S(1)}, bf16[256,512]{1,0:T(8,128)(2,1)S(1)}, u32[]{:S(2)}, u32[]{:S(2)}) collective-permute-start(bf16[256,512]{1,0:T(8,128)(2,1)S(1)} %constant_dynamic-slice_fusion.1), channel_id=1, source_target_pairs={{0,1},{1,0},{2,3},{3,2},{4,5},{5,4},{6,7},{7,6},{8,9},{9,8},{10,11... | collective-permute-start | bytes 786440 | tf_op jit(solution)/shard_map/ppermute | solution.py:34
  12.1 37.6 %collective-permute-start.1 = (bf16[128,3072]{1,0:T(8,128)(2,1)}, bf16[128,3072]{1,0:T(8,128)(2,1)}, u32[]{:S(2)}, u32[]{:S(2)}) collective-permute-start(bf16[128,3072]{1,0:T(8,128)(2,1)} %get-tuple-element.19), channel_id=1, source_target_pairs={{0,4},{2,6},{4,0},{6,2},{1,5},{3,7},{5,1},{7,3},{8,12},{10,14},{12... | collective-permute-start | bytes 2359304 | tf_op jit(solution)/shard_map/ppermute | solution.py:34
  15.1 34.5 %collective-permute-start = (bf16[128,3072]{1,0:T(8,128)(2,1)}, bf16[128,3072]{1,0:T(8,128)(2,1)S(1)}, u32[]{:S(2)}, u32[]{:S(2)}) collective-permute-start(bf16[128,3072]{1,0:T(8,128)(2,1)} %get-tuple-element.18), channel_id=1, source_target_pairs={{0,2},{2,4},{4,6},{6,0},{1,3},{3,5},{5,7},{7,1},{8,10},{10,12},{12... | collective-permute-start | bytes 2359304 | tf_op jit(solution)/shard_map/ppermute | solution.py:34
  15.7 35.0 %collective-permute-start.2 = (bf16[128,3072]{1,0:T(8,128)(2,1)}, bf16[128,3072]{1,0:T(8,128)(2,1)}, u32[]{:S(2)}, u32[]{:S(2)}) collective-permute-start(bf16[128,3072]{1,0:T(8,128)(2,1)} %get-tuple-element.20), channel_id=1, source_target_pairs={{0,6},{2,0},{4,2},{6,4},{1,7},{3,1},{5,3},{7,5},{8,14},{10,8},{12,... | collective-permute-start | bytes 2359304 | tf_op jit(solution)/shard_map/ppermute | solution.py:34
  19.5 7.5 %collective-permute-start.4 = (bf16[256,512]{1,0:T(8,128)(2,1)S(1)}, bf16[256,512]{1,0:T(8,128)(2,1)}, u32[]{:S(2)}, u32[]{:S(2)}) collective-permute-start(bf16[256,512]{1,0:T(8,128)(2,1)S(1)} %collective-permute-done.3), channel_id=1, source_target_pairs={{0,16},{16,0},{32,48},{48,32},{1,17},{17,1},{33,49},{49,33},{2,18}... | collective-permute-start | bytes 786440 | tf_op jit(solution)/shard_map/ppermute | solution.py:124
  20.0 33.6 %copy-start.14 = (pred[512]{0:T(512)(128)(4,1)}, pred[512]{0:T(512)(128)(4,1)S(1)}, u32[]{:S(2)}) copy-start(pred[512]{0:T(512)(128)(4,1)S(1)} %get-tuple-element.61) | copy-start | bytes 1540
  20.0 33.6 %copy-start.16 = (pred[512]{0:T(512)(128)(4,1)}, pred[512]{0:T(512)(128)(4,1)S(1)}, u32[]{:S(2)}) copy-start(pred[512]{0:T(512)(128)(4,1)S(1)} %get-tuple-element.62) | copy-start | bytes 1540
  29.0 22.7 %collective-permute-start.5 = (bf16[512,512]{1,0:T(8,128)(2,1)}, bf16[512,512]{1,0:T(8,128)(2,1)}, u32[]{:S(2)}, u32[]{:S(2)}) collective-permute-start(bf16[512,512]{1,0:T(8,128)(2,1)} %get-tuple-element.54), channel_id=1, source_target_pairs={{0,8},{8,0},{1,9},{9,1},{2,10},{10,2},{3,11},{11,3},{4,12},{12,4},... | collective-permute-start | bytes 1572872 | tf_op jit(solution)/shard_map/ppermute | solution.py:34
  29.0 24.6 %copy-start.18 = (pred[512]{0:T(512)(128)(4,1)}, pred[512]{0:T(512)(128)(4,1)S(1)}, u32[]{:S(2)}) copy-start(pred[512]{0:T(512)(128)(4,1)S(1)} %get-tuple-element.63) | copy-start | bytes 1540
  29.0 24.6 %copy-start.20 = (pred[512]{0:T(512)(128)(4,1)}, pred[512]{0:T(512)(128)(4,1)S(1)}, u32[]{:S(2)}) copy-start(pred[512]{0:T(512)(128)(4,1)S(1)} %get-tuple-element.64) | copy-start | bytes 1540
  29.1 24.5 %copy-start.6 = (s32[512]{0:T(512)}, s32[512]{0:T(512)S(1)}, u32[]{:S(2)}) copy-start(s32[512]{0:T(512)S(1)} %get-tuple-element.69) | copy-start | bytes 6148
  29.1 24.5 %copy-start.8 = (s32[512]{0:T(512)}, s32[512]{0:T(512)S(1)}, u32[]{:S(2)}) copy-start(s32[512]{0:T(512)S(1)} %get-tuple-element.70) | copy-start | bytes 6148
  29.1 24.5 %copy-start.10 = (s32[512]{0:T(512)}, s32[512]{0:T(512)S(1)}, u32[]{:S(2)}) copy-start(s32[512]{0:T(512)S(1)} %get-tuple-element.71) | copy-start | bytes 6148
  29.1 24.5 %copy-start.12 = (s32[512]{0:T(512)}, s32[512]{0:T(512)S(1)}, u32[]{:S(2)}) copy-start(s32[512]{0:T(512)S(1)} %get-tuple-element.72) | copy-start | bytes 6148
  29.2 28.9 %collective-permute-start.6 = (bf16[128,1024]{1,0:T(8,128)(2,1)S(1)}, bf16[128,1024]{1,0:T(8,128)(2,1)S(1)}, u32[]{:S(2)}, u32[]{:S(2)}) collective-permute-start(bf16[128,1024]{1,0:T(8,128)(2,1)S(1)} %constant_dynamic-slice_fusion), channel_id=1, source_target_pairs={{0,1},{1,0},{2,3},{3,2},{4,5},{5,4},{6,7},{7,6},{8,9},{9,8},{10,11... | collective-permute-start | bytes 786440 | tf_op jit(solution)/shard_map/ppermute | solution.py:34
  58.1 13.2 %collective-permute-start.10 = (bf16[128,1024]{1,0:T(8,128)(2,1)S(1)}, bf16[128,1024]{1,0:T(8,128)(2,1)S(1)}, u32[]{:S(2)}, u32[]{:S(2)}) collective-permute-start(bf16[128,1024]{1,0:T(8,128)(2,1)S(1)} %collective-permute-done.6), channel_id=1, source_target_pairs={{0,16},{16,32},{32,48},{48,0},{1,17},{17,33},{33,49},{49,1},{2,18}... | collective-permute-start | bytes 786440 | tf_op jit(solution)/shard_map/ppermute | solution.py:34
  59.8 11.6 %collective-permute-start.8 = (bf16[128,1024]{1,0:T(8,128)(2,1)S(1)}, bf16[128,1024]{1,0:T(8,128)(2,1)S(1)}, u32[]{:S(2)}, u32[]{:S(2)}) collective-permute-start(bf16[128,1024]{1,0:T(8,128)(2,1)S(1)} %collective-permute-done.6), channel_id=1, source_target_pairs={{0,48},{16,0},{32,16},{48,32},{1,49},{17,1},{33,17},{49,33},{2,50}... | collective-permute-start | bytes 786440 | tf_op jit(solution)/shard_map/ppermute | solution.py:34
  60.2 13.8 %collective-permute-start.9 = (bf16[128,1024]{1,0:T(8,128)(2,1)S(1)}, bf16[128,1024]{1,0:T(8,128)(2,1)S(1)}, u32[]{:S(2)}, u32[]{:S(2)}) collective-permute-start(bf16[128,1024]{1,0:T(8,128)(2,1)S(1)} %collective-permute-done.6), channel_id=1, source_target_pairs={{0,32},{16,48},{32,0},{48,16},{1,33},{17,49},{33,1},{49,17},{2,34}... | collective-permute-start | bytes 786440 | tf_op jit(solution)/shard_map/ppermute | solution.py:34
  69.4 4.7 %collective-permute-start.7 = (bf16[256,1024]{1,0:T(8,128)(2,1)S(1)}, bf16[256,1024]{1,0:T(8,128)(2,1)S(1)}, u32[]{:S(2)}, u32[]{:S(2)}) collective-permute-start(bf16[256,1024]{1,0:T(8,128)(2,1)S(1)} %fusion.5), channel_id=1, source_target_pairs={{0,8},{8,0},{1,9},{9,1},{2,10},{10,2},{3,11},{11,3},{4,12},{12,4},... | collective-permute-start | bytes 1572872 | tf_op jit(solution)/shard_map/ppermute | solution.py:34
  75.5 11.9 %collective-permute-start.11 = (bf16[512,1024]{1,0:T(8,128)(2,1)S(1)}, bf16[512,1024]{1,0:T(8,128)(2,1)S(1)}, u32[]{:S(2)}, u32[]{:S(2)}) collective-permute-start(bf16[512,1024]{1,0:T(8,128)(2,1)S(1)} %pad_maximum_fusion.4), channel_id=1, source_target_pairs={{0,8},{8,0},{1,9},{9,1},{2,10},{10,2},{3,11},{11,3},{4,12},{12,4},... | collective-permute-start | bytes 3145736 | tf_op jit(solution)/shard_map/ppermute | solution.py:34
  76.9 6.4 %collective-permute-start.13 = (bf16[64,1024]{1,0:T(8,128)(2,1)S(1)}, bf16[64,1024]{1,0:T(8,128)(2,1)S(1)}, u32[]{:S(2)}, u32[]{:S(2)}) collective-permute-start(bf16[64,1024]{1,0:T(8,128)(2,1)S(1)} %get-tuple-element.51), channel_id=1, source_target_pairs={{0,16},{16,32},{32,48},{48,0},{1,17},{17,33},{33,49},{49,1},{2,18}... | collective-permute-start | bytes 393224 | tf_op jit(solution)/shard_map/ppermute | solution.py:34
  77.0 7.9 %collective-permute-start.14 = (bf16[64,1024]{1,0:T(8,128)(2,1)S(1)}, bf16[64,1024]{1,0:T(8,128)(2,1)S(1)}, u32[]{:S(2)}, u32[]{:S(2)}) collective-permute-start(bf16[64,1024]{1,0:T(8,128)(2,1)S(1)} %get-tuple-element.53), channel_id=1, source_target_pairs={{0,32},{16,48},{32,0},{48,16},{1,33},{17,49},{33,1},{49,17},{2,34}... | collective-permute-start | bytes 393224 | tf_op jit(solution)/shard_map/ppermute | solution.py:34
  79.9 7.4 %collective-permute-start.15 = (bf16[64,1024]{1,0:T(8,128)(2,1)S(1)}, bf16[64,1024]{1,0:T(8,128)(2,1)S(1)}, u32[]{:S(2)}, u32[]{:S(2)}) collective-permute-start(bf16[64,1024]{1,0:T(8,128)(2,1)S(1)} %get-tuple-element.52), channel_id=1, source_target_pairs={{0,48},{16,0},{32,16},{48,32},{1,49},{17,1},{33,17},{49,33},{2,50}... | collective-permute-start | bytes 393224 | tf_op jit(solution)/shard_map/ppermute | solution.py:34
  89.0 29.4 %copy-start.4 = (f32[16,1024]{1,0:T(8,128)S(1)}, f32[16,1024]{1,0:T(8,128)}, u32[]{:S(2)}) copy-start(f32[16,1024]{1,0:T(8,128)} %param.10) | copy-start | bytes 196612
  89.0 29.4 %copy-start.5 = (f32[16,1024]{1,0:T(8,128)S(1)}, f32[16,1024]{1,0:T(8,128)}, u32[]{:S(2)}) copy-start(f32[16,1024]{1,0:T(8,128)} %param.11) | copy-start | bytes 196612
  91.5 12.8 %all-to-all-start = ((bf16[8,16,1024]{2,1,0:T(8,128)(2,1)}), bf16[8,16,1024]{2,1,0:T(8,128)(2,1)S(1)}, u32[]{:S(2)}, u32[]{:S(2)}) async-start(bf16[8,16,1024]{2,1,0:T(8,128)(2,1)} %bitcast.1), calls=%async_computation | async-start | bytes 524288 | tf_op jit(solution)/shard_map/all_to_all | solution.py:168
  94.9 15.3 %collective-permute-start.16 = (bf16[128,2048]{1,0:T(8,128)(2,1)}, bf16[128,2048]{1,0:T(8,128)(2,1)S(1)}, u32[]{:S(2)}, u32[]{:S(2)}) collective-permute-start(bf16[128,2048]{1,0:T(8,128)(2,1)} %pad_maximum_fusion.10), channel_id=1, source_target_pairs={{0,2},{2,4},{4,6},{6,0},{1,3},{3,5},{5,7},{7,1},{8,10},{10,12},{12... | collective-permute-start | bytes 1572872 | tf_op jit(solution)/shard_map/ppermute | solution.py:34
  95.6 14.7 %collective-permute-start.12 = (bf16[128,2048]{1,0:T(8,128)(2,1)}, bf16[128,2048]{1,0:T(8,128)(2,1)}, u32[]{:S(2)}, u32[]{:S(2)}) collective-permute-start(bf16[128,2048]{1,0:T(8,128)(2,1)} %pad_maximum_fusion.8), channel_id=1, source_target_pairs={{0,6},{2,0},{4,2},{6,4},{1,7},{3,1},{5,3},{7,5},{8,14},{10,8},{12,... | collective-permute-start | bytes 1572872 | tf_op jit(solution)/shard_map/ppermute | solution.py:34
  110.3 5.8 %collective-permute-start.17 = (f32[16,1024]{1,0:T(8,128)S(1)}, f32[16,1024]{1,0:T(8,128)S(1)}, u32[]{:S(2)}, u32[]{:S(2)}) collective-permute-start(f32[16,1024]{1,0:T(8,128)S(1)} %convert_reduce_fusion), channel_id=1, source_target_pairs={{0,4},{2,6},{4,0},{6,2},{1,5},{3,7},{5,1},{7,3},{8,12},{10,14},{12... | collective-permute-start | bytes 196616 | tf_op jit(solution)/shard_map/ppermute | solution.py:34
  112.2 5.5 %collective-permute-start.18 = (f32[16,1024]{1,0:T(8,128)S(1)}, f32[16,1024]{1,0:T(8,128)S(1)}, u32[]{:S(2)}, u32[]{:S(2)}) collective-permute-start(f32[16,1024]{1,0:T(8,128)S(1)} %convert_reduce_fusion), channel_id=1, source_target_pairs={{0,2},{2,4},{4,6},{6,0},{1,3},{3,5},{5,7},{7,1},{8,10},{10,12},{12... | collective-permute-start | bytes 196616 | tf_op jit(solution)/shard_map/ppermute | solution.py:34
  114.2 4.3 %collective-permute-start.19 = (f32[16,1024]{1,0:T(8,128)S(1)}, f32[16,1024]{1,0:T(8,128)S(1)}, u32[]{:S(2)}, u32[]{:S(2)}) collective-permute-start(f32[16,1024]{1,0:T(8,128)S(1)} %convert_reduce_fusion), channel_id=1, source_target_pairs={{0,6},{2,0},{4,2},{6,4},{1,7},{3,1},{5,3},{7,5},{8,14},{10,8},{12,... | collective-permute-start | bytes 196616 | tf_op jit(solution)/shard_map/ppermute | solution.py:34
  119.2 5.0 %collective-permute-start.21 = (bf16[16,1024]{1,0:T(8,128)(2,1)S(1)}, bf16[16,1024]{1,0:T(8,128)(2,1)S(1)}, u32[]{:S(2)}, u32[]{:S(2)}) collective-permute-start(bf16[16,1024]{1,0:T(8,128)(2,1)S(1)} %get-tuple-element.32), channel_id=1, source_target_pairs={{0,192},{64,0},{128,64},{192,128},{1,193},{65,1},{129,65},{193,129... | collective-permute-start | bytes 98312 | tf_op jit(solution)/shard_map/ppermute | solution.py:34
  122.6 4.8 %collective-permute-start.22 = (bf16[16,1024]{1,0:T(8,128)(2,1)S(1)}, bf16[16,1024]{1,0:T(8,128)(2,1)S(1)}, u32[]{:S(2)}, u32[]{:S(2)}) collective-permute-start(bf16[16,1024]{1,0:T(8,128)(2,1)S(1)} %get-tuple-element.32), channel_id=1, source_target_pairs={{0,128},{64,192},{128,0},{192,64},{1,129},{65,193},{129,1},{193,65... | collective-permute-start | bytes 98312 | tf_op jit(solution)/shard_map/ppermute | solution.py:34
  122.6 5.7 %collective-permute-start.23 = (bf16[16,1024]{1,0:T(8,128)(2,1)S(1)}, bf16[16,1024]{1,0:T(8,128)(2,1)S(1)}, u32[]{:S(2)}, u32[]{:S(2)}) collective-permute-start(bf16[16,1024]{1,0:T(8,128)(2,1)S(1)} %get-tuple-element.32), channel_id=1, source_target_pairs={{0,64},{64,128},{128,192},{192,0},{1,65},{65,129},{129,193},{193,1... | collective-permute-start | bytes 98312 | tf_op jit(solution)/shard_map/ppermute | solution.py:34
  128.3 6.2 %collective-permute-start.24 = (bf16[64,1024]{1,0:T(8,128)(2,1)S(1)}, bf16[64,1024]{1,0:T(8,128)(2,1)S(1)}, u32[]{:S(2)}, u32[]{:S(2)}) collective-permute-start(bf16[64,1024]{1,0:T(8,128)(2,1)S(1)} %pad_maximum_fusion.12), channel_id=1, source_target_pairs={{0,48},{16,0},{32,16},{48,32},{1,49},{17,1},{33,17},{49,33},{2,50}... | collective-permute-start | bytes 393224 | tf_op jit(solution)/shard_map/ppermute | solution.py:34
  129.1 6.5 %collective-permute-start.25 = (bf16[64,1024]{1,0:T(8,128)(2,1)S(1)}, bf16[64,1024]{1,0:T(8,128)(2,1)S(1)}, u32[]{:S(2)}, u32[]{:S(2)}) collective-permute-start(bf16[64,1024]{1,0:T(8,128)(2,1)S(1)} %pad_maximum_fusion.12), channel_id=1, source_target_pairs={{0,32},{16,48},{32,0},{48,16},{1,33},{17,49},{33,1},{49,17},{2,34}... | collective-permute-start | bytes 393224 | tf_op jit(solution)/shard_map/ppermute | solution.py:34
  131.3 5.7 %collective-permute-start.26 = (bf16[64,1024]{1,0:T(8,128)(2,1)S(1)}, bf16[64,1024]{1,0:T(8,128)(2,1)S(1)}, u32[]{:S(2)}, u32[]{:S(2)}) collective-permute-start(bf16[64,1024]{1,0:T(8,128)(2,1)S(1)} %pad_maximum_fusion.12), channel_id=1, source_target_pairs={{0,16},{16,32},{32,48},{48,0},{1,17},{17,33},{33,49},{49,1},{2,18}... | collective-permute-start | bytes 393224 | tf_op jit(solution)/shard_map/ppermute | solution.py:34
  133.8 11.0 %collective-permute-start.20 = (bf16[128,2048]{1,0:T(8,128)(2,1)}, bf16[128,2048]{1,0:T(8,128)(2,1)}, u32[]{:S(2)}, u32[]{:S(2)}) collective-permute-start(bf16[128,2048]{1,0:T(8,128)(2,1)} %pad_maximum_fusion.9), channel_id=1, source_target_pairs={{0,4},{2,6},{4,0},{6,2},{1,5},{3,7},{5,1},{7,3},{8,12},{10,14},{12... | collective-permute-start | bytes 1572872 | tf_op jit(solution)/shard_map/ppermute | solution.py:34
  137.9 9.9 %collective-permute-start.27 = (bf16[256,1024]{1,0:T(8,128)(2,1)}, bf16[256,1024]{1,0:T(8,128)(2,1)}, u32[]{:S(2)}, u32[]{:S(2)}) collective-permute-start(bf16[256,1024]{1,0:T(8,128)(2,1)} %pad_maximum_fusion.11), channel_id=1, source_target_pairs={{0,8},{8,0},{1,9},{9,1},{2,10},{10,2},{3,11},{11,3},{4,12},{12,4},... | collective-permute-start | bytes 1572872 | tf_op jit(solution)/shard_map/ppermute | solution.py:34
  147.7 2.4 %copy-start.9 = (s32[512]{0:T(512)S(1)}, s32[512]{0:T(512)}, u32[]{:S(2)}) copy-start(s32[512]{0:T(512)} %copy-done.8) | copy-start | bytes 6148
  147.7 2.5 %copy-start.11 = (s32[512]{0:T(512)S(1)}, s32[512]{0:T(512)}, u32[]{:S(2)}) copy-start(s32[512]{0:T(512)} %copy-done.10) | copy-start | bytes 6148
  147.7 2.5 %copy-start.13 = (s32[512]{0:T(512)S(1)}, s32[512]{0:T(512)}, u32[]{:S(2)}) copy-start(s32[512]{0:T(512)} %copy-done.12) | copy-start | bytes 6148
  147.7 2.5 %copy-start.15 = (pred[512]{0:T(512)(128)(4,1)S(1)}, pred[512]{0:T(512)(128)(4,1)}, u32[]{:S(2)}) copy-start(pred[512]{0:T(512)(128)(4,1)} %copy-done.14) | copy-start | bytes 1540
  147.7 2.5 %copy-start.17 = (pred[512]{0:T(512)(128)(4,1)S(1)}, pred[512]{0:T(512)(128)(4,1)}, u32[]{:S(2)}) copy-start(pred[512]{0:T(512)(128)(4,1)} %copy-done.16) | copy-start | bytes 1540
  147.7 2.5 %copy-start.19 = (pred[512]{0:T(512)(128)(4,1)S(1)}, pred[512]{0:T(512)(128)(4,1)}, u32[]{:S(2)}) copy-start(pred[512]{0:T(512)(128)(4,1)} %copy-done.18) | copy-start | bytes 1540
  147.8 2.5 %copy-start.21 = (pred[512]{0:T(512)(128)(4,1)S(1)}, pred[512]{0:T(512)(128)(4,1)}, u32[]{:S(2)}) copy-start(pred[512]{0:T(512)(128)(4,1)} %copy-done.20) | copy-start | bytes 1540
  (3 other events, 6.5 us)

commit v3 on v1

v3 whole, which is shorter than its diff:
```python
import functools
import itertools

import jax
import jax.numpy as jnp
from jax import lax
from jax.experimental import pallas as pl
from jax.experimental.pallas import tpu as pltpu
from jax.sharding import Mesh
from jax.sharding import PartitionSpec as P

beta_one = 0.9
beta_two = 0.999
bias_one = 0.999973438601112
bias_two = 0.0952078528862904
epsilon = 1e-08

NAMES = ("zl", "y", "c", "x", "zh")
SIZES = {"zl": 4, "y": 4, "c": 2, "x": 4, "zh": 2}
DP = ("zl", "y", "c")
SHARD = ("x", "zh")
WIDE = jnp.float32
NARROW = jnp.bfloat16


def send(value, **shift):
    axes = tuple(name for name in NAMES if name in shift)
    sizes = [SIZES[name] for name in axes]
    flat = {at: i for i, at in enumerate(itertools.product(*map(range, sizes)))}
    pairs = [
        (i, flat[tuple((p + shift[n]) % s for p, n, s in zip(at, axes, sizes))])
        for at, i in flat.items()
    ]
    return lax.ppermute(value, axes, pairs)


def adam_step(projected_grad, first_moment, second_moment):
    new_first = beta_one * first_moment + (1.0 - beta_one) * projected_grad
    new_second = beta_two * second_moment + (1.0 - beta_two) * projected_grad * projected_grad
    direction = new_first / bias_one / (jnp.sqrt(new_second / bias_two) + epsilon)
    return (new_first, new_second, direction.astype(NARROW))


def dot(a, b, contract):
    return lax.dot_general(a, b, ((contract[:1], contract[1:]), ((), ())), preferred_element_type=WIDE)


def owner_row(slot, turned):
    cc, dy, dz, low = slot >> 8, (slot >> 6) & 3, (slot >> 4) & 3, slot & 15
    zl = (lax.axis_index("zl") + dz) & 3 if turned else dz
    y = (lax.axis_index("y") + dy) & 3
    c = (lax.axis_index("c") + cc) & 1
    return ((zl * 4 + y) * 2 + c) * 16 + low


def fold(slots, axis, *others):
    rows = slots.shape[0] // 4
    came = [send(slots[rows * s : rows * s + rows], **{axis: s}) for s in (1, 2, 3)]
    came = lax.optimization_barrier((*came, *others))[:3]
    total = slots[:rows].astype(WIDE)
    for part in came:
        total = total + part.astype(WIDE)
    return total


def spread(own, axis):
    return join([own] + [send(own, **{axis: -s}) for s in (1, 2, 3)])


def after(value, *others):
    return lax.optimization_barrier((value,) + others)[0]


def join(parts):
    rows, low = parts[0].shape[0], jnp.array(-jnp.inf, parts[0].dtype)
    padded = [
        lax.pad(part, low, ((i * rows, (len(parts) - 1 - i) * rows, 0), (0, 0, 0)))
        for i, part in enumerate(parts)
    ]
    return functools.reduce(jnp.maximum, padded)


def share_of(mine, ways):
    rows = mine.shape[0] // 2 // ways
    at = (lax.axis_index("c") * ways + lax.axis_index("y") % ways) * rows
    return lax.dynamic_slice_in_dim(mine, at, rows, 0)


def call(kernel, outs, flops, moved, scratch=(), **more):
    return pl.pallas_call(
        kernel,
        out_shape=[jax.ShapeDtypeStruct(*out) for out in outs],
        scratch_shapes=[pltpu.VMEM(*space) for space in scratch],
        cost_estimate=pl.CostEstimate(flops=flops, bytes_accessed=moved, transcendentals=0),
        compiler_params=pltpu.CompilerParams(vmem_limit_bytes=24 << 20),
        **more,
    )


def basis_kernel(mine, part, far, out):
    c, zh = lax.axis_index("c"), lax.axis_index("zh")
    slot = lax.broadcasted_iota(jnp.int32, (512, 1), 0)
    row = lax.broadcasted_iota(jnp.int32, (512, 512), 1)
    order = (row == owner_row(slot, False)).astype(WIDE).astype(NARROW)
    other = (1 - zh) * 1024
    pieces = [(mine[low : low + 256, :], zh * 1024 + low) for low in range(0, 1024, 256)]
    for some, at in ((part, other + c * 512), (far, other + (1 - c) * 512)):
        pieces += [(some[:, :512], at), (some[:, 512:], at + 256)]
    for some, at in pieces:
        moved = dot(order, some, (1, 1)).astype(NARROW)
        out[:, pl.ds(pl.multiple_of(at, 256), 256)] = moved


def project_kernel(x0, g0, xg1, xg2, xg3, basis, far, near, grads, tokens, projected):
    tokens[0:128] = x0[...]
    grads[0:128] = g0[...]
    for s, both in ((1, xg1), (2, xg2), (3, xg3)):
        tokens[128 * s : 128 * s + 128] = both[:, :2048]
        grads[128 * s : 128 * s + 128] = both[:, 2048:]
    for low in range(0, 512, 256):
        some = tokens[low : low + 256, :]
        projected[:, low : low + 256] = dot(basis[...], some, (1, 1)).astype(NARROW)
    far[...] = dot(projected[256:, :], grads[...], (1, 0)).astype(NARROW)
    near[...] = dot(projected[:256, :], grads[...], (1, 0))


def home_kernel(grads, weight, part, other, out):
    x = lax.axis_index("x")
    at = 0
    for some in (weight, part, other):
        for low in range(0, some.shape[0], 256):
            block = dot(grads[...], some[low : low + 256, :], (1, 1)).astype(NARROW)
            for s in range(4):
                out[lax.rem(x + 4 - s, 4), :, at : at + 256] = block[128 * s : 128 * s + 128]
            at += 256


def update_kernel(basis, near, far, out):
    out[...] = dot(basis[:, :256], near[...], (1, 0)) + dot(basis[:, 256:], far[...], (1, 0))


def place_kernel(blocks, out):
    c, y, zh = (lax.axis_index(name) for name in ("c", "y", "zh"))
    other = (1 - zh) * 1024
    spots = [(0, 1024, zh * 1024)]
    for cc, dy in itertools.product(range(2), range(4)):
        to = other + lax.rem(c + cc, 2) * 512 + lax.rem(y + dy, 4) * 128
        spots.append((1024 + (cc * 4 + dy) * 128, 128, to))
    for s in range(4):
        for at, size, to in spots:
            out[:, pl.ds(pl.multiple_of(2048 * s + to, 128), size)] = blocks[s, :, at : at + size]


def body(inputs, grad_out, weight, projector, first_moment, second_moment):
    x = lax.axis_index("x")

    columns = [lax.dynamic_slice_in_dim(inputs, (x + s) % 4 * 2048, 2048, 1) for s in range(4)]
    cut = [jnp.concatenate([columns[s], grad_out], 1) for s in (1, 2, 3)]
    basis_part = share_of(projector, 1)
    basis_part = jnp.concatenate([basis_part[:256], basis_part[256:]], 1)
    rows = jnp.concatenate([basis_part, share_of(weight, 4)], 0)
    cut = lax.optimization_barrier((*cut, rows))
    met = {s: send(cut[s - 1], x=s) for s in (1, 3, 2)}

    rows = send(cut[3], zh=1)
    basis_part, weight_part = rows[:256], rows[256:]
    (basis,) = call(basis_kernel, [((512, 2048), NARROW)], 1 << 20, 1 << 20)(
        projector, basis_part, send(basis_part, c=1)
    )
    quarters = [weight_part] + [send(weight_part, y=-s) for s in (1, 2, 3)]

    far, near, grads = call(
        project_kernel,
        [((256, 1024), NARROW), ((256, 1024), WIDE), ((512, 1024), NARROW)],
        4 << 30,
        10 << 20,
        [((512, 2048), NARROW), ((512, 512), NARROW)],
    )(columns[0], grad_out, met[1], met[2], met[3], basis)

    kept = near + send(far, c=1).astype(WIDE)
    kept = kept.astype(NARROW)

    kept = fold(kept, "y").astype(NARROW)
    kept = jnp.broadcast_to(kept.reshape(4, 1, 16, 1024), (4, 2, 16, 1024)).reshape(8, 16, 1024)
    kept = lax.all_to_all(kept, ("zl", "zh"), 0, 0, tiled=True)
    kept, *quarters = lax.optimization_barrier((kept, *quarters))
    kept = kept.astype(WIDE).sum(0)

    weight_part = join(quarters)
    weight_other = send(weight_part, c=1)
    (home,) = call(home_kernel, [((4, 128, 2048), NARROW)], 2 << 30, 8 << 20)(
        grads, weight, weight_part, weight_other
    )

    away = [send(kept, x=s) for s in (1, 3, 2)]
    *away, home = lax.optimization_barrier((*away, home))
    projected_grad = (kept + away[2]) + (away[0] + away[1])
    home, projected_grad = lax.optimization_barrier((home, projected_grad))
    home = lax.all_to_all(home, "x", 0, 0, tiled=True)

    new_first, new_second, direction = adam_step(projected_grad, first_moment, second_moment)

    slot = lax.broadcasted_iota(jnp.int32, (512, 512), 1)
    row = lax.broadcasted_iota(jnp.int32, (512, 512), 0)
    order = (row == owner_row(slot, True)).astype(NARROW)
    own_basis = dot(projector, order, (1, 0)).astype(NARROW)
    near = after(spread(spread(direction, "zl"), "y"), own_basis, home)
    far = send(near, c=1)
    (input_grad,) = call(place_kernel, [((128, 8192), NARROW)], 1 << 20, 4 << 20)(home)
    (weight_update,) = call(
        update_kernel,
        [((1024, 1024), WIDE)],
        1 << 30,
        6 << 20,
        grid=(4,),
        in_specs=[
            pl.BlockSpec((256, 512), lambda i: (i, 0)),
            pl.BlockSpec((256, 1024), lambda i: (0, 0)),
            pl.BlockSpec((256, 1024), lambda i: (0, 0)),
        ],
        out_specs=[pl.BlockSpec((256, 1024), lambda i: (i, 0))],
    )(own_basis, near, far)
    return (input_grad, weight_update, new_first, new_second)


def solution(mesh):
    fine = Mesh(mesh.devices.reshape([SIZES[name] for name in NAMES]), NAMES)
    return jax.shard_map(
        body,
        mesh=fine,
        in_specs=(
            P(DP + SHARD, None),
            P(DP + SHARD, None),
            P(SHARD, None),
            P(SHARD, None),
            P(DP, None),
            P(DP, None),
        ),
        out_specs=(P(DP + SHARD, None), P(SHARD, None), P(DP, None), P(DP, None)),
        check_vma=False,
    )
```

time: 203 us -> 135 us (0.67)
  waiting for transfers between devices: 97.6 us -> 62.9 us
  local copies, waits for them, and re-layouts: 27.9 us -> 7.68 us
  matrix products: 16 us -> 1.73 us
  Pallas kernels: 0 us -> 10.5 us
  starting transfers between devices: 55.6 us -> 46.4 us
    ppermute x31 -> x23, waiting for transfers between devices: 97.6 us -> 55.2 us  [send(): return lax.ppermute(value, axes, pairs)]
    ppermute x31 -> x23, starting transfers between devices: 55.6 us -> 36.5 us  [send(): return lax.ppermute(value, axes, pairs)]
    dot_general x4 -> x1, matrix products: 16 us -> 1.73 us  [dot(): lax.dot_general(a, b, ((contract[:1], contract[1:]), ((), ())), preferred...]
    pallas_call x0 -> x5, Pallas kernels: none -> 10.5 us  [the longest x1 3.26 us: body(): call(update_kernel, [((1024, 1024), WIDE)], 1 << 30, 6 << 20, grid=(4,),...]
    all_to_all x0 -> x2, starting transfers between devices: none -> 9.97 us  [the longest x1 6.22 us: body(): kept = lax.all_to_all(kept, ('zl', 'zh'), 0, 0, tiled=True)]
    all_to_all x0 -> x2, waiting for transfers between devices: none -> 7.62 us  [the longest x1 7.62 us: body(): home = lax.all_to_all(home, 'x', 0, 0, tiled=True)]
    unnamed x29 -> x28, local copies, waits for them, and re-layouts: 10.4 us -> 3.59 us
    dynamic_update_slice x9 -> x0, local copies, waits for them, and re-layouts: 5.97 us -> none  [the longest x3 3.23 us: body(): lax.dynamic_update_slice_in_dim(input_grad, part, (x + s) % 4 * 2048, 1)]
  transfers between devices with their start and end apart: 31 -> 25, of which waited for: 18 -> 17; matrix products, arithmetic and copies ran while one was open for 17% -> 3% of each run, Pallas kernels for 0% -> 4%
where the time goes in v3:
time: 135 us; the launch traced here: 133 us
  waiting for transfers between devices  62.9 us (47%)
  starting transfers between devices  46.4 us (34%)
  Pallas kernels  10.5 us (8%)
  local copies, waits for them, and re-layouts  7.68 us (6%)
  other arithmetic  2.63 us (2%)
  matrix products  1.73 us (1%)
    ppermute x23, waiting for transfers between devices, send(): return lax.ppermute(value, axes, pairs)  55.2 us
    ppermute x23, starting transfers between devices, send(): return lax.ppermute(value, axes, pairs)  36.5 us
    all_to_all x1, waiting for transfers between devices, body(): home = lax.all_to_all(home, 'x', 0, 0, tiled=True)  7.62 us
    all_to_all x1, starting transfers between devices, body(): kept = lax.all_to_all(kept, ('zl', 'zh'), 0, 0, tiled=True)  6.22 us
    all_to_all x1, starting transfers between devices, body(): home = lax.all_to_all(home, 'x', 0, 0, tiled=True)  3.75 us
    unnamed x28, local copies, waits for them, and re-layouts  3.59 us
    pallas_call x1, Pallas kernels, body(): call(update_kernel, [((1024, 1024), WIDE)], 1 << 30, 6 << 20, grid=(4,),...  3.26 us
  transfers between devices with their start and end apart: 25, of which 17 were waited for; matrix products, arithmetic and copies ran while one was open for 3% of the time, Pallas kernels for 4%

profile of v3, /device:TPU:8, one launch (start us, length us, event | category | flops | bytes accessed | tf_op | source)
XLA Modules:
  0.0 132.8 jit_solution(228745046496895316)
XLA Ops:
  0.7 1.1 constant_dynamic-slice_fusion.1
  1.8 1.1 constant_dynamic-slice_fusion
  3.2 0.8 copy-done.3
  4.1 7.3 %collective-permute-start.3 = (bf16[384,1024]{1,0:T(8,128)(2,1)S(1)}, bf16[384,1024]{1,0:T(8,128)(2,1)S(1)}, u32[]{:S(2)}, u32[]{:S(2)}) collective-permute-start(bf16[384,1024]{1,0:T(8,128)(2,1)S(1)} %pad_maximum_fusion.4), channel_id=1, source_target_pairs={{0,1},{1,0},{2,3},{3,2},{4,5},{5,4},{6,7},{7,6},{8,9},{9,8},{10,11... | collective-permute-start | bytes 2359304 | tf_op jit(solution)/shard_map/ppermute | solution.py:34
  11.4 1.5 %collective-permute-start = (bf16[128,3072]{1,0:T(8,128)(2,1)S(1)}, bf16[128,3072]{1,0:T(8,128)(2,1)S(1)}, u32[]{:S(2)}, u32[]{:S(2)}) collective-permute-start(bf16[128,3072]{1,0:T(8,128)(2,1)S(1)} %get-tuple-element.26), channel_id=1, source_target_pairs={{0,2},{2,4},{4,6},{6,0},{1,3},{3,5},{5,7},{7,1},{8,10},{10,12},{12... | collective-permute-start | bytes 2359304 | tf_op jit(solution)/shard_map/ppermute | solution.py:34
  12.9 2.7 %collective-permute-start.1 = (bf16[128,3072]{1,0:T(8,128)(2,1)S(1)}, bf16[128,3072]{1,0:T(8,128)(2,1)S(1)}, u32[]{:S(2)}, u32[]{:S(2)}) collective-permute-start(bf16[128,3072]{1,0:T(8,128)(2,1)S(1)} %get-tuple-element.27), channel_id=1, source_target_pairs={{0,4},{2,6},{4,0},{6,2},{1,5},{3,7},{5,1},{7,3},{8,12},{10,14},{12... | collective-permute-start | bytes 2359304 | tf_op jit(solution)/shard_map/ppermute | solution.py:34
  15.6 1.4 %collective-permute-start.2 = (bf16[128,3072]{1,0:T(8,128)(2,1)S(1)}, bf16[128,3072]{1,0:T(8,128)(2,1)S(1)}, u32[]{:S(2)}, u32[]{:S(2)}) collective-permute-start(bf16[128,3072]{1,0:T(8,128)(2,1)S(1)} %get-tuple-element.28), channel_id=1, source_target_pairs={{0,6},{2,0},{4,2},{6,4},{1,7},{3,1},{5,3},{7,5},{8,14},{10,8},{12,... | collective-permute-start | bytes 2359304 | tf_op jit(solution)/shard_map/ppermute | solution.py:34
  17.1 27.4 %collective-permute-done.3 = bf16[384,1024]{1,0:T(8,128)(2,1)S(1)} collective-permute-done((bf16[384,1024]{1,0:T(8,128)(2,1)S(1)}, bf16[384,1024]{1,0:T(8,128)(2,1)S(1)}, u32[]{:S(2)}, u32[]{:S(2)}) %collective-permute-start.3) | collective-permute-done | bytes 786464 | tf_op jit(solution)/shard_map/ppermute | solution.py:34
  44.6 0.7 copy-done.9
  45.4 1.2 collective-permute-done.4.far
  46.5 1.3 %shard_map.93.basis = bf16[512,2048]{1,0:T(8,128)(2,1)S(1)} custom-call(bf16[1024,512]{1,0:T(8,128)(2,1)S(1)} %copy-done, bf16[256,1024]{1,0:T(8,128)(2,1)S(1)} %slice.32.part, bf16[256,1024]{1,0:T(8,128)(2,1)S(1)} %collective-permute-done.4.far), custom_call_target="tpu_custom_call" | custom-call | flops 1048576 | bytes 1048576 | tf_op jit(solution)/shard_map/pallas_call | solution.py:167
  47.9 1.6 %collective-permute-done.1.xg2 = bf16[128,3072]{1,0:T(8,128)(2,1)S(1)} collective-permute-done((bf16[128,3072]{1,0:T(8,128)(2,1)S(1)}, bf16[128,3072]{1,0:T(8,128)(2,1)S(1)}, u32[]{:S(2)}, u32[]{:S(2)}) %collective-permute-start.1) | collective-permute-done | bytes 786464 | tf_op jit(solution)/shard_map/ppermute | solution.py:34
  49.5 1.9 %shard_map.94 = (bf16[256,1024]{1,0:T(8,128)(2,1)S(1)}, f32[256,1024]{1,0:T(8,128)S(1)}, bf16[512,1024]{1,0:T(8,128)(2,1)S(1)}) custom-call(bf16[128,2048]{1,0:T(8,128)(2,1)S(1)} %get-tuple-element.53.x0, bf16[128,1024]{1,0:T(8,128)(2,1)S(1)} %copy-done.3, bf16[128,3072]{1,0:T(8,128)(2,1)S(1)} %collective-permute-done.xg1, ...), custom_call_target="tpu_custom_call" | custom-call | flops 4294967296 | bytes 10485760 | tf_op jit(solution)/shard_map/pallas_call | solution.py:172
  51.5 1.9 %collective-permute-done.5 = bf16[256,1024]{1,0:T(8,128)(2,1)S(1)} collective-permute-done((bf16[256,1024]{1,0:T(8,128)(2,1)S(1)}, bf16[256,1024]{1,0:T(8,128)(2,1)S(1)}, u32[]{:S(2)}, u32[]{:S(2)}) %collective-permute-start.5) | collective-permute-done | bytes 524320 | tf_op jit(solution)/shard_map/ppermute | solution.py:34
  53.6 1.7 %collective-permute-start.6 = (bf16[64,1024]{1,0:T(8,128)(2,1)S(1)}, bf16[64,1024]{1,0:T(8,128)(2,1)S(1)}, u32[]{:S(2)}, u32[]{:S(2)}) collective-permute-start(bf16[64,1024]{1,0:T(8,128)(2,1)S(1)} %get-tuple-element.59), channel_id=1, source_target_pairs={{0,16},{16,32},{32,48},{48,0},{1,17},{17,33},{33,49},{49,1},{2,18}... | collective-permute-start | bytes 393224 | tf_op jit(solution)/shard_map/ppermute | solution.py:34
  55.2 0.9 collective-permute-start.7
  56.2 2.4 %collective-permute-start.8 = (bf16[64,1024]{1,0:T(8,128)(2,1)S(1)}, bf16[64,1024]{1,0:T(8,128)(2,1)S(1)}, u32[]{:S(2)}, u32[]{:S(2)}) collective-permute-start(bf16[64,1024]{1,0:T(8,128)(2,1)S(1)} %get-tuple-element.57), channel_id=1, source_target_pairs={{0,48},{16,0},{32,16},{48,32},{1,49},{17,1},{33,17},{49,33},{2,50}... | collective-permute-start | bytes 393224 | tf_op jit(solution)/shard_map/ppermute | solution.py:34
  58.6 0.7 collective-permute-done.6
  59.3 3.8 %collective-permute-done.7 = bf16[64,1024]{1,0:T(8,128)(2,1)S(1)} collective-permute-done((bf16[64,1024]{1,0:T(8,128)(2,1)S(1)}, bf16[64,1024]{1,0:T(8,128)(2,1)S(1)}, u32[]{:S(2)}, u32[]{:S(2)}) %collective-permute-start.7) | collective-permute-done | bytes 131104 | tf_op jit(solution)/shard_map/ppermute | solution.py:34
  63.1 1.0 collective-permute-done.8
  64.2 0.7 broadcast_in_dim.8
  64.9 6.2 %all-to-all-start = ((bf16[8,16,1024]{2,1,0:T(8,128)(2,1)}), bf16[8,16,1024]{2,1,0:T(8,128)(2,1)S(1)}, u32[]{:S(2)}, u32[]{:S(2)}) async-start(bf16[8,16,1024]{2,1,0:T(8,128)(2,1)} %bitcast.5), calls=%async_computation | async-start | bytes 524288 | tf_op jit(solution)/shard_map/all_to_all | solution.py:185
  71.2 1.0 slice.37
  72.1 1.9 %collective-permute-start.10 = (bf16[128,1024]{1,0:T(8,128)(2,1)S(1)}, bf16[128,1024]{1,0:T(8,128)(2,1)S(1)}, u32[]{:S(2)}, u32[]{:S(2)}) collective-permute-start(bf16[128,1024]{1,0:T(8,128)(2,1)S(1)} %slice.37), channel_id=1, source_target_pairs={{0,32},{16,48},{32,0},{48,16},{1,33},{17,49},{33,1},{49,17},{2,34}... | collective-permute-start | bytes 786440 | tf_op jit(solution)/shard_map/ppermute | solution.py:34
  74.5 1.6 %collective-permute-start.9 = (bf16[128,1024]{1,0:T(8,128)(2,1)S(1)}, bf16[128,1024]{1,0:T(8,128)(2,1)}, u32[]{:S(2)}, u32[]{:S(2)}) collective-permute-start(bf16[128,1024]{1,0:T(8,128)(2,1)S(1)} %slice.37), channel_id=1, source_target_pairs={{0,48},{16,0},{32,16},{48,32},{1,49},{17,1},{33,17},{49,33},{2,50}... | collective-permute-start | bytes 786440 | tf_op jit(solution)/shard_map/ppermute | solution.py:34
  76.0 7.0 %collective-permute-done.10 = bf16[128,1024]{1,0:T(8,128)(2,1)S(1)} collective-permute-done((bf16[128,1024]{1,0:T(8,128)(2,1)S(1)}, bf16[128,1024]{1,0:T(8,128)(2,1)S(1)}, u32[]{:S(2)}, u32[]{:S(2)}) %collective-permute-start.10) | collective-permute-done | bytes 262176 | tf_op jit(solution)/shard_map/ppermute | solution.py:34
  83.0 3.2 %collective-permute-done.11 = bf16[128,1024]{1,0:T(8,128)(2,1)S(1)} collective-permute-done((bf16[128,1024]{1,0:T(8,128)(2,1)S(1)}, bf16[128,1024]{1,0:T(8,128)(2,1)S(1)}, u32[]{:S(2)}, u32[]{:S(2)}) %collective-permute-start.11) | collective-permute-done | bytes 262176 | tf_op jit(solution)/shard_map/ppermute | solution.py:34
  86.2 0.7 copy-done.11
  86.9 1.3 %pad_maximum_fusion.3.part = bf16[512,1024]{1,0:T(8,128)(2,1)S(1)} fusion(bf16[128,1024]{1,0:T(8,128)(2,1)} %copy-done.11, bf16[128,1024]{1,0:T(8,128)(2,1)} %copy-done.10, bf16[128,1024]{1,0:T(8,128)(2,1)} %collective-permute-done.9, bf16[128,1024]{1,0:T(8,128)(2,1)} %copy-done.8), kind=kLoop, calls=%fused_computation.6 | loop fusion | flops 4194304 | bytes 2097152 | tf_op jit(solution)/shard_map/max | solution.py:80
  88.6 1.6 %collective-permute-start.12 = (f32[16,1024]{1,0:T(8,128)S(1)}, f32[16,1024]{1,0:T(8,128)S(1)}, u32[]{:S(2)}, u32[]{:S(2)}) collective-permute-start(f32[16,1024]{1,0:T(8,128)S(1)} %convert_reduce_fusion), channel_id=1, source_target_pairs={{0,2},{2,4},{4,6},{6,0},{1,3},{3,5},{5,7},{7,1},{8,10},{10,12},{12... | collective-permute-start | bytes 196616 | tf_op jit(solution)/shard_map/ppermute | solution.py:34
  90.2 1.7 %collective-permute-start.13 = (f32[16,1024]{1,0:T(8,128)S(1)}, f32[16,1024]{1,0:T(8,128)S(1)}, u32[]{:S(2)}, u32[]{:S(2)}) collective-permute-start(f32[16,1024]{1,0:T(8,128)S(1)} %convert_reduce_fusion), channel_id=1, source_target_pairs={{0,6},{2,0},{4,2},{6,4},{1,7},{3,1},{5,3},{7,5},{8,14},{10,8},{12,... | collective-permute-start | bytes 196616 | tf_op jit(solution)/shard_map/ppermute | solution.py:34
  91.9 1.8 %collective-permute-start.14 = (f32[16,1024]{1,0:T(8,128)S(1)}, f32[16,1024]{1,0:T(8,128)S(1)}, u32[]{:S(2)}, u32[]{:S(2)}) collective-permute-start(f32[16,1024]{1,0:T(8,128)S(1)} %convert_reduce_fusion), channel_id=1, source_target_pairs={{0,4},{2,6},{4,0},{6,2},{1,5},{3,7},{5,1},{7,3},{8,12},{10,14},{12... | collective-permute-start | bytes 196616 | tf_op jit(solution)/shard_map/ppermute | solution.py:34
  93.7 2.4 %shard_map.95 = bf16[4,128,2048]{2,1,0:T(8,128)(2,1)S(1)} custom-call(bf16[512,1024]{1,0:T(8,128)(2,1)S(1)} %copy-done.6, bf16[1024,1024]{1,0:T(8,128)(2,1)S(1)} %copy-done.4, bf16[512,1024]{1,0:T(8,128)(2,1)S(1)} %pad_maximum_fusion.3.part, bf16[512,1024]{1,0:T(8,128)(2,1)S(1)} %collective-permute-done.15.other), custom_call_target="tpu_custom_call" | custom-call | flops 2147483648 | bytes 8388608 | tf_op jit(solution)/shard_map/pallas_call | solution.py:191
  96.1 1.3 copy-done.1
  97.7 3.8 %all-to-all-start.1 = ((bf16[4,128,2048]{2,1,0:T(8,128)(2,1)}), bf16[4,128,2048]{2,1,0:T(8,128)(2,1)S(1)}, u32[]{:S(2)}, u32[]{:S(2)}) async-start(bf16[4,128,2048]{2,1,0:T(8,128)(2,1)} %copy-done.1), calls=%async_computation.1 | async-start | bytes 4194304 | tf_op jit(solution)/shard_map/all_to_all | solution.py:199
  102.2 3.5 %collective-permute-start.16 = (bf16[16,1024]{1,0:T(8,128)(2,1)S(1)}, bf16[16,1024]{1,0:T(8,128)(2,1)S(1)}, u32[]{:S(2)}, u32[]{:S(2)}) collective-permute-start(bf16[16,1024]{1,0:T(8,128)(2,1)S(1)} %get-tuple-element.48), channel_id=1, source_target_pairs={{0,192},{64,0},{128,64},{192,128},{1,193},{65,1},{129,65},{193,129... | collective-permute-start | bytes 98312 | tf_op jit(solution)/shard_map/ppermute | solution.py:34
  105.7 1.1 collective-permute-start.18
  107.3 3.2 %collective-permute-done.17 = bf16[16,1024]{1,0:T(8,128)(2,1)S(1)} collective-permute-done((bf16[16,1024]{1,0:T(8,128)(2,1)S(1)}, bf16[16,1024]{1,0:T(8,128)(2,1)S(1)}, u32[]{:S(2)}, u32[]{:S(2)}) %collective-permute-start.17) | collective-permute-done | bytes 32800 | tf_op jit(solution)/shard_map/ppermute | solution.py:34
  110.5 0.9 collective-permute-done.18
  111.5 1.3 collective-permute-start.19
  112.7 1.1 collective-permute-start.20
  113.9 2.0 %collective-permute-start.21 = (bf16[64,1024]{1,0:T(8,128)(2,1)S(1)}, bf16[64,1024]{1,0:T(8,128)(2,1)S(1)}, u32[]{:S(2)}, u32[]{:S(2)}) collective-permute-start(bf16[64,1024]{1,0:T(8,128)(2,1)S(1)} %pad_maximum_fusion.6), channel_id=1, source_target_pairs={{0,16},{16,32},{32,48},{48,0},{1,17},{17,33},{33,49},{49,1},{2,18}... | collective-permute-start | bytes 393224 | tf_op jit(solution)/shard_map/ppermute | solution.py:34
  115.8 1.7 %fusion.basis = bf16[1024,512]{1,0:T(8,128)(2,1)} fusion(bf16[1024,512]{1,0:T(8,128)(2,1)S(1)} %copy-done, s32[512]{0:T(512)S(1)} %and_add_fusion), kind=kOutput, calls=%fused_computation.1 | convolution fusion | flops 537657344 | bytes 2099200 | tf_op jit(solution)/shard_map/dot_general | solution.py:45
  117.6 1.6 %collective-permute-done.20 = bf16[64,1024]{1,0:T(8,128)(2,1)S(1)} collective-permute-done((bf16[64,1024]{1,0:T(8,128)(2,1)S(1)}, bf16[64,1024]{1,0:T(8,128)(2,1)S(1)}, u32[]{:S(2)}, u32[]{:S(2)}) %collective-permute-start.20) | collective-permute-done | bytes 131104 | tf_op jit(solution)/shard_map/ppermute | solution.py:34
  119.2 0.8 collective-permute-done.21
  120.0 7.6 %all-to-all-done.1.blocks = bf16[4,128,2048]{2,1,0:T(8,128)(2,1)S(1)} async-done(((bf16[4,128,2048]{2,1,0:T(8,128)(2,1)}), bf16[4,128,2048]{2,1,0:T(8,128)(2,1)S(1)}, u32[]{:S(2)}, u32[]{:S(2)}) %all-to-all-start.1) | async-done | bytes 2097184 | tf_op jit(solution)/shard_map/all_to_all | solution.py:199
  127.6 1.6 %shard_map.96 = bf16[128,8192]{1,0:T(8,128)(2,1)} custom-call(bf16[4,128,2048]{2,1,0:T(8,128)(2,1)S(1)} %all-to-all-done.1.blocks), custom_call_target="tpu_custom_call" | custom-call | flops 1048576 | bytes 4194304 | tf_op jit(solution)/shard_map/pallas_call | solution.py:209
  129.6 3.3 %shard_map.97 = f32[1024,1024]{1,0:T(8,128)} custom-call(bf16[1024,512]{1,0:T(8,128)(2,1)S(1)} %copy-done.2, bf16[256,1024]{1,0:T(8,128)(2,1)S(1)} %pad_maximum_fusion.5.near, bf16[256,1024]{1,0:T(8,128)(2,1)S(1)} %collective-permute-done.22.far), custom_call_target="tpu_custom_call" | custom-call | flops 1073741824 | bytes 6291456 | tf_op jit(solution)/shard_map/pallas_call | solution.py:210
  (54 shorter events, 3.5 us)
Async XLA Ops:
  0.6 2.4 %copy-start.7 = (bf16[128,8192]{1,0:T(8,128)(2,1)S(1)}, bf16[128,8192]{1,0:T(8,128)(2,1)}, u32[]{:S(2)}) copy-start(bf16[128,8192]{1,0:T(8,128)(2,1)} %param.6) | copy-start | bytes 6291460
  3.0 1.0 copy-start.3
  4.0 42.6 %copy-start = (bf16[1024,512]{1,0:T(8,128)(2,1)S(1)}, bf16[1024,512]{1,0:T(8,128)(2,1)}, u32[]{:S(2)}) copy-start(bf16[1024,512]{1,0:T(8,128)(2,1)} %mine.1) | copy-start | bytes 3145732
  4.1 40.3 %collective-permute-start.3 = (bf16[384,1024]{1,0:T(8,128)(2,1)S(1)}, bf16[384,1024]{1,0:T(8,128)(2,1)S(1)}, u32[]{:S(2)}, u32[]{:S(2)}) collective-permute-start(bf16[384,1024]{1,0:T(8,128)(2,1)S(1)} %pad_maximum_fusion.4), channel_id=1, source_target_pairs={{0,1},{1,0},{2,3},{3,2},{4,5},{5,4},{6,7},{7,6},{8,9},{9,8},{10,11... | collective-permute-start | bytes 2359304 | tf_op jit(solution)/shard_map/ppermute | solution.py:34
  11.4 36.5 %collective-permute-start = (bf16[128,3072]{1,0:T(8,128)(2,1)S(1)}, bf16[128,3072]{1,0:T(8,128)(2,1)S(1)}, u32[]{:S(2)}, u32[]{:S(2)}) collective-permute-start(bf16[128,3072]{1,0:T(8,128)(2,1)S(1)} %get-tuple-element.26), channel_id=1, source_target_pairs={{0,2},{2,4},{4,6},{6,0},{1,3},{3,5},{5,7},{7,1},{8,10},{10,12},{12... | collective-permute-start | bytes 2359304 | tf_op jit(solution)/shard_map/ppermute | solution.py:34
  12.9 36.6 %collective-permute-start.1 = (bf16[128,3072]{1,0:T(8,128)(2,1)S(1)}, bf16[128,3072]{1,0:T(8,128)(2,1)S(1)}, u32[]{:S(2)}, u32[]{:S(2)}) collective-permute-start(bf16[128,3072]{1,0:T(8,128)(2,1)S(1)} %get-tuple-element.27), channel_id=1, source_target_pairs={{0,4},{2,6},{4,0},{6,2},{1,5},{3,7},{5,1},{7,3},{8,12},{10,14},{12... | collective-permute-start | bytes 2359304 | tf_op jit(solution)/shard_map/ppermute | solution.py:34
  15.6 33.8 %collective-permute-start.2 = (bf16[128,3072]{1,0:T(8,128)(2,1)S(1)}, bf16[128,3072]{1,0:T(8,128)(2,1)S(1)}, u32[]{:S(2)}, u32[]{:S(2)}) collective-permute-start(bf16[128,3072]{1,0:T(8,128)(2,1)S(1)} %get-tuple-element.28), channel_id=1, source_target_pairs={{0,6},{2,0},{4,2},{6,4},{1,7},{3,1},{5,3},{7,5},{8,14},{10,8},{12,... | collective-permute-start | bytes 2359304 | tf_op jit(solution)/shard_map/ppermute | solution.py:34
  44.5 0.9 copy-start.9
  44.5 2.0 %collective-permute-start.4 = (bf16[256,1024]{1,0:T(8,128)(2,1)S(1)}, bf16[256,1024]{1,0:T(8,128)(2,1)S(1)}, u32[]{:S(2)}, u32[]{:S(2)}) collective-permute-start(bf16[256,1024]{1,0:T(8,128)(2,1)S(1)} %slice.32.part), channel_id=1, source_target_pairs={{0,8},{8,0},{1,9},{9,1},{2,10},{10,2},{3,11},{11,3},{4,12},{12,4},... | collective-permute-start | bytes 1572872 | tf_op jit(solution)/shard_map/ppermute | solution.py:34
  51.4 12.7 %copy-start.5 = (bf16[512,1024]{1,0:T(8,128)(2,1)}, bf16[512,1024]{1,0:T(8,128)(2,1)S(1)}, u32[]{:S(2)}) copy-start(bf16[512,1024]{1,0:T(8,128)(2,1)S(1)} %get-tuple-element.36.grads) | copy-start | bytes 3145732
  51.4 2.0 %collective-permute-start.5 = (bf16[256,1024]{1,0:T(8,128)(2,1)S(1)}, bf16[256,1024]{1,0:T(8,128)(2,1)S(1)}, u32[]{:S(2)}, u32[]{:S(2)}) collective-permute-start(bf16[256,1024]{1,0:T(8,128)(2,1)S(1)} %get-tuple-element.31), channel_id=1, source_target_pairs={{0,8},{8,0},{1,9},{9,1},{2,10},{10,2},{3,11},{11,3},{4,12},{12,4},... | collective-permute-start | bytes 1572872 | tf_op jit(solution)/shard_map/ppermute | solution.py:34
  53.6 5.7 %collective-permute-start.6 = (bf16[64,1024]{1,0:T(8,128)(2,1)S(1)}, bf16[64,1024]{1,0:T(8,128)(2,1)S(1)}, u32[]{:S(2)}, u32[]{:S(2)}) collective-permute-start(bf16[64,1024]{1,0:T(8,128)(2,1)S(1)} %get-tuple-element.59), channel_id=1, source_target_pairs={{0,16},{16,32},{32,48},{48,0},{1,17},{17,33},{33,49},{49,1},{2,18}... | collective-permute-start | bytes 393224 | tf_op jit(solution)/shard_map/ppermute | solution.py:34
  55.2 7.9 %collective-permute-start.7 = (bf16[64,1024]{1,0:T(8,128)(2,1)S(1)}, bf16[64,1024]{1,0:T(8,128)(2,1)S(1)}, u32[]{:S(2)}, u32[]{:S(2)}) collective-permute-start(bf16[64,1024]{1,0:T(8,128)(2,1)S(1)} %get-tuple-element.58), channel_id=1, source_target_pairs={{0,32},{16,48},{32,0},{48,16},{1,33},{17,49},{33,1},{49,17},{2,34}... | collective-permute-start | bytes 393224 | tf_op jit(solution)/shard_map/ppermute | solution.py:34
  56.2 7.9 %collective-permute-start.8 = (bf16[64,1024]{1,0:T(8,128)(2,1)S(1)}, bf16[64,1024]{1,0:T(8,128)(2,1)S(1)}, u32[]{:S(2)}, u32[]{:S(2)}) collective-permute-start(bf16[64,1024]{1,0:T(8,128)(2,1)S(1)} %get-tuple-element.57), channel_id=1, source_target_pairs={{0,48},{16,0},{32,16},{48,32},{1,49},{17,1},{33,17},{49,33},{2,50}... | collective-permute-start | bytes 393224 | tf_op jit(solution)/shard_map/ppermute | solution.py:34
  64.2 29.5 %copy-start.4 = (bf16[1024,1024]{1,0:T(8,128)(2,1)S(1)}, bf16[1024,1024]{1,0:T(8,128)(2,1)}, u32[]{:S(2)}) copy-start(bf16[1024,1024]{1,0:T(8,128)(2,1)} %weight.1) | copy-start | bytes 6291460
  64.9 22.0 %all-to-all-start = ((bf16[8,16,1024]{2,1,0:T(8,128)(2,1)}), bf16[8,16,1024]{2,1,0:T(8,128)(2,1)S(1)}, u32[]{:S(2)}, u32[]{:S(2)}) async-start(bf16[8,16,1024]{2,1,0:T(8,128)(2,1)} %bitcast.5), calls=%async_computation | async-start | bytes 524288 | tf_op jit(solution)/shard_map/all_to_all | solution.py:185
  72.1 14.1 %copy-start.8 = (bf16[128,1024]{1,0:T(8,128)(2,1)}, bf16[128,1024]{1,0:T(8,128)(2,1)S(1)}, u32[]{:S(2)}) copy-start(bf16[128,1024]{1,0:T(8,128)(2,1)S(1)} %slice.37) | copy-start | bytes 786436
  72.1 10.9 %collective-permute-start.10 = (bf16[128,1024]{1,0:T(8,128)(2,1)S(1)}, bf16[128,1024]{1,0:T(8,128)(2,1)S(1)}, u32[]{:S(2)}, u32[]{:S(2)}) collective-permute-start(bf16[128,1024]{1,0:T(8,128)(2,1)S(1)} %slice.37), channel_id=1, source_target_pairs={{0,32},{16,48},{32,0},{48,16},{1,33},{17,49},{33,1},{49,17},{2,34}... | collective-permute-start | bytes 786440 | tf_op jit(solution)/shard_map/ppermute | solution.py:34
  74.0 12.2 %collective-permute-start.11 = (bf16[128,1024]{1,0:T(8,128)(2,1)S(1)}, bf16[128,1024]{1,0:T(8,128)(2,1)S(1)}, u32[]{:S(2)}, u32[]{:S(2)}) collective-permute-start(bf16[128,1024]{1,0:T(8,128)(2,1)S(1)} %slice.37), channel_id=1, source_target_pairs={{0,16},{16,32},{32,48},{48,0},{1,17},{17,33},{33,49},{49,1},{2,18}... | collective-permute-start | bytes 786440 | tf_op jit(solution)/shard_map/ppermute | solution.py:34
  74.5 12.4 %collective-permute-start.9 = (bf16[128,1024]{1,0:T(8,128)(2,1)S(1)}, bf16[128,1024]{1,0:T(8,128)(2,1)}, u32[]{:S(2)}, u32[]{:S(2)}) collective-permute-start(bf16[128,1024]{1,0:T(8,128)(2,1)S(1)} %slice.37), channel_id=1, source_target_pairs={{0,48},{16,0},{32,16},{48,32},{1,49},{17,1},{33,17},{49,33},{2,50}... | collective-permute-start | bytes 786440 | tf_op jit(solution)/shard_map/ppermute | solution.py:34
  83.0 3.2 %copy-start.10 = (bf16[128,1024]{1,0:T(8,128)(2,1)}, bf16[128,1024]{1,0:T(8,128)(2,1)S(1)}, u32[]{:S(2)}) copy-start(bf16[128,1024]{1,0:T(8,128)(2,1)S(1)} %collective-permute-done.10) | copy-start | bytes 786436
  86.2 0.7 copy-start.11
  86.9 6.8 %copy-start.6 = (bf16[512,1024]{1,0:T(8,128)(2,1)S(1)}, bf16[512,1024]{1,0:T(8,128)(2,1)}, u32[]{:S(2)}) copy-start(bf16[512,1024]{1,0:T(8,128)(2,1)} %copy-done.5) | copy-start | bytes 3145732
  88.3 5.5 %collective-permute-start.15 = (bf16[512,1024]{1,0:T(8,128)(2,1)S(1)}, bf16[512,1024]{1,0:T(8,128)(2,1)S(1)}, u32[]{:S(2)}, u32[]{:S(2)}) collective-permute-start(bf16[512,1024]{1,0:T(8,128)(2,1)S(1)} %pad_maximum_fusion.3.part), channel_id=1, source_target_pairs={{0,8},{8,0},{1,9},{9,1},{2,10},{10,2},{3,11},{11,3},{4,12},{12,4},... | collective-permute-start | bytes 3145736 | tf_op jit(solution)/shard_map/ppermute | solution.py:34
  88.6 8.8 %collective-permute-start.12 = (f32[16,1024]{1,0:T(8,128)S(1)}, f32[16,1024]{1,0:T(8,128)S(1)}, u32[]{:S(2)}, u32[]{:S(2)}) collective-permute-start(f32[16,1024]{1,0:T(8,128)S(1)} %convert_reduce_fusion), channel_id=1, source_target_pairs={{0,2},{2,4},{4,6},{6,0},{1,3},{3,5},{5,7},{7,1},{8,10},{10,12},{12... | collective-permute-start | bytes 196616 | tf_op jit(solution)/shard_map/ppermute | solution.py:34
  90.2 7.3 %collective-permute-start.13 = (f32[16,1024]{1,0:T(8,128)S(1)}, f32[16,1024]{1,0:T(8,128)S(1)}, u32[]{:S(2)}, u32[]{:S(2)}) collective-permute-start(f32[16,1024]{1,0:T(8,128)S(1)} %convert_reduce_fusion), channel_id=1, source_target_pairs={{0,6},{2,0},{4,2},{6,4},{1,7},{3,1},{5,3},{7,5},{8,14},{10,8},{12,... | collective-permute-start | bytes 196616 | tf_op jit(solution)/shard_map/ppermute | solution.py:34
  91.9 5.8 %collective-permute-start.14 = (f32[16,1024]{1,0:T(8,128)S(1)}, f32[16,1024]{1,0:T(8,128)S(1)}, u32[]{:S(2)}, u32[]{:S(2)}) collective-permute-start(f32[16,1024]{1,0:T(8,128)S(1)} %convert_reduce_fusion), channel_id=1, source_target_pairs={{0,4},{2,6},{4,0},{6,2},{1,5},{3,7},{5,1},{7,3},{8,12},{10,14},{12... | collective-permute-start | bytes 196616 | tf_op jit(solution)/shard_map/ppermute | solution.py:34
  96.1 1.3 copy-start.1
  97.7 3.8 %copy-start.12 = (f32[16,1024]{1,0:T(8,128)S(1)}, f32[16,1024]{1,0:T(8,128)}, u32[]{:S(2)}) copy-start(f32[16,1024]{1,0:T(8,128)} %param.10) | copy-start | bytes 196612
  97.7 3.8 %copy-start.13 = (f32[16,1024]{1,0:T(8,128)S(1)}, f32[16,1024]{1,0:T(8,128)}, u32[]{:S(2)}) copy-start(f32[16,1024]{1,0:T(8,128)} %param.11) | copy-start | bytes 196612
  97.7 29.9 %all-to-all-start.1 = ((bf16[4,128,2048]{2,1,0:T(8,128)(2,1)}), bf16[4,128,2048]{2,1,0:T(8,128)(2,1)S(1)}, u32[]{:S(2)}, u32[]{:S(2)}) async-start(bf16[4,128,2048]{2,1,0:T(8,128)(2,1)} %copy-done.1), calls=%async_computation.1 | async-start | bytes 4194304 | tf_op jit(solution)/shard_map/all_to_all | solution.py:199
  102.2 5.1 %collective-permute-start.16 = (bf16[16,1024]{1,0:T(8,128)(2,1)S(1)}, bf16[16,1024]{1,0:T(8,128)(2,1)S(1)}, u32[]{:S(2)}, u32[]{:S(2)}) collective-permute-start(bf16[16,1024]{1,0:T(8,128)(2,1)S(1)} %get-tuple-element.48), channel_id=1, source_target_pairs={{0,192},{64,0},{128,64},{192,128},{1,193},{65,1},{129,65},{193,129... | collective-permute-start | bytes 98312 | tf_op jit(solution)/shard_map/ppermute | solution.py:34
  105.7 4.8 %collective-permute-start.17 = (bf16[16,1024]{1,0:T(8,128)(2,1)S(1)}, bf16[16,1024]{1,0:T(8,128)(2,1)S(1)}, u32[]{:S(2)}, u32[]{:S(2)}) collective-permute-start(bf16[16,1024]{1,0:T(8,128)(2,1)S(1)} %get-tuple-element.48), channel_id=1, source_target_pairs={{0,128},{64,192},{128,0},{192,64},{1,129},{65,193},{129,1},{193,65... | collective-permute-start | bytes 98312 | tf_op jit(solution)/shard_map/ppermute | solution.py:34
  105.7 5.7 %collective-permute-start.18 = (bf16[16,1024]{1,0:T(8,128)(2,1)S(1)}, bf16[16,1024]{1,0:T(8,128)(2,1)S(1)}, u32[]{:S(2)}, u32[]{:S(2)}) collective-permute-start(bf16[16,1024]{1,0:T(8,128)(2,1)S(1)} %get-tuple-element.48), channel_id=1, source_target_pairs={{0,64},{64,128},{128,192},{192,0},{1,65},{65,129},{129,193},{193,1... | collective-permute-start | bytes 98312 | tf_op jit(solution)/shard_map/ppermute | solution.py:34
  111.5 6.1 %collective-permute-start.19 = (bf16[64,1024]{1,0:T(8,128)(2,1)S(1)}, bf16[64,1024]{1,0:T(8,128)(2,1)S(1)}, u32[]{:S(2)}, u32[]{:S(2)}) collective-permute-start(bf16[64,1024]{1,0:T(8,128)(2,1)S(1)} %pad_maximum_fusion.6), channel_id=1, source_target_pairs={{0,48},{16,0},{32,16},{48,32},{1,49},{17,1},{33,17},{49,33},{2,50}... | collective-permute-start | bytes 393224 | tf_op jit(solution)/shard_map/ppermute | solution.py:34
  112.7 6.5 %collective-permute-start.20 = (bf16[64,1024]{1,0:T(8,128)(2,1)S(1)}, bf16[64,1024]{1,0:T(8,128)(2,1)S(1)}, u32[]{:S(2)}, u32[]{:S(2)}) collective-permute-start(bf16[64,1024]{1,0:T(8,128)(2,1)S(1)} %pad_maximum_fusion.6), channel_id=1, source_target_pairs={{0,32},{16,48},{32,0},{48,16},{1,33},{17,49},{33,1},{49,17},{2,34}... | collective-permute-start | bytes 393224 | tf_op jit(solution)/shard_map/ppermute | solution.py:34
  113.9 6.1 %collective-permute-start.21 = (bf16[64,1024]{1,0:T(8,128)(2,1)S(1)}, bf16[64,1024]{1,0:T(8,128)(2,1)S(1)}, u32[]{:S(2)}, u32[]{:S(2)}) collective-permute-start(bf16[64,1024]{1,0:T(8,128)(2,1)S(1)} %pad_maximum_fusion.6), channel_id=1, source_target_pairs={{0,16},{16,32},{32,48},{48,0},{1,17},{17,33},{33,49},{49,1},{2,18}... | collective-permute-start | bytes 393224 | tf_op jit(solution)/shard_map/ppermute | solution.py:34
  127.6 1.9 %copy-start.2 = (bf16[1024,512]{1,0:T(8,128)(2,1)S(1)}, bf16[1024,512]{1,0:T(8,128)(2,1)}, u32[]{:S(2)}) copy-start(bf16[1024,512]{1,0:T(8,128)(2,1)} %fusion.basis) | copy-start | bytes 3145732
  127.6 1.9 %collective-permute-start.22 = (bf16[256,1024]{1,0:T(8,128)(2,1)S(1)}, bf16[256,1024]{1,0:T(8,128)(2,1)S(1)}, u32[]{:S(2)}, u32[]{:S(2)}) collective-permute-start(bf16[256,1024]{1,0:T(8,128)(2,1)S(1)} %pad_maximum_fusion.5.near), channel_id=1, source_target_pairs={{0,8},{8,0},{1,9},{9,1},{2,10},{10,2},{3,11},{11,3},{4,12},{12,4},... | collective-permute-start | bytes 1572872 | tf_op jit(solution)/shard_map/ppermute | solution.py:34

commit v4 on v3

--- a/solution.py
+++ b/solution.py
@@ -204,9 +204,8 @@
     row = lax.broadcasted_iota(jnp.int32, (512, 512), 0)
     order = (row == owner_row(slot, True)).astype(NARROW)
     own_basis = dot(projector, order, (1, 0)).astype(NARROW)
-    near = after(spread(spread(direction, "zl"), "y"), own_basis, home)
+    near = after(spread(spread(direction, "zl"), "y"), own_basis)
     far = send(near, c=1)
-    (input_grad,) = call(place_kernel, [((128, 8192), NARROW)], 1 << 20, 4 << 20)(home)
     (weight_update,) = call(
         update_kernel,
         [((1024, 1024), WIDE)],
@@ -220,6 +219,9 @@
         ],
         out_specs=[pl.BlockSpec((256, 1024), lambda i: (i, 0))],
     )(own_basis, near, far)
+    (input_grad,) = call(place_kernel, [((128, 8192), NARROW)], 1 << 20, 4 << 20)(
+        after(home, weight_update)
+    )
     return (input_grad, weight_update, new_first, new_second)
 
 

time: 135 us -> 132 us (0.978)
  waiting for transfers between devices: 62.9 us -> 57.9 us
  starting transfers between devices: 46.4 us -> 48.9 us
    all_to_all x1, waiting for transfers between devices: 7.62 us -> 2.53 us  [body(): home = lax.all_to_all(home, 'x', 0, 0, tiled=True)]
    ppermute x23, starting transfers between devices: 36.5 us -> 39 us  [send(): return lax.ppermute(value, axes, pairs)]
    unnamed x28 -> x26, local copies, waits for them, and re-layouts: 3.59 us -> 3.58 us
  transfers between devices with their start and end apart: 25 -> 25, of which waited for: 17 -> 19; matrix products, arithmetic and copies ran while one was open for 3% -> 2% of each run, Pallas kernels for 4% -> 5%
where the time goes in v4:
time: 132 us; the launch traced here: 129 us
  waiting for transfers between devices  57.9 us (44%)
  starting transfers between devices  48.9 us (37%)
  Pallas kernels  10.5 us (8%)
  local copies, waits for them, and re-layouts  7.66 us (6%)
  other arithmetic  2.63 us (2%)
    ppermute x23, waiting for transfers between devices, send(): return lax.ppermute(value, axes, pairs)  55.4 us
    ppermute x23, starting transfers between devices, send(): return lax.ppermute(value, axes, pairs)  39 us
    all_to_all x1, starting transfers between devices, body(): kept = lax.all_to_all(kept, ('zl', 'zh'), 0, 0, tiled=True)  6.22 us
    all_to_all x1, starting transfers between devices, body(): home = lax.all_to_all(home, 'x', 0, 0, tiled=True)  3.75 us
    unnamed x26, local copies, waits for them, and re-layouts  3.58 us
    pallas_call x1, Pallas kernels, body(): call(update_kernel, [((1024, 1024), WIDE)], 1 << 30, 6 << 20, grid=(4,),...  3.26 us
  transfers between devices with their start and end apart: 25, of which 19 were waited for; matrix products, arithmetic and copies ran while one was open for 2% of the time, Pallas kernels for 5%

profile of v4, /device:TPU:8, one launch (start us, length us, event | category | flops | bytes accessed | tf_op | source)
XLA Modules:
  0.0 129.4 jit_solution(12108684360591557434)
XLA Ops:
  0.7 1.1 constant_dynamic-slice_fusion.1
  1.8 1.1 constant_dynamic-slice_fusion
  3.2 0.8 copy-done.2
  4.1 7.3 %collective-permute-start.3 = (bf16[384,1024]{1,0:T(8,128)(2,1)S(1)}, bf16[384,1024]{1,0:T(8,128)(2,1)S(1)}, u32[]{:S(2)}, u32[]{:S(2)}) collective-permute-start(bf16[384,1024]{1,0:T(8,128)(2,1)S(1)} %pad_maximum_fusion.4), channel_id=1, source_target_pairs={{0,1},{1,0},{2,3},{3,2},{4,5},{5,4},{6,7},{7,6},{8,9},{9,8},{10,11... | collective-permute-start | bytes 2359304 | tf_op jit(solution)/shard_map/ppermute | solution.py:34
  11.4 1.5 %collective-permute-start = (bf16[128,3072]{1,0:T(8,128)(2,1)S(1)}, bf16[128,3072]{1,0:T(8,128)(2,1)S(1)}, u32[]{:S(2)}, u32[]{:S(2)}) collective-permute-start(bf16[128,3072]{1,0:T(8,128)(2,1)S(1)} %get-tuple-element.27), channel_id=1, source_target_pairs={{0,2},{2,4},{4,6},{6,0},{1,3},{3,5},{5,7},{7,1},{8,10},{10,12},{12... | collective-permute-start | bytes 2359304 | tf_op jit(solution)/shard_map/ppermute | solution.py:34
  12.9 2.7 %collective-permute-start.1 = (bf16[128,3072]{1,0:T(8,128)(2,1)S(1)}, bf16[128,3072]{1,0:T(8,128)(2,1)S(1)}, u32[]{:S(2)}, u32[]{:S(2)}) collective-permute-start(bf16[128,3072]{1,0:T(8,128)(2,1)S(1)} %get-tuple-element.28), channel_id=1, source_target_pairs={{0,4},{2,6},{4,0},{6,2},{1,5},{3,7},{5,1},{7,3},{8,12},{10,14},{12... | collective-permute-start | bytes 2359304 | tf_op jit(solution)/shard_map/ppermute | solution.py:34
  15.6 1.4 %collective-permute-start.2 = (bf16[128,3072]{1,0:T(8,128)(2,1)S(1)}, bf16[128,3072]{1,0:T(8,128)(2,1)S(1)}, u32[]{:S(2)}, u32[]{:S(2)}) collective-permute-start(bf16[128,3072]{1,0:T(8,128)(2,1)S(1)} %get-tuple-element.29), channel_id=1, source_target_pairs={{0,6},{2,0},{4,2},{6,4},{1,7},{3,1},{5,3},{7,5},{8,14},{10,8},{12,... | collective-permute-start | bytes 2359304 | tf_op jit(solution)/shard_map/ppermute | solution.py:34
  17.1 27.4 %collective-permute-done.3 = bf16[384,1024]{1,0:T(8,128)(2,1)S(1)} collective-permute-done((bf16[384,1024]{1,0:T(8,128)(2,1)S(1)}, bf16[384,1024]{1,0:T(8,128)(2,1)S(1)}, u32[]{:S(2)}, u32[]{:S(2)}) %collective-permute-start.3) | collective-permute-done | bytes 786464 | tf_op jit(solution)/shard_map/ppermute | solution.py:34
  44.6 0.7 copy-done.8
  45.4 1.2 collective-permute-done.4.far
  46.5 1.3 %shard_map.93.basis = bf16[512,2048]{1,0:T(8,128)(2,1)S(1)} custom-call(bf16[1024,512]{1,0:T(8,128)(2,1)S(1)} %copy-done, bf16[256,1024]{1,0:T(8,128)(2,1)S(1)} %slice.32.part, bf16[256,1024]{1,0:T(8,128)(2,1)S(1)} %collective-permute-done.4.far), custom_call_target="tpu_custom_call" | custom-call | flops 1048576 | bytes 1048576 | tf_op jit(solution)/shard_map/pallas_call | solution.py:167
  47.9 1.6 %collective-permute-done.1.xg2 = bf16[128,3072]{1,0:T(8,128)(2,1)S(1)} collective-permute-done((bf16[128,3072]{1,0:T(8,128)(2,1)S(1)}, bf16[128,3072]{1,0:T(8,128)(2,1)S(1)}, u32[]{:S(2)}, u32[]{:S(2)}) %collective-permute-start.1) | collective-permute-done | bytes 786464 | tf_op jit(solution)/shard_map/ppermute | solution.py:34
  49.5 1.9 %shard_map.94 = (bf16[256,1024]{1,0:T(8,128)(2,1)S(1)}, f32[256,1024]{1,0:T(8,128)S(1)}, bf16[512,1024]{1,0:T(8,128)(2,1)S(1)}) custom-call(bf16[128,2048]{1,0:T(8,128)(2,1)S(1)} %get-tuple-element.55.x0, bf16[128,1024]{1,0:T(8,128)(2,1)S(1)} %copy-done.2, bf16[128,3072]{1,0:T(8,128)(2,1)S(1)} %collective-permute-done.xg1, ...), custom_call_target="tpu_custom_call" | custom-call | flops 4294967296 | bytes 10485760 | tf_op jit(solution)/shard_map/pallas_call | solution.py:172
  51.5 1.9 %collective-permute-done.5 = bf16[256,1024]{1,0:T(8,128)(2,1)S(1)} collective-permute-done((bf16[256,1024]{1,0:T(8,128)(2,1)S(1)}, bf16[256,1024]{1,0:T(8,128)(2,1)S(1)}, u32[]{:S(2)}, u32[]{:S(2)}) %collective-permute-start.5) | collective-permute-done | bytes 524320 | tf_op jit(solution)/shard_map/ppermute | solution.py:34
  53.6 1.7 %collective-permute-start.6 = (bf16[64,1024]{1,0:T(8,128)(2,1)S(1)}, bf16[64,1024]{1,0:T(8,128)(2,1)S(1)}, u32[]{:S(2)}, u32[]{:S(2)}) collective-permute-start(bf16[64,1024]{1,0:T(8,128)(2,1)S(1)} %get-tuple-element.61), channel_id=1, source_target_pairs={{0,16},{16,32},{32,48},{48,0},{1,17},{17,33},{33,49},{49,1},{2,18}... | collective-permute-start | bytes 393224 | tf_op jit(solution)/shard_map/ppermute | solution.py:34
  55.2 0.9 collective-permute-start.7
  56.2 2.4 %collective-permute-start.8 = (bf16[64,1024]{1,0:T(8,128)(2,1)S(1)}, bf16[64,1024]{1,0:T(8,128)(2,1)S(1)}, u32[]{:S(2)}, u32[]{:S(2)}) collective-permute-start(bf16[64,1024]{1,0:T(8,128)(2,1)S(1)} %get-tuple-element.59), channel_id=1, source_target_pairs={{0,48},{16,0},{32,16},{48,32},{1,49},{17,1},{33,17},{49,33},{2,50}... | collective-permute-start | bytes 393224 | tf_op jit(solution)/shard_map/ppermute | solution.py:34
  58.6 0.7 collective-permute-done.6
  59.3 3.8 %collective-permute-done.7 = bf16[64,1024]{1,0:T(8,128)(2,1)S(1)} collective-permute-done((bf16[64,1024]{1,0:T(8,128)(2,1)S(1)}, bf16[64,1024]{1,0:T(8,128)(2,1)S(1)}, u32[]{:S(2)}, u32[]{:S(2)}) %collective-permute-start.7) | collective-permute-done | bytes 131104 | tf_op jit(solution)/shard_map/ppermute | solution.py:34
  63.1 1.0 collective-permute-done.8
  64.9 6.2 %all-to-all-start = ((bf16[8,16,1024]{2,1,0:T(8,128)(2,1)}), bf16[8,16,1024]{2,1,0:T(8,128)(2,1)S(1)}, u32[]{:S(2)}, u32[]{:S(2)}) async-start(bf16[8,16,1024]{2,1,0:T(8,128)(2,1)} %bitcast.5), calls=%async_computation | async-start | bytes 524288 | tf_op jit(solution)/shard_map/all_to_all | solution.py:185
  71.1 1.0 slice.37
  72.1 0.9 collective-permute-start.9
  73.0 2.0 %collective-permute-start.10 = (bf16[128,1024]{1,0:T(8,128)(2,1)S(1)}, bf16[128,1024]{1,0:T(8,128)(2,1)S(1)}, u32[]{:S(2)}, u32[]{:S(2)}) collective-permute-start(bf16[128,1024]{1,0:T(8,128)(2,1)S(1)} %slice.37), channel_id=1, source_target_pairs={{0,32},{16,48},{32,0},{48,16},{1,33},{17,49},{33,1},{49,17},{2,34}... | collective-permute-start | bytes 786440 | tf_op jit(solution)/shard_map/ppermute | solution.py:34
  75.0 1.7 %collective-permute-start.11 = (bf16[128,1024]{1,0:T(8,128)(2,1)S(1)}, bf16[128,1024]{1,0:T(8,128)(2,1)}, u32[]{:S(2)}, u32[]{:S(2)}) collective-permute-start(bf16[128,1024]{1,0:T(8,128)(2,1)S(1)} %slice.37), channel_id=1, source_target_pairs={{0,16},{16,32},{32,48},{48,0},{1,17},{17,33},{33,49},{49,1},{2,18}... | collective-permute-start | bytes 786440 | tf_op jit(solution)/shard_map/ppermute | solution.py:34
  76.6 4.6 %collective-permute-done.9 = bf16[128,1024]{1,0:T(8,128)(2,1)S(1)} collective-permute-done((bf16[128,1024]{1,0:T(8,128)(2,1)S(1)}, bf16[128,1024]{1,0:T(8,128)(2,1)S(1)}, u32[]{:S(2)}, u32[]{:S(2)}) %collective-permute-start.9) | collective-permute-done | bytes 262176 | tf_op jit(solution)/shard_map/ppermute | solution.py:34
  81.2 4.3 %collective-permute-done.10 = bf16[128,1024]{1,0:T(8,128)(2,1)S(1)} collective-permute-done((bf16[128,1024]{1,0:T(8,128)(2,1)S(1)}, bf16[128,1024]{1,0:T(8,128)(2,1)S(1)}, u32[]{:S(2)}, u32[]{:S(2)}) %collective-permute-start.10) | collective-permute-done | bytes 262176 | tf_op jit(solution)/shard_map/ppermute | solution.py:34
  86.2 0.8 collective-permute-done.11
  87.0 1.3 %pad_maximum_fusion.3.part = bf16[512,1024]{1,0:T(8,128)(2,1)S(1)} fusion(bf16[128,1024]{1,0:T(8,128)(2,1)} %collective-permute-done.11, bf16[128,1024]{1,0:T(8,128)(2,1)} %copy-done.10, bf16[128,1024]{1,0:T(8,128)(2,1)} %copy-done.9, bf16[128,1024]{1,0:T(8,128)(2,1)} %copy-done.7), kind=kLoop, calls=%fused_computation.6 | loop fusion | flops 4194304 | bytes 2097152 | tf_op jit(solution)/shard_map/max | solution.py:80
  88.7 1.6 %collective-permute-start.12 = (f32[16,1024]{1,0:T(8,128)S(1)}, f32[16,1024]{1,0:T(8,128)S(1)}, u32[]{:S(2)}, u32[]{:S(2)}) collective-permute-start(f32[16,1024]{1,0:T(8,128)S(1)} %convert_reduce_fusion), channel_id=1, source_target_pairs={{0,2},{2,4},{4,6},{6,0},{1,3},{3,5},{5,7},{7,1},{8,10},{10,12},{12... | collective-permute-start | bytes 196616 | tf_op jit(solution)/shard_map/ppermute | solution.py:34
  90.2 1.7 %collective-permute-start.13 = (f32[16,1024]{1,0:T(8,128)S(1)}, f32[16,1024]{1,0:T(8,128)S(1)}, u32[]{:S(2)}, u32[]{:S(2)}) collective-permute-start(f32[16,1024]{1,0:T(8,128)S(1)} %convert_reduce_fusion), channel_id=1, source_target_pairs={{0,6},{2,0},{4,2},{6,4},{1,7},{3,1},{5,3},{7,5},{8,14},{10,8},{12,... | collective-permute-start | bytes 196616 | tf_op jit(solution)/shard_map/ppermute | solution.py:34
  92.0 1.8 %collective-permute-start.14 = (f32[16,1024]{1,0:T(8,128)S(1)}, f32[16,1024]{1,0:T(8,128)S(1)}, u32[]{:S(2)}, u32[]{:S(2)}) collective-permute-start(f32[16,1024]{1,0:T(8,128)S(1)} %convert_reduce_fusion), channel_id=1, source_target_pairs={{0,4},{2,6},{4,0},{6,2},{1,5},{3,7},{5,1},{7,3},{8,12},{10,14},{12... | collective-permute-start | bytes 196616 | tf_op jit(solution)/shard_map/ppermute | solution.py:34
  93.8 2.4 %shard_map.95 = bf16[4,128,2048]{2,1,0:T(8,128)(2,1)S(1)} custom-call(bf16[512,1024]{1,0:T(8,128)(2,1)S(1)} %copy-done.5, bf16[1024,1024]{1,0:T(8,128)(2,1)S(1)} %copy-done.3, bf16[512,1024]{1,0:T(8,128)(2,1)S(1)} %pad_maximum_fusion.3.part, bf16[512,1024]{1,0:T(8,128)(2,1)S(1)} %collective-permute-done.15.other), custom_call_target="tpu_custom_call" | custom-call | flops 2147483648 | bytes 8388608 | tf_op jit(solution)/shard_map/pallas_call | solution.py:191
  96.2 1.3 %copy-done.1 = bf16[4,128,2048]{2,1,0:T(8,128)(2,1)} copy-done((bf16[4,128,2048]{2,1,0:T(8,128)(2,1)}, bf16[4,128,2048]{2,1,0:T(8,128)(2,1)S(1)}, u32[]{:S(2)}) %copy-start.1) | copy-done | bytes 2097176
  97.8 3.8 %all-to-all-start.1 = ((bf16[4,128,2048]{2,1,0:T(8,128)(2,1)}), bf16[4,128,2048]{2,1,0:T(8,128)(2,1)S(1)}, u32[]{:S(2)}, u32[]{:S(2)}) async-start(bf16[4,128,2048]{2,1,0:T(8,128)(2,1)} %copy-done.1), calls=%async_computation.1 | async-start | bytes 4194304 | tf_op jit(solution)/shard_map/all_to_all | solution.py:199
  102.3 1.7 %collective-permute-start.18 = (bf16[16,1024]{1,0:T(8,128)(2,1)S(1)}, bf16[16,1024]{1,0:T(8,128)(2,1)S(1)}, u32[]{:S(2)}, u32[]{:S(2)}) collective-permute-start(bf16[16,1024]{1,0:T(8,128)(2,1)S(1)} %get-tuple-element.50), channel_id=1, source_target_pairs={{0,64},{64,128},{128,192},{192,0},{1,65},{65,129},{129,193},{193,1... | collective-permute-start | bytes 98312 | tf_op jit(solution)/shard_map/ppermute | solution.py:34
  104.0 2.4 %collective-permute-start.17 = (bf16[16,1024]{1,0:T(8,128)(2,1)S(1)}, bf16[16,1024]{1,0:T(8,128)(2,1)S(1)}, u32[]{:S(2)}, u32[]{:S(2)}) collective-permute-start(bf16[16,1024]{1,0:T(8,128)(2,1)S(1)} %get-tuple-element.50), channel_id=1, source_target_pairs={{0,128},{64,192},{128,0},{192,64},{1,129},{65,193},{129,1},{193,65... | collective-permute-start | bytes 98312 | tf_op jit(solution)/shard_map/ppermute | solution.py:34
  106.4 1.5 %collective-permute-start.16 = (bf16[16,1024]{1,0:T(8,128)(2,1)S(1)}, bf16[16,1024]{1,0:T(8,128)(2,1)S(1)}, u32[]{:S(2)}, u32[]{:S(2)}) collective-permute-start(bf16[16,1024]{1,0:T(8,128)(2,1)S(1)} %get-tuple-element.50), channel_id=1, source_target_pairs={{0,192},{64,0},{128,64},{192,128},{1,193},{65,1},{129,65},{193,129... | collective-permute-start | bytes 98312 | tf_op jit(solution)/shard_map/ppermute | solution.py:34
  109.0 1.3 %collective-permute-done.16 = bf16[16,1024]{1,0:T(8,128)(2,1)S(1)} collective-permute-done((bf16[16,1024]{1,0:T(8,128)(2,1)S(1)}, bf16[16,1024]{1,0:T(8,128)(2,1)S(1)}, u32[]{:S(2)}, u32[]{:S(2)}) %collective-permute-start.16) | collective-permute-done | bytes 32800 | tf_op jit(solution)/shard_map/ppermute | solution.py:34
  110.3 1.5 %collective-permute-start.21 = (bf16[64,1024]{1,0:T(8,128)(2,1)S(1)}, bf16[64,1024]{1,0:T(8,128)(2,1)S(1)}, u32[]{:S(2)}, u32[]{:S(2)}) collective-permute-start(bf16[64,1024]{1,0:T(8,128)(2,1)S(1)} %pad_maximum_fusion.6), channel_id=1, source_target_pairs={{0,16},{16,32},{32,48},{48,0},{1,17},{17,33},{33,49},{49,1},{2,18}... | collective-permute-start | bytes 393224 | tf_op jit(solution)/shard_map/ppermute | solution.py:34
  111.8 3.1 %collective-permute-start.20 = (bf16[64,1024]{1,0:T(8,128)(2,1)S(1)}, bf16[64,1024]{1,0:T(8,128)(2,1)S(1)}, u32[]{:S(2)}, u32[]{:S(2)}) collective-permute-start(bf16[64,1024]{1,0:T(8,128)(2,1)S(1)} %pad_maximum_fusion.6), channel_id=1, source_target_pairs={{0,32},{16,48},{32,0},{48,16},{1,33},{17,49},{33,1},{49,17},{2,34}... | collective-permute-start | bytes 393224 | tf_op jit(solution)/shard_map/ppermute | solution.py:34
  115.6 0.8 fusion.basis
  117.0 1.3 %collective-permute-done.20 = bf16[64,1024]{1,0:T(8,128)(2,1)S(1)} collective-permute-done((bf16[64,1024]{1,0:T(8,128)(2,1)S(1)}, bf16[64,1024]{1,0:T(8,128)(2,1)S(1)}, u32[]{:S(2)}, u32[]{:S(2)}) %collective-permute-start.20) | collective-permute-done | bytes 131104 | tf_op jit(solution)/shard_map/ppermute | solution.py:34
  118.3 1.6 %collective-permute-done.19 = bf16[64,1024]{1,0:T(8,128)(2,1)S(1)} collective-permute-done((bf16[64,1024]{1,0:T(8,128)(2,1)S(1)}, bf16[64,1024]{1,0:T(8,128)(2,1)S(1)}, u32[]{:S(2)}, u32[]{:S(2)}) %collective-permute-start.19) | collective-permute-done | bytes 131104 | tf_op jit(solution)/shard_map/ppermute | solution.py:34
  120.0 1.9 %collective-permute-done.22.far = bf16[256,1024]{1,0:T(8,128)(2,1)S(1)} collective-permute-done((bf16[256,1024]{1,0:T(8,128)(2,1)S(1)}, bf16[256,1024]{1,0:T(8,128)(2,1)S(1)}, u32[]{:S(2)}, u32[]{:S(2)}) %collective-permute-start.22) | collective-permute-done | bytes 524320 | tf_op jit(solution)/shard_map/ppermute | solution.py:34
  121.9 3.3 %shard_map.96 = f32[1024,1024]{1,0:T(8,128)} custom-call(bf16[1024,512]{1,0:T(8,128)(2,1)S(1)} %fusion.basis, bf16[256,1024]{1,0:T(8,128)(2,1)S(1)} %pad_maximum_fusion.5.near, bf16[256,1024]{1,0:T(8,128)(2,1)S(1)} %collective-permute-done.22.far), custom_call_target="tpu_custom_call" | custom-call | flops 1073741824 | bytes 6291456 | tf_op jit(solution)/shard_map/pallas_call | solution.py:209
  125.2 2.5 %all-to-all-done.1.blocks = bf16[4,128,2048]{2,1,0:T(8,128)(2,1)S(1)} async-done(((bf16[4,128,2048]{2,1,0:T(8,128)(2,1)}), bf16[4,128,2048]{2,1,0:T(8,128)(2,1)S(1)}, u32[]{:S(2)}, u32[]{:S(2)}) %all-to-all-start.1) | async-done | bytes 2097184 | tf_op jit(solution)/shard_map/all_to_all | solution.py:199
  127.7 1.6 %shard_map.97 = bf16[128,8192]{1,0:T(8,128)(2,1)} custom-call(bf16[4,128,2048]{2,1,0:T(8,128)(2,1)S(1)} %all-to-all-done.1.blocks), custom_call_target="tpu_custom_call" | custom-call | flops 1048576 | bytes 4194304 | tf_op jit(solution)/shard_map/pallas_call | solution.py:222
  (52 shorter events, 6.2 us)
Async XLA Ops:
  0.6 2.4 %copy-start.6 = (bf16[128,8192]{1,0:T(8,128)(2,1)S(1)}, bf16[128,8192]{1,0:T(8,128)(2,1)}, u32[]{:S(2)}) copy-start(bf16[128,8192]{1,0:T(8,128)(2,1)} %param.6) | copy-start | bytes 6291460
  3.0 1.0 copy-start.2
  4.0 42.6 %copy-start = (bf16[1024,512]{1,0:T(8,128)(2,1)S(1)}, bf16[1024,512]{1,0:T(8,128)(2,1)}, u32[]{:S(2)}) copy-start(bf16[1024,512]{1,0:T(8,128)(2,1)} %mine.1) | copy-start | bytes 3145732
  4.1 40.3 %collective-permute-start.3 = (bf16[384,1024]{1,0:T(8,128)(2,1)S(1)}, bf16[384,1024]{1,0:T(8,128)(2,1)S(1)}, u32[]{:S(2)}, u32[]{:S(2)}) collective-permute-start(bf16[384,1024]{1,0:T(8,128)(2,1)S(1)} %pad_maximum_fusion.4), channel_id=1, source_target_pairs={{0,1},{1,0},{2,3},{3,2},{4,5},{5,4},{6,7},{7,6},{8,9},{9,8},{10,11... | collective-permute-start | bytes 2359304 | tf_op jit(solution)/shard_map/ppermute | solution.py:34
  11.4 36.5 %collective-permute-start = (bf16[128,3072]{1,0:T(8,128)(2,1)S(1)}, bf16[128,3072]{1,0:T(8,128)(2,1)S(1)}, u32[]{:S(2)}, u32[]{:S(2)}) collective-permute-start(bf16[128,3072]{1,0:T(8,128)(2,1)S(1)} %get-tuple-element.27), channel_id=1, source_target_pairs={{0,2},{2,4},{4,6},{6,0},{1,3},{3,5},{5,7},{7,1},{8,10},{10,12},{12... | collective-permute-start | bytes 2359304 | tf_op jit(solution)/shard_map/ppermute | solution.py:34
  12.9 36.6 %collective-permute-start.1 = (bf16[128,3072]{1,0:T(8,128)(2,1)S(1)}, bf16[128,3072]{1,0:T(8,128)(2,1)S(1)}, u32[]{:S(2)}, u32[]{:S(2)}) collective-permute-start(bf16[128,3072]{1,0:T(8,128)(2,1)S(1)} %get-tuple-element.28), channel_id=1, source_target_pairs={{0,4},{2,6},{4,0},{6,2},{1,5},{3,7},{5,1},{7,3},{8,12},{10,14},{12... | collective-permute-start | bytes 2359304 | tf_op jit(solution)/shard_map/ppermute | solution.py:34
  15.6 33.8 %collective-permute-start.2 = (bf16[128,3072]{1,0:T(8,128)(2,1)S(1)}, bf16[128,3072]{1,0:T(8,128)(2,1)S(1)}, u32[]{:S(2)}, u32[]{:S(2)}) collective-permute-start(bf16[128,3072]{1,0:T(8,128)(2,1)S(1)} %get-tuple-element.29), channel_id=1, source_target_pairs={{0,6},{2,0},{4,2},{6,4},{1,7},{3,1},{5,3},{7,5},{8,14},{10,8},{12,... | collective-permute-start | bytes 2359304 | tf_op jit(solution)/shard_map/ppermute | solution.py:34
  44.5 0.9 copy-start.8
  44.5 2.0 %collective-permute-start.4 = (bf16[256,1024]{1,0:T(8,128)(2,1)S(1)}, bf16[256,1024]{1,0:T(8,128)(2,1)S(1)}, u32[]{:S(2)}, u32[]{:S(2)}) collective-permute-start(bf16[256,1024]{1,0:T(8,128)(2,1)S(1)} %slice.32.part), channel_id=1, source_target_pairs={{0,8},{8,0},{1,9},{9,1},{2,10},{10,2},{3,11},{11,3},{4,12},{12,4},... | collective-permute-start | bytes 1572872 | tf_op jit(solution)/shard_map/ppermute | solution.py:34
  51.4 12.7 %copy-start.4 = (bf16[512,1024]{1,0:T(8,128)(2,1)}, bf16[512,1024]{1,0:T(8,128)(2,1)S(1)}, u32[]{:S(2)}) copy-start(bf16[512,1024]{1,0:T(8,128)(2,1)S(1)} %get-tuple-element.37.grads) | copy-start | bytes 3145732
  51.4 2.0 %collective-permute-start.5 = (bf16[256,1024]{1,0:T(8,128)(2,1)S(1)}, bf16[256,1024]{1,0:T(8,128)(2,1)S(1)}, u32[]{:S(2)}, u32[]{:S(2)}) collective-permute-start(bf16[256,1024]{1,0:T(8,128)(2,1)S(1)} %get-tuple-element.32), channel_id=1, source_target_pairs={{0,8},{8,0},{1,9},{9,1},{2,10},{10,2},{3,11},{11,3},{4,12},{12,4},... | collective-permute-start | bytes 1572872 | tf_op jit(solution)/shard_map/ppermute | solution.py:34
  53.6 5.7 %collective-permute-start.6 = (bf16[64,1024]{1,0:T(8,128)(2,1)S(1)}, bf16[64,1024]{1,0:T(8,128)(2,1)S(1)}, u32[]{:S(2)}, u32[]{:S(2)}) collective-permute-start(bf16[64,1024]{1,0:T(8,128)(2,1)S(1)} %get-tuple-element.61), channel_id=1, source_target_pairs={{0,16},{16,32},{32,48},{48,0},{1,17},{17,33},{33,49},{49,1},{2,18}... | collective-permute-start | bytes 393224 | tf_op jit(solution)/shard_map/ppermute | solution.py:34
  55.2 7.9 %collective-permute-start.7 = (bf16[64,1024]{1,0:T(8,128)(2,1)S(1)}, bf16[64,1024]{1,0:T(8,128)(2,1)S(1)}, u32[]{:S(2)}, u32[]{:S(2)}) collective-permute-start(bf16[64,1024]{1,0:T(8,128)(2,1)S(1)} %get-tuple-element.60), channel_id=1, source_target_pairs={{0,32},{16,48},{32,0},{48,16},{1,33},{17,49},{33,1},{49,17},{2,34}... | collective-permute-start | bytes 393224 | tf_op jit(solution)/shard_map/ppermute | solution.py:34
  56.2 7.9 %collective-permute-start.8 = (bf16[64,1024]{1,0:T(8,128)(2,1)S(1)}, bf16[64,1024]{1,0:T(8,128)(2,1)S(1)}, u32[]{:S(2)}, u32[]{:S(2)}) collective-permute-start(bf16[64,1024]{1,0:T(8,128)(2,1)S(1)} %get-tuple-element.59), channel_id=1, source_target_pairs={{0,48},{16,0},{32,16},{48,32},{1,49},{17,1},{33,17},{49,33},{2,50}... | collective-permute-start | bytes 393224 | tf_op jit(solution)/shard_map/ppermute | solution.py:34
  64.2 29.6 %copy-start.3 = (bf16[1024,1024]{1,0:T(8,128)(2,1)S(1)}, bf16[1024,1024]{1,0:T(8,128)(2,1)}, u32[]{:S(2)}) copy-start(bf16[1024,1024]{1,0:T(8,128)(2,1)} %weight.1) | copy-start | bytes 6291460
  64.9 22.1 %all-to-all-start = ((bf16[8,16,1024]{2,1,0:T(8,128)(2,1)}), bf16[8,16,1024]{2,1,0:T(8,128)(2,1)S(1)}, u32[]{:S(2)}, u32[]{:S(2)}) async-start(bf16[8,16,1024]{2,1,0:T(8,128)(2,1)} %bitcast.5), calls=%async_computation | async-start | bytes 524288 | tf_op jit(solution)/shard_map/all_to_all | solution.py:185
  72.1 13.4 %copy-start.7 = (bf16[128,1024]{1,0:T(8,128)(2,1)}, bf16[128,1024]{1,0:T(8,128)(2,1)S(1)}, u32[]{:S(2)}) copy-start(bf16[128,1024]{1,0:T(8,128)(2,1)S(1)} %slice.37) | copy-start | bytes 786436
  72.1 9.1 %collective-permute-start.9 = (bf16[128,1024]{1,0:T(8,128)(2,1)S(1)}, bf16[128,1024]{1,0:T(8,128)(2,1)S(1)}, u32[]{:S(2)}, u32[]{:S(2)}) collective-permute-start(bf16[128,1024]{1,0:T(8,128)(2,1)S(1)} %slice.37), channel_id=1, source_target_pairs={{0,48},{16,0},{32,16},{48,32},{1,49},{17,1},{33,17},{49,33},{2,50}... | collective-permute-start | bytes 786440 | tf_op jit(solution)/shard_map/ppermute | solution.py:34
  73.0 12.5 %collective-permute-start.10 = (bf16[128,1024]{1,0:T(8,128)(2,1)S(1)}, bf16[128,1024]{1,0:T(8,128)(2,1)S(1)}, u32[]{:S(2)}, u32[]{:S(2)}) collective-permute-start(bf16[128,1024]{1,0:T(8,128)(2,1)S(1)} %slice.37), channel_id=1, source_target_pairs={{0,32},{16,48},{32,0},{48,16},{1,33},{17,49},{33,1},{49,17},{2,34}... | collective-permute-start | bytes 786440 | tf_op jit(solution)/shard_map/ppermute | solution.py:34
  75.0 12.0 %collective-permute-start.11 = (bf16[128,1024]{1,0:T(8,128)(2,1)S(1)}, bf16[128,1024]{1,0:T(8,128)(2,1)}, u32[]{:S(2)}, u32[]{:S(2)}) collective-permute-start(bf16[128,1024]{1,0:T(8,128)(2,1)S(1)} %slice.37), channel_id=1, source_target_pairs={{0,16},{16,32},{32,48},{48,0},{1,17},{17,33},{33,49},{49,1},{2,18}... | collective-permute-start | bytes 786440 | tf_op jit(solution)/shard_map/ppermute | solution.py:34
  81.2 4.3 %copy-start.9 = (bf16[128,1024]{1,0:T(8,128)(2,1)}, bf16[128,1024]{1,0:T(8,128)(2,1)S(1)}, u32[]{:S(2)}) copy-start(bf16[128,1024]{1,0:T(8,128)(2,1)S(1)} %collective-permute-done.9) | copy-start | bytes 786436
  85.5 0.7 copy-start.10
  87.0 6.8 %copy-start.5 = (bf16[512,1024]{1,0:T(8,128)(2,1)S(1)}, bf16[512,1024]{1,0:T(8,128)(2,1)}, u32[]{:S(2)}) copy-start(bf16[512,1024]{1,0:T(8,128)(2,1)} %copy-done.4) | copy-start | bytes 3145732
  88.3 5.5 %collective-permute-start.15 = (bf16[512,1024]{1,0:T(8,128)(2,1)S(1)}, bf16[512,1024]{1,0:T(8,128)(2,1)S(1)}, u32[]{:S(2)}, u32[]{:S(2)}) collective-permute-start(bf16[512,1024]{1,0:T(8,128)(2,1)S(1)} %pad_maximum_fusion.3.part), channel_id=1, source_target_pairs={{0,8},{8,0},{1,9},{9,1},{2,10},{10,2},{3,11},{11,3},{4,12},{12,4},... | collective-permute-start | bytes 3145736 | tf_op jit(solution)/shard_map/ppermute | solution.py:34
  88.7 8.8 %collective-permute-start.12 = (f32[16,1024]{1,0:T(8,128)S(1)}, f32[16,1024]{1,0:T(8,128)S(1)}, u32[]{:S(2)}, u32[]{:S(2)}) collective-permute-start(f32[16,1024]{1,0:T(8,128)S(1)} %convert_reduce_fusion), channel_id=1, source_target_pairs={{0,2},{2,4},{4,6},{6,0},{1,3},{3,5},{5,7},{7,1},{8,10},{10,12},{12... | collective-permute-start | bytes 196616 | tf_op jit(solution)/shard_map/ppermute | solution.py:34
  90.2 7.3 %collective-permute-start.13 = (f32[16,1024]{1,0:T(8,128)S(1)}, f32[16,1024]{1,0:T(8,128)S(1)}, u32[]{:S(2)}, u32[]{:S(2)}) collective-permute-start(f32[16,1024]{1,0:T(8,128)S(1)} %convert_reduce_fusion), channel_id=1, source_target_pairs={{0,6},{2,0},{4,2},{6,4},{1,7},{3,1},{5,3},{7,5},{8,14},{10,8},{12,... | collective-permute-start | bytes 196616 | tf_op jit(solution)/shard_map/ppermute | solution.py:34
  92.0 5.8 %collective-permute-start.14 = (f32[16,1024]{1,0:T(8,128)S(1)}, f32[16,1024]{1,0:T(8,128)S(1)}, u32[]{:S(2)}, u32[]{:S(2)}) collective-permute-start(f32[16,1024]{1,0:T(8,128)S(1)} %convert_reduce_fusion), channel_id=1, source_target_pairs={{0,4},{2,6},{4,0},{6,2},{1,5},{3,7},{5,1},{7,3},{8,12},{10,14},{12... | collective-permute-start | bytes 196616 | tf_op jit(solution)/shard_map/ppermute | solution.py:34
  96.2 1.3 %copy-start.1 = (bf16[4,128,2048]{2,1,0:T(8,128)(2,1)}, bf16[4,128,2048]{2,1,0:T(8,128)(2,1)S(1)}, u32[]{:S(2)}) copy-start(bf16[4,128,2048]{2,1,0:T(8,128)(2,1)S(1)} %shard_map.95) | copy-start | bytes 6291460
  97.8 3.8 %copy-start.11 = (f32[16,1024]{1,0:T(8,128)S(1)}, f32[16,1024]{1,0:T(8,128)}, u32[]{:S(2)}) copy-start(f32[16,1024]{1,0:T(8,128)} %param.10) | copy-start | bytes 196612
  97.8 3.8 %copy-start.12 = (f32[16,1024]{1,0:T(8,128)S(1)}, f32[16,1024]{1,0:T(8,128)}, u32[]{:S(2)}) copy-start(f32[16,1024]{1,0:T(8,128)} %param.11) | copy-start | bytes 196612
  97.8 29.9 %all-to-all-start.1 = ((bf16[4,128,2048]{2,1,0:T(8,128)(2,1)}), bf16[4,128,2048]{2,1,0:T(8,128)(2,1)S(1)}, u32[]{:S(2)}, u32[]{:S(2)}) async-start(bf16[4,128,2048]{2,1,0:T(8,128)(2,1)} %copy-done.1), calls=%async_computation.1 | async-start | bytes 4194304 | tf_op jit(solution)/shard_map/all_to_all | solution.py:199
  102.3 6.1 %collective-permute-start.18 = (bf16[16,1024]{1,0:T(8,128)(2,1)S(1)}, bf16[16,1024]{1,0:T(8,128)(2,1)S(1)}, u32[]{:S(2)}, u32[]{:S(2)}) collective-permute-start(bf16[16,1024]{1,0:T(8,128)(2,1)S(1)} %get-tuple-element.50), channel_id=1, source_target_pairs={{0,64},{64,128},{128,192},{192,0},{1,65},{65,129},{129,193},{193,1... | collective-permute-start | bytes 98312 | tf_op jit(solution)/shard_map/ppermute | solution.py:34
  104.0 4.9 %collective-permute-start.17 = (bf16[16,1024]{1,0:T(8,128)(2,1)S(1)}, bf16[16,1024]{1,0:T(8,128)(2,1)S(1)}, u32[]{:S(2)}, u32[]{:S(2)}) collective-permute-start(bf16[16,1024]{1,0:T(8,128)(2,1)S(1)} %get-tuple-element.50), channel_id=1, source_target_pairs={{0,128},{64,192},{128,0},{192,64},{1,129},{65,193},{129,1},{193,65... | collective-permute-start | bytes 98312 | tf_op jit(solution)/shard_map/ppermute | solution.py:34
  106.4 3.9 %collective-permute-start.16 = (bf16[16,1024]{1,0:T(8,128)(2,1)S(1)}, bf16[16,1024]{1,0:T(8,128)(2,1)S(1)}, u32[]{:S(2)}, u32[]{:S(2)}) collective-permute-start(bf16[16,1024]{1,0:T(8,128)(2,1)S(1)} %get-tuple-element.50), channel_id=1, source_target_pairs={{0,192},{64,0},{128,64},{192,128},{1,193},{65,1},{129,65},{193,129... | collective-permute-start | bytes 98312 | tf_op jit(solution)/shard_map/ppermute | solution.py:34
  110.3 6.7 %collective-permute-start.21 = (bf16[64,1024]{1,0:T(8,128)(2,1)S(1)}, bf16[64,1024]{1,0:T(8,128)(2,1)S(1)}, u32[]{:S(2)}, u32[]{:S(2)}) collective-permute-start(bf16[64,1024]{1,0:T(8,128)(2,1)S(1)} %pad_maximum_fusion.6), channel_id=1, source_target_pairs={{0,16},{16,32},{32,48},{48,0},{1,17},{17,33},{33,49},{49,1},{2,18}... | collective-permute-start | bytes 393224 | tf_op jit(solution)/shard_map/ppermute | solution.py:34
  111.8 6.5 %collective-permute-start.20 = (bf16[64,1024]{1,0:T(8,128)(2,1)S(1)}, bf16[64,1024]{1,0:T(8,128)(2,1)S(1)}, u32[]{:S(2)}, u32[]{:S(2)}) collective-permute-start(bf16[64,1024]{1,0:T(8,128)(2,1)S(1)} %pad_maximum_fusion.6), channel_id=1, source_target_pairs={{0,32},{16,48},{32,0},{48,16},{1,33},{17,49},{33,1},{49,17},{2,34}... | collective-permute-start | bytes 393224 | tf_op jit(solution)/shard_map/ppermute | solution.py:34
  114.9 5.0 %collective-permute-start.19 = (bf16[64,1024]{1,0:T(8,128)(2,1)S(1)}, bf16[64,1024]{1,0:T(8,128)(2,1)S(1)}, u32[]{:S(2)}, u32[]{:S(2)}) collective-permute-start(bf16[64,1024]{1,0:T(8,128)(2,1)S(1)} %pad_maximum_fusion.6), channel_id=1, source_target_pairs={{0,48},{16,0},{32,16},{48,32},{1,49},{17,1},{33,17},{49,33},{2,50}... | collective-permute-start | bytes 393224 | tf_op jit(solution)/shard_map/ppermute | solution.py:34
  119.9 2.0 %collective-permute-start.22 = (bf16[256,1024]{1,0:T(8,128)(2,1)S(1)}, bf16[256,1024]{1,0:T(8,128)(2,1)S(1)}, u32[]{:S(2)}, u32[]{:S(2)}) collective-permute-start(bf16[256,1024]{1,0:T(8,128)(2,1)S(1)} %pad_maximum_fusion.5.near), channel_id=1, source_target_pairs={{0,8},{8,0},{1,9},{9,1},{2,10},{10,2},{3,11},{11,3},{4,12},{12,4},... | collective-permute-start | bytes 1572872 | tf_op jit(solution)/shard_map/ppermute | solution.py:34

commit v5 on v4

--- a/solution.py
+++ b/solution.py
@@ -124,15 +124,16 @@
     near[...] = dot(projected[:256, :], grads[...], (1, 0))
 
 
-def home_kernel(grads, weight, part, other, out):
+def home_kernel(grads, weight, *refs):
+    quarters, out = refs[:8], refs[8]
     x = lax.axis_index("x")
-    at = 0
-    for some in (weight, part, other):
-        for low in range(0, some.shape[0], 256):
-            block = dot(grads[...], some[low : low + 256, :], (1, 1)).astype(NARROW)
-            for s in range(4):
-                out[lax.rem(x + 4 - s, 4), :, at : at + 256] = block[128 * s : 128 * s + 128]
-            at += 256
+    some = [weight[low : low + 256, :] for low in range(0, 1024, 256)]
+    some += [jnp.concatenate([quarters[i][...], quarters[i + 1][...]], 0) for i in range(0, 8, 2)]
+    for i, rows in enumerate(some):
+        block = dot(grads[...], rows, (1, 1)).astype(NARROW)
+        for s in range(4):
+            to = lax.rem(x + 4 - s, 4)
+            out[to, :, 256 * i : 256 * i + 256] = block[128 * s : 128 * s + 128]
 
 
 def update_kernel(basis, near, far, out):
@@ -186,10 +187,9 @@
     kept, *quarters = lax.optimization_barrier((kept, *quarters))
     kept = kept.astype(WIDE).sum(0)
 
-    weight_part = join(quarters)
-    weight_other = send(weight_part, c=1)
+    quarters += [send(quarter, c=1) for quarter in quarters]
     (home,) = call(home_kernel, [((4, 128, 2048), NARROW)], 2 << 30, 8 << 20)(
-        grads, weight, weight_part, weight_other
+        grads, weight, *quarters
     )
 
     away = [send(kept, x=s) for s in (1, 3, 2)]

time: 132 us -> 136 us (1.030)
  local copies, waits for them, and re-layouts: 7.66 us -> 10.8 us
    unnamed x26 -> x28, local copies, waits for them, and re-layouts: 3.58 us -> 6.7 us
    ppermute x23 -> x26, starting transfers between devices: 39 us -> 39.7 us  [send(): return lax.ppermute(value, axes, pairs)]
    ppermute x23 -> x26, waiting for transfers between devices: 55.4 us -> 55.1 us  [send(): return lax.ppermute(value, axes, pairs)]
  transfers between devices with their start and end apart: 25 -> 28, of which waited for: 19 -> 18; matrix products, arithmetic and copies ran while one was open for 2% -> 3% of each run, Pallas kernels for 5% -> 6%
where the time goes in v5:
time: 136 us; the launch traced here: 133 us
  waiting for transfers between devices  57.4 us (42%)
  starting transfers between devices  49.7 us (37%)
  Pallas kernels  11.4 us (8%)
  local copies, waits for them, and re-layouts  10.8 us (8%)
  other arithmetic  2.24 us (2%)
    ppermute x26, waiting for transfers between devices, send(): return lax.ppermute(value, axes, pairs)  55.1 us
    ppermute x26, starting transfers between devices, send(): return lax.ppermute(value, axes, pairs)  39.7 us
    unnamed x28, local copies, waits for them, and re-layouts  6.7 us
    all_to_all x1, starting transfers between devices, body(): kept = lax.all_to_all(kept, ('zl', 'zh'), 0, 0, tiled=True)  6.22 us
    all_to_all x1, starting transfers between devices, body(): home = lax.all_to_all(home, 'x', 0, 0, tiled=True)  3.75 us
    pallas_call x1, Pallas kernels, body(): call(home_kernel, [((4, 128, 2048), NARROW)], 2 << 30, 8 << 20)  3.31 us
    pallas_call x1, Pallas kernels, body(): call(update_kernel, [((1024, 1024), WIDE)], 1 << 30, 6 << 20, grid=(4,),...  3.26 us
  transfers between devices with their start and end apart: 28, of which 18 were waited for; matrix products, arithmetic and copies ran while one was open for 3% of the time, Pallas kernels for 6%

profile of v5, /device:TPU:8, one launch (start us, length us, event | category | flops | bytes accessed | tf_op | source)
XLA Modules:
  0.0 133.3 jit_solution(12265028815643529697)
XLA Ops:
  0.7 1.1 constant_dynamic-slice_fusion.1
  1.8 1.1 constant_dynamic-slice_fusion
  3.2 0.8 copy-done.2
  4.2 7.3 %collective-permute-start.3 = (bf16[384,1024]{1,0:T(8,128)(2,1)S(1)}, bf16[384,1024]{1,0:T(8,128)(2,1)S(1)}, u32[]{:S(2)}, u32[]{:S(2)}) collective-permute-start(bf16[384,1024]{1,0:T(8,128)(2,1)S(1)} %pad_maximum_fusion.3), channel_id=1, source_target_pairs={{0,1},{1,0},{2,3},{3,2},{4,5},{5,4},{6,7},{7,6},{8,9},{9,8},{10,11... | collective-permute-start | bytes 2359304 | tf_op jit(solution)/shard_map/ppermute | solution.py:34
  11.4 1.5 %collective-permute-start = (bf16[128,3072]{1,0:T(8,128)(2,1)S(1)}, bf16[128,3072]{1,0:T(8,128)(2,1)S(1)}, u32[]{:S(2)}, u32[]{:S(2)}) collective-permute-start(bf16[128,3072]{1,0:T(8,128)(2,1)S(1)} %get-tuple-element.27), channel_id=1, source_target_pairs={{0,2},{2,4},{4,6},{6,0},{1,3},{3,5},{5,7},{7,1},{8,10},{10,12},{12... | collective-permute-start | bytes 2359304 | tf_op jit(solution)/shard_map/ppermute | solution.py:34
  12.9 2.7 %collective-permute-start.1 = (bf16[128,3072]{1,0:T(8,128)(2,1)S(1)}, bf16[128,3072]{1,0:T(8,128)(2,1)S(1)}, u32[]{:S(2)}, u32[]{:S(2)}) collective-permute-start(bf16[128,3072]{1,0:T(8,128)(2,1)S(1)} %get-tuple-element.28), channel_id=1, source_target_pairs={{0,4},{2,6},{4,0},{6,2},{1,5},{3,7},{5,1},{7,3},{8,12},{10,14},{12... | collective-permute-start | bytes 2359304 | tf_op jit(solution)/shard_map/ppermute | solution.py:34
  15.7 1.4 %collective-permute-start.2 = (bf16[128,3072]{1,0:T(8,128)(2,1)S(1)}, bf16[128,3072]{1,0:T(8,128)(2,1)S(1)}, u32[]{:S(2)}, u32[]{:S(2)}) collective-permute-start(bf16[128,3072]{1,0:T(8,128)(2,1)S(1)} %get-tuple-element.29), channel_id=1, source_target_pairs={{0,6},{2,0},{4,2},{6,4},{1,7},{3,1},{5,3},{7,5},{8,14},{10,8},{12,... | collective-permute-start | bytes 2359304 | tf_op jit(solution)/shard_map/ppermute | solution.py:34
  17.1 27.4 %collective-permute-done.3 = bf16[384,1024]{1,0:T(8,128)(2,1)S(1)} collective-permute-done((bf16[384,1024]{1,0:T(8,128)(2,1)S(1)}, bf16[384,1024]{1,0:T(8,128)(2,1)S(1)}, u32[]{:S(2)}, u32[]{:S(2)}) %collective-permute-start.3) | collective-permute-done | bytes 786464 | tf_op jit(solution)/shard_map/ppermute | solution.py:34
  45.4 1.2 collective-permute-done.4.far
  46.6 1.3 shard_map.93.basis
  47.9 1.6 %collective-permute-done.1.xg2 = bf16[128,3072]{1,0:T(8,128)(2,1)S(1)} collective-permute-done((bf16[128,3072]{1,0:T(8,128)(2,1)S(1)}, bf16[128,3072]{1,0:T(8,128)(2,1)S(1)}, u32[]{:S(2)}, u32[]{:S(2)}) %collective-permute-start.1) | collective-permute-done | bytes 786464 | tf_op jit(solution)/shard_map/ppermute | solution.py:34
  49.5 1.9 %shard_map.94 = (bf16[256,1024]{1,0:T(8,128)(2,1)S(1)}, f32[256,1024]{1,0:T(8,128)S(1)}, bf16[512,1024]{1,0:T(8,128)(2,1)S(1)}) custom-call(bf16[128,2048]{1,0:T(8,128)(2,1)S(1)} %get-tuple-element.55.x0, bf16[128,1024]{1,0:T(8,128)(2,1)S(1)} %copy-done.2, bf16[128,3072]{1,0:T(8,128)(2,1)S(1)} %collective-permute-done.xg1, ...), custom_call_target="tpu_custom_call" | custom-call | flops 4294967296 | bytes 10485760 | tf_op jit(solution)/shard_map/pallas_call | solution.py:173
  51.5 1.9 %collective-permute-done.5 = bf16[256,1024]{1,0:T(8,128)(2,1)S(1)} collective-permute-done((bf16[256,1024]{1,0:T(8,128)(2,1)S(1)}, bf16[256,1024]{1,0:T(8,128)(2,1)S(1)}, u32[]{:S(2)}, u32[]{:S(2)}) %collective-permute-start.5) | collective-permute-done | bytes 524320 | tf_op jit(solution)/shard_map/ppermute | solution.py:34
  53.6 1.7 %collective-permute-start.6 = (bf16[64,1024]{1,0:T(8,128)(2,1)S(1)}, bf16[64,1024]{1,0:T(8,128)(2,1)S(1)}, u32[]{:S(2)}, u32[]{:S(2)}) collective-permute-start(bf16[64,1024]{1,0:T(8,128)(2,1)S(1)} %get-tuple-element.61), channel_id=1, source_target_pairs={{0,16},{16,32},{32,48},{48,0},{1,17},{17,33},{33,49},{49,1},{2,18}... | collective-permute-start | bytes 393224 | tf_op jit(solution)/shard_map/ppermute | solution.py:34
  55.3 0.9 collective-permute-start.7
  56.2 2.4 %collective-permute-start.8 = (bf16[64,1024]{1,0:T(8,128)(2,1)S(1)}, bf16[64,1024]{1,0:T(8,128)(2,1)S(1)}, u32[]{:S(2)}, u32[]{:S(2)}) collective-permute-start(bf16[64,1024]{1,0:T(8,128)(2,1)S(1)} %get-tuple-element.59), channel_id=1, source_target_pairs={{0,48},{16,0},{32,16},{48,32},{1,49},{17,1},{33,17},{49,33},{2,50}... | collective-permute-start | bytes 393224 | tf_op jit(solution)/shard_map/ppermute | solution.py:34
  59.3 3.8 %collective-permute-done.7 = bf16[64,1024]{1,0:T(8,128)(2,1)S(1)} collective-permute-done((bf16[64,1024]{1,0:T(8,128)(2,1)S(1)}, bf16[64,1024]{1,0:T(8,128)(2,1)S(1)}, u32[]{:S(2)}, u32[]{:S(2)}) %collective-permute-start.7) | collective-permute-done | bytes 131104 | tf_op jit(solution)/shard_map/ppermute | solution.py:34
  63.2 1.0 collective-permute-done.8
  65.0 6.2 %all-to-all-start = ((bf16[8,16,1024]{2,1,0:T(8,128)(2,1)}), bf16[8,16,1024]{2,1,0:T(8,128)(2,1)}, u32[]{:S(2)}, u32[]{:S(2)}) async-start(bf16[8,16,1024]{2,1,0:T(8,128)(2,1)} %bitcast.1), calls=%async_computation | async-start | bytes 524288 | tf_op jit(solution)/shard_map/all_to_all | solution.py:186
  71.2 1.0 slice.37.refs_0_
  72.2 0.9 collective-permute-start.9
  73.0 2.0 %collective-permute-start.10 = (bf16[128,1024]{1,0:T(8,128)(2,1)S(1)}, bf16[128,1024]{1,0:T(8,128)(2,1)S(1)}, u32[]{:S(2)}, u32[]{:S(2)}) collective-permute-start(bf16[128,1024]{1,0:T(8,128)(2,1)S(1)} %slice.37.refs_0_), channel_id=1, source_target_pairs={{0,32},{16,48},{32,0},{48,16},{1,33},{17,49},{33,1},{49,17},{2,34}... | collective-permute-start | bytes 786440 | tf_op jit(solution)/shard_map/ppermute | solution.py:34
  75.0 1.7 %collective-permute-start.11 = (bf16[128,1024]{1,0:T(8,128)(2,1)S(1)}, bf16[128,1024]{1,0:T(8,128)(2,1)}, u32[]{:S(2)}, u32[]{:S(2)}) collective-permute-start(bf16[128,1024]{1,0:T(8,128)(2,1)S(1)} %slice.37.refs_0_), channel_id=1, source_target_pairs={{0,16},{16,32},{32,48},{48,0},{1,17},{17,33},{33,49},{49,1},{2,18}... | collective-permute-start | bytes 786440 | tf_op jit(solution)/shard_map/ppermute | solution.py:34
  76.7 4.6 %collective-permute-done.9.refs_1_ = bf16[128,1024]{1,0:T(8,128)(2,1)S(1)} collective-permute-done((bf16[128,1024]{1,0:T(8,128)(2,1)S(1)}, bf16[128,1024]{1,0:T(8,128)(2,1)S(1)}, u32[]{:S(2)}, u32[]{:S(2)}) %collective-permute-start.9) | collective-permute-done | bytes 262176 | tf_op jit(solution)/shard_map/ppermute | solution.py:34
  81.3 4.3 %collective-permute-done.10.refs_2_ = bf16[128,1024]{1,0:T(8,128)(2,1)S(1)} collective-permute-done((bf16[128,1024]{1,0:T(8,128)(2,1)S(1)}, bf16[128,1024]{1,0:T(8,128)(2,1)S(1)}, u32[]{:S(2)}, u32[]{:S(2)}) %collective-permute-start.10) | collective-permute-done | bytes 262176 | tf_op jit(solution)/shard_map/ppermute | solution.py:34
  86.3 0.8 collective-permute-done.11.refs_3_
  88.1 1.0 convert_reduce_fusion
  89.1 1.6 %collective-permute-start.12 = (f32[16,1024]{1,0:T(8,128)S(1)}, f32[16,1024]{1,0:T(8,128)S(1)}, u32[]{:S(2)}, u32[]{:S(2)}) collective-permute-start(f32[16,1024]{1,0:T(8,128)S(1)} %convert_reduce_fusion), channel_id=1, source_target_pairs={{0,2},{2,4},{4,6},{6,0},{1,3},{3,5},{5,7},{7,1},{8,10},{10,12},{12... | collective-permute-start | bytes 196616 | tf_op jit(solution)/shard_map/ppermute | solution.py:34
  90.6 1.7 %collective-permute-start.13 = (f32[16,1024]{1,0:T(8,128)S(1)}, f32[16,1024]{1,0:T(8,128)S(1)}, u32[]{:S(2)}, u32[]{:S(2)}) collective-permute-start(f32[16,1024]{1,0:T(8,128)S(1)} %convert_reduce_fusion), channel_id=1, source_target_pairs={{0,6},{2,0},{4,2},{6,4},{1,7},{3,1},{5,3},{7,5},{8,14},{10,8},{12,... | collective-permute-start | bytes 196616 | tf_op jit(solution)/shard_map/ppermute | solution.py:34
  92.4 1.8 %collective-permute-start.14 = (f32[16,1024]{1,0:T(8,128)S(1)}, f32[16,1024]{1,0:T(8,128)S(1)}, u32[]{:S(2)}, u32[]{:S(2)}) collective-permute-start(f32[16,1024]{1,0:T(8,128)S(1)} %convert_reduce_fusion), channel_id=1, source_target_pairs={{0,4},{2,6},{4,0},{6,2},{1,5},{3,7},{5,1},{7,3},{8,12},{10,14},{12... | collective-permute-start | bytes 196616 | tf_op jit(solution)/shard_map/ppermute | solution.py:34
  94.2 0.9 copy-done.5
  95.2 0.9 copy-done.7
  96.1 1.2 copy-done.9
  97.3 3.3 %shard_map.95 = bf16[4,128,2048]{2,1,0:T(8,128)(2,1)S(1)} custom-call(bf16[512,1024]{1,0:T(8,128)(2,1)S(1)} %copy-done.9, bf16[1024,1024]{1,0:T(8,128)(2,1)S(1)} %copy-done.3, bf16[128,1024]{1,0:T(8,128)(2,1)S(1)} %slice.37.refs_0_, bf16[128,1024]{1,0:T(8,128)(2,1)S(1)} %copy-done.5, bf16[128,1024]{1,0:T(8,128)(2,1)S(1)} %copy-done.7, ...), custom_call_target="tpu_custom_call" | custom-call | flops 2147483648 | bytes 8388608 | tf_op jit(solution)/shard_map/pallas_call | solution.py:191
  100.7 1.3 copy-done.1
  102.0 3.8 %all-to-all-start.1 = ((bf16[4,128,2048]{2,1,0:T(8,128)(2,1)}), bf16[4,128,2048]{2,1,0:T(8,128)(2,1)S(1)}, u32[]{:S(2)}, u32[]{:S(2)}) async-start(bf16[4,128,2048]{2,1,0:T(8,128)(2,1)} %copy-done.1), calls=%async_computation.1 | async-start | bytes 4194304 | tf_op jit(solution)/shard_map/all_to_all | solution.py:199
  106.5 1.7 %collective-permute-start.21 = (bf16[16,1024]{1,0:T(8,128)(2,1)S(1)}, bf16[16,1024]{1,0:T(8,128)(2,1)S(1)}, u32[]{:S(2)}, u32[]{:S(2)}) collective-permute-start(bf16[16,1024]{1,0:T(8,128)(2,1)S(1)} %get-tuple-element.50), channel_id=1, source_target_pairs={{0,64},{64,128},{128,192},{192,0},{1,65},{65,129},{129,193},{193,1... | collective-permute-start | bytes 98312 | tf_op jit(solution)/shard_map/ppermute | solution.py:34
  108.3 2.4 %collective-permute-start.20 = (bf16[16,1024]{1,0:T(8,128)(2,1)S(1)}, bf16[16,1024]{1,0:T(8,128)(2,1)S(1)}, u32[]{:S(2)}, u32[]{:S(2)}) collective-permute-start(bf16[16,1024]{1,0:T(8,128)(2,1)S(1)} %get-tuple-element.50), channel_id=1, source_target_pairs={{0,128},{64,192},{128,0},{192,64},{1,129},{65,193},{129,1},{193,65... | collective-permute-start | bytes 98312 | tf_op jit(solution)/shard_map/ppermute | solution.py:34
  110.6 1.5 %collective-permute-start.19 = (bf16[16,1024]{1,0:T(8,128)(2,1)S(1)}, bf16[16,1024]{1,0:T(8,128)(2,1)S(1)}, u32[]{:S(2)}, u32[]{:S(2)}) collective-permute-start(bf16[16,1024]{1,0:T(8,128)(2,1)S(1)} %get-tuple-element.50), channel_id=1, source_target_pairs={{0,192},{64,0},{128,64},{192,128},{1,193},{65,1},{129,65},{193,129... | collective-permute-start | bytes 98312 | tf_op jit(solution)/shard_map/ppermute | solution.py:34
  113.1 1.5 %collective-permute-done.19 = bf16[16,1024]{1,0:T(8,128)(2,1)S(1)} collective-permute-done((bf16[16,1024]{1,0:T(8,128)(2,1)S(1)}, bf16[16,1024]{1,0:T(8,128)(2,1)S(1)}, u32[]{:S(2)}, u32[]{:S(2)}) %collective-permute-start.19) | collective-permute-done | bytes 32800 | tf_op jit(solution)/shard_map/ppermute | solution.py:34
  114.5 1.5 %collective-permute-start.24 = (bf16[64,1024]{1,0:T(8,128)(2,1)S(1)}, bf16[64,1024]{1,0:T(8,128)(2,1)S(1)}, u32[]{:S(2)}, u32[]{:S(2)}) collective-permute-start(bf16[64,1024]{1,0:T(8,128)(2,1)S(1)} %pad_maximum_fusion.5), channel_id=1, source_target_pairs={{0,16},{16,32},{32,48},{48,0},{1,17},{17,33},{33,49},{49,1},{2,18}... | collective-permute-start | bytes 393224 | tf_op jit(solution)/shard_map/ppermute | solution.py:34
  116.0 3.1 %collective-permute-start.23 = (bf16[64,1024]{1,0:T(8,128)(2,1)S(1)}, bf16[64,1024]{1,0:T(8,128)(2,1)S(1)}, u32[]{:S(2)}, u32[]{:S(2)}) collective-permute-start(bf16[64,1024]{1,0:T(8,128)(2,1)S(1)} %pad_maximum_fusion.5), channel_id=1, source_target_pairs={{0,32},{16,48},{32,0},{48,16},{1,33},{17,49},{33,1},{49,17},{2,34}... | collective-permute-start | bytes 393224 | tf_op jit(solution)/shard_map/ppermute | solution.py:34
  121.2 1.3 collective-permute-done.23
  122.5 1.6 %collective-permute-done.22 = bf16[64,1024]{1,0:T(8,128)(2,1)S(1)} collective-permute-done((bf16[64,1024]{1,0:T(8,128)(2,1)S(1)}, bf16[64,1024]{1,0:T(8,128)(2,1)S(1)}, u32[]{:S(2)}, u32[]{:S(2)}) %collective-permute-start.22) | collective-permute-done | bytes 131104 | tf_op jit(solution)/shard_map/ppermute | solution.py:34
  124.3 1.9 %collective-permute-done.25.far = bf16[256,1024]{1,0:T(8,128)(2,1)S(1)} collective-permute-done((bf16[256,1024]{1,0:T(8,128)(2,1)S(1)}, bf16[256,1024]{1,0:T(8,128)(2,1)S(1)}, u32[]{:S(2)}, u32[]{:S(2)}) %collective-permute-start.25) | collective-permute-done | bytes 524320 | tf_op jit(solution)/shard_map/ppermute | solution.py:34
  126.2 3.3 %shard_map.96 = f32[1024,1024]{1,0:T(8,128)} custom-call(bf16[1024,512]{1,0:T(8,128)(2,1)S(1)} %fusion.basis, bf16[256,1024]{1,0:T(8,128)(2,1)S(1)} %pad_maximum_fusion.4.near, bf16[256,1024]{1,0:T(8,128)(2,1)S(1)} %collective-permute-done.25.far), custom_call_target="tpu_custom_call" | custom-call | flops 1073741824 | bytes 6291456 | tf_op jit(solution)/shard_map/pallas_call | solution.py:209
  129.4 2.3 %all-to-all-done.1.blocks = bf16[4,128,2048]{2,1,0:T(8,128)(2,1)S(1)} async-done(((bf16[4,128,2048]{2,1,0:T(8,128)(2,1)}), bf16[4,128,2048]{2,1,0:T(8,128)(2,1)S(1)}, u32[]{:S(2)}, u32[]{:S(2)}) %all-to-all-start.1) | async-done | bytes 2097184 | tf_op jit(solution)/shard_map/all_to_all | solution.py:199
  131.7 1.6 %shard_map.97 = bf16[128,8192]{1,0:T(8,128)(2,1)} custom-call(bf16[4,128,2048]{2,1,0:T(8,128)(2,1)S(1)} %all-to-all-done.1.blocks), custom_call_target="tpu_custom_call" | custom-call | flops 1048576 | bytes 4194304 | tf_op jit(solution)/shard_map/pallas_call | solution.py:222
  (59 shorter events, 8.8 us)
Async XLA Ops:
  0.7 2.3 %copy-start.10 = (bf16[128,8192]{1,0:T(8,128)(2,1)S(1)}, bf16[128,8192]{1,0:T(8,128)(2,1)}, u32[]{:S(2)}) copy-start(bf16[128,8192]{1,0:T(8,128)(2,1)} %param.6) | copy-start | bytes 6291460
  3.0 1.0 copy-start.2
  4.2 42.4 %copy-start = (bf16[1024,512]{1,0:T(8,128)(2,1)S(1)}, bf16[1024,512]{1,0:T(8,128)(2,1)}, u32[]{:S(2)}) copy-start(bf16[1024,512]{1,0:T(8,128)(2,1)} %mine.1) | copy-start | bytes 3145732
  4.2 40.3 %collective-permute-start.3 = (bf16[384,1024]{1,0:T(8,128)(2,1)S(1)}, bf16[384,1024]{1,0:T(8,128)(2,1)S(1)}, u32[]{:S(2)}, u32[]{:S(2)}) collective-permute-start(bf16[384,1024]{1,0:T(8,128)(2,1)S(1)} %pad_maximum_fusion.3), channel_id=1, source_target_pairs={{0,1},{1,0},{2,3},{3,2},{4,5},{5,4},{6,7},{7,6},{8,9},{9,8},{10,11... | collective-permute-start | bytes 2359304 | tf_op jit(solution)/shard_map/ppermute | solution.py:34
  11.4 36.5 %collective-permute-start = (bf16[128,3072]{1,0:T(8,128)(2,1)S(1)}, bf16[128,3072]{1,0:T(8,128)(2,1)S(1)}, u32[]{:S(2)}, u32[]{:S(2)}) collective-permute-start(bf16[128,3072]{1,0:T(8,128)(2,1)S(1)} %get-tuple-element.27), channel_id=1, source_target_pairs={{0,2},{2,4},{4,6},{6,0},{1,3},{3,5},{5,7},{7,1},{8,10},{10,12},{12... | collective-permute-start | bytes 2359304 | tf_op jit(solution)/shard_map/ppermute | solution.py:34
  12.9 36.6 %collective-permute-start.1 = (bf16[128,3072]{1,0:T(8,128)(2,1)S(1)}, bf16[128,3072]{1,0:T(8,128)(2,1)S(1)}, u32[]{:S(2)}, u32[]{:S(2)}) collective-permute-start(bf16[128,3072]{1,0:T(8,128)(2,1)S(1)} %get-tuple-element.28), channel_id=1, source_target_pairs={{0,4},{2,6},{4,0},{6,2},{1,5},{3,7},{5,1},{7,3},{8,12},{10,14},{12... | collective-permute-start | bytes 2359304 | tf_op jit(solution)/shard_map/ppermute | solution.py:34
  15.7 33.8 %collective-permute-start.2 = (bf16[128,3072]{1,0:T(8,128)(2,1)S(1)}, bf16[128,3072]{1,0:T(8,128)(2,1)S(1)}, u32[]{:S(2)}, u32[]{:S(2)}) collective-permute-start(bf16[128,3072]{1,0:T(8,128)(2,1)S(1)} %get-tuple-element.29), channel_id=1, source_target_pairs={{0,6},{2,0},{4,2},{6,4},{1,7},{3,1},{5,3},{7,5},{8,14},{10,8},{12,... | collective-permute-start | bytes 2359304 | tf_op jit(solution)/shard_map/ppermute | solution.py:34
  44.5 0.9 copy-start.11
  44.6 2.0 %collective-permute-start.4 = (bf16[256,1024]{1,0:T(8,128)(2,1)S(1)}, bf16[256,1024]{1,0:T(8,128)(2,1)S(1)}, u32[]{:S(2)}, u32[]{:S(2)}) collective-permute-start(bf16[256,1024]{1,0:T(8,128)(2,1)S(1)} %slice.32.part), channel_id=1, source_target_pairs={{0,8},{8,0},{1,9},{9,1},{2,10},{10,2},{3,11},{11,3},{4,12},{12,4},... | collective-permute-start | bytes 1572872 | tf_op jit(solution)/shard_map/ppermute | solution.py:34
  51.4 12.8 %copy-start.8 = (bf16[512,1024]{1,0:T(8,128)(2,1)}, bf16[512,1024]{1,0:T(8,128)(2,1)S(1)}, u32[]{:S(2)}) copy-start(bf16[512,1024]{1,0:T(8,128)(2,1)S(1)} %get-tuple-element.37.grads) | copy-start | bytes 3145732
  51.4 2.0 %collective-permute-start.5 = (bf16[256,1024]{1,0:T(8,128)(2,1)S(1)}, bf16[256,1024]{1,0:T(8,128)(2,1)S(1)}, u32[]{:S(2)}, u32[]{:S(2)}) collective-permute-start(bf16[256,1024]{1,0:T(8,128)(2,1)S(1)} %get-tuple-element.32), channel_id=1, source_target_pairs={{0,8},{8,0},{1,9},{9,1},{2,10},{10,2},{3,11},{11,3},{4,12},{12,4},... | collective-permute-start | bytes 1572872 | tf_op jit(solution)/shard_map/ppermute | solution.py:34
  53.6 40.6 %copy-start.3 = (bf16[1024,1024]{1,0:T(8,128)(2,1)S(1)}, bf16[1024,1024]{1,0:T(8,128)(2,1)}, u32[]{:S(2)}) copy-start(bf16[1024,1024]{1,0:T(8,128)(2,1)} %weight.1) | copy-start | bytes 6291460
  53.6 5.7 %collective-permute-start.6 = (bf16[64,1024]{1,0:T(8,128)(2,1)S(1)}, bf16[64,1024]{1,0:T(8,128)(2,1)S(1)}, u32[]{:S(2)}, u32[]{:S(2)}) collective-permute-start(bf16[64,1024]{1,0:T(8,128)(2,1)S(1)} %get-tuple-element.61), channel_id=1, source_target_pairs={{0,16},{16,32},{32,48},{48,0},{1,17},{17,33},{33,49},{49,1},{2,18}... | collective-permute-start | bytes 393224 | tf_op jit(solution)/shard_map/ppermute | solution.py:34
  55.3 7.9 %collective-permute-start.7 = (bf16[64,1024]{1,0:T(8,128)(2,1)S(1)}, bf16[64,1024]{1,0:T(8,128)(2,1)S(1)}, u32[]{:S(2)}, u32[]{:S(2)}) collective-permute-start(bf16[64,1024]{1,0:T(8,128)(2,1)S(1)} %get-tuple-element.60), channel_id=1, source_target_pairs={{0,32},{16,48},{32,0},{48,16},{1,33},{17,49},{33,1},{49,17},{2,34}... | collective-permute-start | bytes 393224 | tf_op jit(solution)/shard_map/ppermute | solution.py:34
  56.2 7.9 %collective-permute-start.8 = (bf16[64,1024]{1,0:T(8,128)(2,1)S(1)}, bf16[64,1024]{1,0:T(8,128)(2,1)S(1)}, u32[]{:S(2)}, u32[]{:S(2)}) collective-permute-start(bf16[64,1024]{1,0:T(8,128)(2,1)S(1)} %get-tuple-element.59), channel_id=1, source_target_pairs={{0,48},{16,0},{32,16},{48,32},{1,49},{17,1},{33,17},{49,33},{2,50}... | collective-permute-start | bytes 393224 | tf_op jit(solution)/shard_map/ppermute | solution.py:34
  65.0 22.1 %all-to-all-start = ((bf16[8,16,1024]{2,1,0:T(8,128)(2,1)}), bf16[8,16,1024]{2,1,0:T(8,128)(2,1)}, u32[]{:S(2)}, u32[]{:S(2)}) async-start(bf16[8,16,1024]{2,1,0:T(8,128)(2,1)} %bitcast.1), calls=%async_computation | async-start | bytes 524288 | tf_op jit(solution)/shard_map/all_to_all | solution.py:186
  72.2 9.1 %collective-permute-start.9 = (bf16[128,1024]{1,0:T(8,128)(2,1)S(1)}, bf16[128,1024]{1,0:T(8,128)(2,1)S(1)}, u32[]{:S(2)}, u32[]{:S(2)}) collective-permute-start(bf16[128,1024]{1,0:T(8,128)(2,1)S(1)} %slice.37.refs_0_), channel_id=1, source_target_pairs={{0,48},{16,0},{32,16},{48,32},{1,49},{17,1},{33,17},{49,33},{2,50}... | collective-permute-start | bytes 786440 | tf_op jit(solution)/shard_map/ppermute | solution.py:34
  73.0 12.5 %collective-permute-start.10 = (bf16[128,1024]{1,0:T(8,128)(2,1)S(1)}, bf16[128,1024]{1,0:T(8,128)(2,1)S(1)}, u32[]{:S(2)}, u32[]{:S(2)}) collective-permute-start(bf16[128,1024]{1,0:T(8,128)(2,1)S(1)} %slice.37.refs_0_), channel_id=1, source_target_pairs={{0,32},{16,48},{32,0},{48,16},{1,33},{17,49},{33,1},{49,17},{2,34}... | collective-permute-start | bytes 786440 | tf_op jit(solution)/shard_map/ppermute | solution.py:34
  75.0 12.0 %collective-permute-start.11 = (bf16[128,1024]{1,0:T(8,128)(2,1)S(1)}, bf16[128,1024]{1,0:T(8,128)(2,1)}, u32[]{:S(2)}, u32[]{:S(2)}) collective-permute-start(bf16[128,1024]{1,0:T(8,128)(2,1)S(1)} %slice.37.refs_0_), channel_id=1, source_target_pairs={{0,16},{16,32},{32,48},{48,0},{1,17},{17,33},{33,49},{49,1},{2,18}... | collective-permute-start | bytes 786440 | tf_op jit(solution)/shard_map/ppermute | solution.py:34
  81.3 4.3 %copy-start.4 = (bf16[128,1024]{1,0:T(8,128)(2,1)}, bf16[128,1024]{1,0:T(8,128)(2,1)S(1)}, u32[]{:S(2)}) copy-start(bf16[128,1024]{1,0:T(8,128)(2,1)S(1)} %collective-permute-done.9.refs_1_) | copy-start | bytes 786436
  85.6 0.7 copy-start.6
  87.0 3.6 %collective-permute-start.15 = (bf16[128,1024]{1,0:T(8,128)(2,1)S(1)}, bf16[128,1024]{1,0:T(8,128)(2,1)S(1)}, u32[]{:S(2)}, u32[]{:S(2)}) collective-permute-start(bf16[128,1024]{1,0:T(8,128)(2,1)S(1)} %slice.37.refs_0_), channel_id=1, source_target_pairs={{0,8},{8,0},{1,9},{9,1},{2,10},{10,2},{3,11},{11,3},{4,12},{12,4},... | collective-permute-start | bytes 786440 | tf_op jit(solution)/shard_map/ppermute | solution.py:34
  87.0 5.3 %collective-permute-start.16 = (bf16[128,1024]{1,0:T(8,128)(2,1)}, bf16[128,1024]{1,0:T(8,128)(2,1)S(1)}, u32[]{:S(2)}, u32[]{:S(2)}) collective-permute-start(bf16[128,1024]{1,0:T(8,128)(2,1)} %copy-done.4), channel_id=1, source_target_pairs={{0,8},{8,0},{1,9},{9,1},{2,10},{10,2},{3,11},{11,3},{4,12},{12,4},... | collective-permute-start | bytes 786440 | tf_op jit(solution)/shard_map/ppermute | solution.py:34
  87.5 6.6 %collective-permute-start.17 = (bf16[128,1024]{1,0:T(8,128)(2,1)}, bf16[128,1024]{1,0:T(8,128)(2,1)S(1)}, u32[]{:S(2)}, u32[]{:S(2)}) collective-permute-start(bf16[128,1024]{1,0:T(8,128)(2,1)} %copy-done.6), channel_id=1, source_target_pairs={{0,8},{8,0},{1,9},{9,1},{2,10},{10,2},{3,11},{11,3},{4,12},{12,4},... | collective-permute-start | bytes 786440 | tf_op jit(solution)/shard_map/ppermute | solution.py:34
  87.6 6.6 %collective-permute-start.18 = (bf16[128,1024]{1,0:T(8,128)(2,1)}, bf16[128,1024]{1,0:T(8,128)(2,1)S(1)}, u32[]{:S(2)}, u32[]{:S(2)}) collective-permute-start(bf16[128,1024]{1,0:T(8,128)(2,1)} %collective-permute-done.11.refs_3_), channel_id=1, source_target_pairs={{0,8},{8,0},{1,9},{9,1},{2,10},{10,2},{3,11},{11,3},{4,12},{12,4},... | collective-permute-start | bytes 786440 | tf_op jit(solution)/shard_map/ppermute | solution.py:34
  89.1 12.9 %collective-permute-start.12 = (f32[16,1024]{1,0:T(8,128)S(1)}, f32[16,1024]{1,0:T(8,128)S(1)}, u32[]{:S(2)}, u32[]{:S(2)}) collective-permute-start(f32[16,1024]{1,0:T(8,128)S(1)} %convert_reduce_fusion), channel_id=1, source_target_pairs={{0,2},{2,4},{4,6},{6,0},{1,3},{3,5},{5,7},{7,1},{8,10},{10,12},{12... | collective-permute-start | bytes 196616 | tf_op jit(solution)/shard_map/ppermute | solution.py:34
  90.6 11.3 %collective-permute-start.13 = (f32[16,1024]{1,0:T(8,128)S(1)}, f32[16,1024]{1,0:T(8,128)S(1)}, u32[]{:S(2)}, u32[]{:S(2)}) collective-permute-start(f32[16,1024]{1,0:T(8,128)S(1)} %convert_reduce_fusion), channel_id=1, source_target_pairs={{0,6},{2,0},{4,2},{6,4},{1,7},{3,1},{5,3},{7,5},{8,14},{10,8},{12,... | collective-permute-start | bytes 196616 | tf_op jit(solution)/shard_map/ppermute | solution.py:34
  92.4 9.6 %collective-permute-start.14 = (f32[16,1024]{1,0:T(8,128)S(1)}, f32[16,1024]{1,0:T(8,128)S(1)}, u32[]{:S(2)}, u32[]{:S(2)}) collective-permute-start(f32[16,1024]{1,0:T(8,128)S(1)} %convert_reduce_fusion), channel_id=1, source_target_pairs={{0,4},{2,6},{4,0},{6,2},{1,5},{3,7},{5,1},{7,3},{8,12},{10,14},{12... | collective-permute-start | bytes 196616 | tf_op jit(solution)/shard_map/ppermute | solution.py:34
  94.2 1.0 copy-start.5
  95.2 0.9 copy-start.7
  96.1 1.2 copy-start.9
  100.7 1.3 copy-start.1
  102.0 3.8 %copy-start.12 = (f32[16,1024]{1,0:T(8,128)S(1)}, f32[16,1024]{1,0:T(8,128)}, u32[]{:S(2)}) copy-start(f32[16,1024]{1,0:T(8,128)} %param.10) | copy-start | bytes 196612
  102.0 3.8 %copy-start.13 = (f32[16,1024]{1,0:T(8,128)S(1)}, f32[16,1024]{1,0:T(8,128)}, u32[]{:S(2)}) copy-start(f32[16,1024]{1,0:T(8,128)} %param.11) | copy-start | bytes 196612
  102.0 29.7 %all-to-all-start.1 = ((bf16[4,128,2048]{2,1,0:T(8,128)(2,1)}), bf16[4,128,2048]{2,1,0:T(8,128)(2,1)S(1)}, u32[]{:S(2)}, u32[]{:S(2)}) async-start(bf16[4,128,2048]{2,1,0:T(8,128)(2,1)} %copy-done.1), calls=%async_computation.1 | async-start | bytes 4194304 | tf_op jit(solution)/shard_map/all_to_all | solution.py:199
  106.5 6.1 %collective-permute-start.21 = (bf16[16,1024]{1,0:T(8,128)(2,1)S(1)}, bf16[16,1024]{1,0:T(8,128)(2,1)S(1)}, u32[]{:S(2)}, u32[]{:S(2)}) collective-permute-start(bf16[16,1024]{1,0:T(8,128)(2,1)S(1)} %get-tuple-element.50), channel_id=1, source_target_pairs={{0,64},{64,128},{128,192},{192,0},{1,65},{65,129},{129,193},{193,1... | collective-permute-start | bytes 98312 | tf_op jit(solution)/shard_map/ppermute | solution.py:34
  108.3 4.8 %collective-permute-start.20 = (bf16[16,1024]{1,0:T(8,128)(2,1)S(1)}, bf16[16,1024]{1,0:T(8,128)(2,1)S(1)}, u32[]{:S(2)}, u32[]{:S(2)}) collective-permute-start(bf16[16,1024]{1,0:T(8,128)(2,1)S(1)} %get-tuple-element.50), channel_id=1, source_target_pairs={{0,128},{64,192},{128,0},{192,64},{1,129},{65,193},{129,1},{193,65... | collective-permute-start | bytes 98312 | tf_op jit(solution)/shard_map/ppermute | solution.py:34
  110.6 3.9 %collective-permute-start.19 = (bf16[16,1024]{1,0:T(8,128)(2,1)S(1)}, bf16[16,1024]{1,0:T(8,128)(2,1)S(1)}, u32[]{:S(2)}, u32[]{:S(2)}) collective-permute-start(bf16[16,1024]{1,0:T(8,128)(2,1)S(1)} %get-tuple-element.50), channel_id=1, source_target_pairs={{0,192},{64,0},{128,64},{192,128},{1,193},{65,1},{129,65},{193,129... | collective-permute-start | bytes 98312 | tf_op jit(solution)/shard_map/ppermute | solution.py:34
  114.5 6.7 %collective-permute-start.24 = (bf16[64,1024]{1,0:T(8,128)(2,1)S(1)}, bf16[64,1024]{1,0:T(8,128)(2,1)S(1)}, u32[]{:S(2)}, u32[]{:S(2)}) collective-permute-start(bf16[64,1024]{1,0:T(8,128)(2,1)S(1)} %pad_maximum_fusion.5), channel_id=1, source_target_pairs={{0,16},{16,32},{32,48},{48,0},{1,17},{17,33},{33,49},{49,1},{2,18}... | collective-permute-start | bytes 393224 | tf_op jit(solution)/shard_map/ppermute | solution.py:34
  116.0 6.5 %collective-permute-start.23 = (bf16[64,1024]{1,0:T(8,128)(2,1)S(1)}, bf16[64,1024]{1,0:T(8,128)(2,1)S(1)}, u32[]{:S(2)}, u32[]{:S(2)}) collective-permute-start(bf16[64,1024]{1,0:T(8,128)(2,1)S(1)} %pad_maximum_fusion.5), channel_id=1, source_target_pairs={{0,32},{16,48},{32,0},{48,16},{1,33},{17,49},{33,1},{49,17},{2,34}... | collective-permute-start | bytes 393224 | tf_op jit(solution)/shard_map/ppermute | solution.py:34
  119.2 5.0 %collective-permute-start.22 = (bf16[64,1024]{1,0:T(8,128)(2,1)S(1)}, bf16[64,1024]{1,0:T(8,128)(2,1)S(1)}, u32[]{:S(2)}, u32[]{:S(2)}) collective-permute-start(bf16[64,1024]{1,0:T(8,128)(2,1)S(1)} %pad_maximum_fusion.5), channel_id=1, source_target_pairs={{0,48},{16,0},{32,16},{48,32},{1,49},{17,1},{33,17},{49,33},{2,50}... | collective-permute-start | bytes 393224 | tf_op jit(solution)/shard_map/ppermute | solution.py:34
  124.2 2.0 %collective-permute-start.25 = (bf16[256,1024]{1,0:T(8,128)(2,1)S(1)}, bf16[256,1024]{1,0:T(8,128)(2,1)S(1)}, u32[]{:S(2)}, u32[]{:S(2)}) collective-permute-start(bf16[256,1024]{1,0:T(8,128)(2,1)S(1)} %pad_maximum_fusion.4.near), channel_id=1, source_target_pairs={{0,8},{8,0},{1,9},{9,1},{2,10},{10,2},{3,11},{11,3},{4,12},{12,4},... | collective-permute-start | bytes 1572872 | tf_op jit(solution)/shard_map/ppermute | solution.py:34
